TPU v7x, 256 devices: a whole 4x4x8 slice. The times are simulated.
256 devices in a mesh: wide: 32 (over y, z), narrow: 8 (over x, core).
Axes of the slice: x: 4, y: 4, z: 8, core: 2. Of those that a mesh axis runs over, the one named last changes fastest.
Arguments:
- step_one: bfloat16 [512, 18432], P('wide'), may hold values from -6 to 6
- step_two: bfloat16 [512, 18432], P('wide'), may hold values from -6 to 6
- gain: float32 [18432], replicated, may hold values from 0.1 to 1.9
- w_query: bfloat16 [18432, 12288], P('narrow', 'wide'), may hold values from -0.046875 to 0.046875
- w_keyval: bfloat16 [18432, 512], P('narrow', 'wide'), may hold values from -0.046875 to 0.046875
- w_out: bfloat16 [12288, 18432], P('wide', 'narrow'), may hold values from -0.4375 to 0.4375
- kv_cache: bfloat16 [512, 2048, 512], P(('wide', 'narrow'))
- lengths: int32 [512], P(('wide', 'narrow')), may hold values from 2 to 2048, as said below
Outputs:
- branch_one: bfloat16 [512, 18432], P('wide', 'narrow')
- branch_two: bfloat16 [512, 18432], P('wide', 'narrow')
Inputs may be any that keep to these rules, and one draw needn't show every extreme that they name: `lengths`: at least one sequence has length 2048.
All inputs are finite; a program needn't handle non-finite values.
Results may differ from a plain program's by a relative error of at most 0.012.
Values may be sent and summed in bfloat16 or wider, within the bound.
No kernel may reach another device: no remote copies, remote signals or barrier semaphores. Data moves between devices by JAX's collectives and lax.ppermute only.
A program may use at most 64 MiB of HBM per device.

v0:
```python
import jax
import jax.numpy as jnp
from jax import lax
from jax.sharding import PartitionSpec as P

HEADS = 48


EPSILON = 1e-05
NEG_FILL = -1e30


def normalize(inputs, gain):
    values = inputs.astype(jnp.float32)
    average = jnp.mean(values, axis=-1, keepdims=True)
    variance = jnp.mean(values * values, axis=-1, keepdims=True) - average * average
    return ((values - average) * lax.rsqrt(variance + EPSILON) * gain).astype(jnp.bfloat16)


def attend(
    queries,
    stored_key_rows,
    stored_value_rows,
    live_mask,
    new_keys,
    new_values,
    head_count,
    head_size,
):
    rows_here = queries.shape[0]
    head_outputs = queries.reshape(rows_here, head_count, head_size)
    logit_scale_factor = head_size ** (-0.5)
    attention_logits = (
        jnp.einsum(
            "xfw,xmw->xfm", head_outputs, stored_key_rows, preferred_element_type=jnp.float32
        )
        * logit_scale_factor
    )
    new_scores = (
        jnp.einsum("bhd,bjd->bhj", head_outputs, new_keys, preferred_element_type=jnp.float32)
        * logit_scale_factor
    )
    attention_logits = jnp.where(live_mask[:, None, :], attention_logits, NEG_FILL)
    row_top = jnp.maximum(jnp.max(attention_logits, axis=-1), jnp.max(new_scores, axis=-1))
    stored_weight_matrix = jnp.where(
        live_mask[:, None, :], jnp.exp(attention_logits - row_top[..., None]), 0.0
    )
    new_weights = jnp.exp(new_scores - row_top[..., None])
    denominator = jnp.sum(stored_weight_matrix, axis=-1) + jnp.sum(new_weights, axis=-1)
    weighted_value_sum = jnp.einsum(
        "tiz,tzo->tio",
        stored_weight_matrix.astype(jnp.bfloat16),
        stored_value_rows,
        preferred_element_type=jnp.float32,
    )
    weighted_value_sum = weighted_value_sum + jnp.einsum(
        "bhj,bjd->bhd",
        new_weights.astype(jnp.bfloat16),
        new_values,
        preferred_element_type=jnp.float32,
    )
    return (
        (weighted_value_sum / denominator[..., None])
        .astype(jnp.bfloat16)
        .reshape(rows_here, head_count * head_size)
    )


def shards(step_one, step_two, gain, w_query, w_keyval, w_out, kv_cache, lengths):
    head_size = kv_cache.shape[2] // 2
    head_count = HEADS
    wide_size = lax.axis_size("wide")
    slice_width = w_query.shape[0]
    query_cols = w_query.shape[1]
    own_rows = kv_cache.shape[0]
    column_start = lax.axis_index("narrow") * slice_width
    joined = jnp.concatenate([w_query, w_keyval], axis=1)
    joined_cols = joined.shape[1]
    stored_key_rows = kv_cache[:, :, :head_size]
    stored_value_rows = kv_cache[:, :, head_size:]
    live_mask = jnp.arange(kv_cache.shape[1])[None, :] < lengths[:, None]

    def project(rows_piece):
        return jnp.dot(rows_piece, joined, preferred_element_type=jnp.float32)

    def decode_layer(inputs, earlier_keys, earlier_values):
        normed = normalize(inputs, gain)
        my_slice = lax.dynamic_slice_in_dim(normed, column_start, slice_width, 1)
        partials = project(lax.all_gather(my_slice, "wide", axis=0, tiled=True))
        arrived = lax.all_to_all(partials, "wide", split_axis=0, concat_axis=1, tiled=True)
        summed = lax.psum_scatter(arrived, "narrow", scatter_dimension=0, tiled=True)
        projected = summed.astype(jnp.bfloat16)
        grouped = projected.reshape(own_rows, wide_size, joined_cols)
        queries = grouped[:, :, :query_cols].reshape(own_rows, wide_size * query_cols)
        keyval = grouped[:, :, query_cols:].reshape(own_rows, 2 * head_size)
        new_keys = jnp.concatenate(earlier_keys + [keyval[:, None, :head_size]], axis=1)
        new_values = jnp.concatenate(earlier_values + [keyval[:, None, head_size:]], axis=1)
        attended = attend(
            queries,
            stored_key_rows,
            stored_value_rows,
            live_mask,
            new_keys,
            new_values,
            head_count,
            head_size,
        )
        gathered = lax.all_gather(attended, "narrow", axis=0, tiled=True)
        returned = lax.all_to_all(gathered, "wide", split_axis=1, concat_axis=0, tiled=True)
        branch = lax.psum_scatter(
            jnp.dot(returned, w_out, preferred_element_type=jnp.float32),
            "wide",
            scatter_dimension=0,
            tiled=True,
        )
        return (branch.astype(jnp.bfloat16), keyval)

    branch_one, keyval_one = decode_layer(step_one, [], [])
    branch_two, keyval_two = decode_layer(
        step_two, [keyval_one[:, None, :head_size]], [keyval_one[:, None, head_size:]]
    )
    return (branch_one, branch_two)


def solution(mesh):
    return jax.shard_map(
        shards,
        mesh=mesh,
        in_specs=(
            P("wide", None),
            P("wide", None),
            P(),
            P("narrow", "wide"),
            P("narrow", "wide"),
            P("wide", "narrow"),
            P(("wide", "narrow"), None, None),
            P(("wide", "narrow")),
        ),
        out_specs=(P("wide", "narrow"), P("wide", "narrow")),
        check_vma=False,
    )
```

profile of v0, /device:TPU:8, one launch (start us, length us, event | category | flops | bytes accessed | tf_op | source)
XLA Modules:
  0.0 764.7 jit_solution(551204503217510850)
XLA Ops:
  7.2 1.5 convert_reduce_fusion.1
  8.7 1.1 convert_element_type.43
  9.9 0.3 convert_reduce_fusion
  10.2 1.1 convert_element_type.50
  11.3 0.8 dynamic-slice.4
  12.1 1.7 fusion.42
  13.9 0.7 all-gather.7.cloned.1.call-update
  14.6 1.2 copy.30
  15.8 78.1 %all-gather.5.cloned.1.call-done = bf16[512,2304]{1,0:T(8,128)(2,1)} async-done(((bf16[16,2304]{1,0:T(8,128)(2,1)}), bf16[512,2304]{1,0:T(8,128)(2,1)}) %all-gather.5.cloned.1.call-update) | async-done | bytes 2359312 | tf_op jit(solution)/shard_map/all_gather | solution.py:89
  93.9 4.6 fusion.9
  98.5 7.4 all-to-all-start
  106.0 68.1 %all-gather.7.cloned.1.call-done = bf16[512,2304]{1,0:T(8,128)(2,1)} async-done(((bf16[16,2304]{1,0:T(8,128)(2,1)}), bf16[512,2304]{1,0:T(8,128)(2,1)}) %all-gather.7.cloned.1.call-update) | async-done | bytes 2359312 | tf_op jit(solution)/shard_map/all_gather | solution.py:89
  174.0 4.5 fusion.8
  178.6 7.5 all-to-all-start.2
  186.2 0.6 dynamic-slice
  187.5 1.8 copy.32
  189.3 1.4 all_to_all.59
  190.8 17.9 %all-to-all-done.2 = f32[32,16,400]{2,1,0:T(8,128)} async-done(((f32[32,16,400]{2,1,0:T(8,128)}), f32[32,16,400]{2,1,0:T(8,128)}, u32[]{:S(2)}, u32[]{:S(2)}) %all-to-all-start.2) | async-done | bytes 819232 | tf_op jit(solution)/shard_map/all_to_all | solution.py:90
  208.7 1.8 copy.35
  210.5 1.4 all_to_all.67
  211.9 51.8 %all-reduce.4 = (bf16[16,12800]{1,0:T(8,128)(2,1)S(1)}, bf16[16,12800]{1,0:T(8,128)(2,1)S(1)}) all-reduce(f32[16,12800]{1,0:T(8,128)} %all_to_all.59, f32[16,12800]{1,0:T(8,128)} %all_to_all.67), channel_id=2, replica_groups=mesh['wide'=32,'narrow'=8] {'narrow'}, use_global_device_ids=true, to_apply=%region_2.0.clone | all-reduce | flops 409600 | bytes 2457600
  263.8 0.2 reshape.118
  264.1 0.2 reshape.121
  264.3 0.1 reshape.119
  264.5 0.1 reshape.122
  264.6 0.1 fusion.53
  264.8 2.4 fusion.66
  267.2 2.6 fusion.67
  269.8 0.1 fusion.68
  269.9 0.2 fusion.49
  270.2 0.4 fusion.30
  270.6 0.5 fusion.25
  271.1 13.1 %all-gather.1 = bf16[8,2,12288]{2,1,0:T(2,128)(2,1)S(1)} all-gather(bf16[1,2,12288]{2,1,0:T(2,128)(2,1)S(1)} %reshape.126), channel_id=1, replica_groups=mesh['wide'=32,'narrow'=8] {'narrow'}, dimensions={0}, use_global_device_ids=true | all-gather | bytes 442368 | tf_op jit(solution)/shard_map/all_gather | solution.py:108
  284.2 0.3 all_to_all.68
  284.5 0.1 copy.40
  284.7 20.8 %all_to_all.76 = bf16[16,32,384]{2,0,1:T(8,128)(2,1)S(1)} all-to-all(bf16[16,32,384]{2,0,1:T(8,128)(2,1)S(1)} %copy.40), channel_id=1, replica_groups=mesh['wide'=32,'narrow'=8] {'wide'}, dimensions={1} | all-to-all | bytes 786432 | tf_op jit(solution)/shard_map/all_to_all | solution.py:109
  305.5 3.6 fusion.70
  309.1 0.2 reduce-scatter.3.cloned.1.call-start
  309.4 2.1 fusion.22
  311.5 13.0 %all-gather = bf16[8,2,12288]{2,1,0:T(2,128)(2,1)S(1)} all-gather(bf16[1,2,12288]{2,1,0:T(2,128)(2,1)S(1)} %reshape.124), channel_id=1, replica_groups=mesh['wide'=32,'narrow'=8] {'narrow'}, dimensions={0}, use_global_device_ids=true | all-gather | bytes 442368 | tf_op jit(solution)/shard_map/all_gather | solution.py:108
  324.5 0.3 all_to_all.60
  324.8 0.1 copy.33
  324.9 22.0 %all_to_all.77 = bf16[16,32,384]{2,0,1:T(8,128)(2,1)S(1)} all-to-all(bf16[16,32,384]{2,0,1:T(8,128)(2,1)S(1)} %copy.33), channel_id=1, replica_groups=mesh['wide'=32,'narrow'=8] {'wide'}, dimensions={1} | all-to-all | bytes 786432 | tf_op jit(solution)/shard_map/all_to_all | solution.py:109
  346.9 3.5 fusion.69
  350.5 180.6 %reduce-scatter.5.cloned.1.call-done = f32[16,2304]{1,0:T(8,128)} async-done(((f32[512,2304]{1,0:T(8,128)}), f32[16,2304]{1,0:T(8,128)}) %reduce-scatter.5.cloned.1.call-update) | async-done | bytes 147472 | tf_op jit(solution)/shard_map/reduce_scatter | solution.py:110
  531.1 1.6 convert_element_type.56
  532.7 224.0 %reduce-scatter.3.cloned.1.call-done = f32[16,2304]{1,0:T(8,128)} async-done(((f32[512,2304]{1,0:T(8,128)}), f32[16,2304]{1,0:T(8,128)}) %reduce-scatter.3.cloned.1.call-update) | async-done | bytes 147472 | tf_op jit(solution)/shard_map/reduce_scatter | solution.py:110
  756.6 1.6 convert_element_type.49
  (42 shorter events, 0.7 us)
Async XLA Ops:
  7.2 298.4 %copy-start = (bf16[384,2304]{1,0:T(8,128)(2,1)S(1)}, bf16[384,2304]{1,0:T(8,128)(2,1)}, u32[]{:S(2)}) copy-start(bf16[384,2304]{1,0:T(8,128)(2,1)} %param.13) | copy-start | bytes 5308420
  7.2 2.7 copy-start.2
  7.2 86.7 %all-gather.5.cloned.1.call-start = ((), (), s32[]{:S(2)}) async-start(), calls=%async_computation.6 | async-start | bytes 2433024 | tf_op jit(solution)/shard_map/all_gather | solution.py:89
  13.8 160.2 %all-gather.7.cloned.1.call-start = ((), (), s32[]{:S(2)}) async-start(), calls=%async_computation.8 | async-start | bytes 2433024 | tf_op jit(solution)/shard_map/all_gather | solution.py:89
  98.5 80.1 %all-to-all-start = ((f32[32,16,400]{2,1,0:T(8,128)}), f32[32,16,400]{2,1,0:T(8,128)S(1)}, u32[]{:S(2)}, u32[]{:S(2)}) async-start(f32[32,16,400]{2,1,0:T(8,128)} %bitcast.37), calls=%async_computation | async-start | bytes 2097152 | tf_op jit(solution)/shard_map/all_to_all | solution.py:90
  105.9 80.2 %copy-start.5 = (u32[256]{0:T(256)S(1)}, u32[256]{0:T(256)}, u32[]{:S(2)}) copy-start(u32[256]{0:T(256)} %constant.35) | copy-start | bytes 3076
  105.9 81.4 %copy-start.3 = (s32[2]{0:T(128)S(1)}, s32[2]{0:T(128)}, u32[]{:S(2)}) copy-start(s32[2]{0:T(128)} %param.15) | copy-start | bytes 28
  178.6 8.9 %copy-start.1 = (f32[32,16,400]{2,1,0:T(8,128)}, f32[32,16,400]{2,1,0:T(8,128)S(1)}, u32[]{:S(2)}) copy-start(f32[32,16,400]{2,1,0:T(8,128)S(1)} %all-to-all-done) | copy-start | bytes 2457604
  178.6 30.1 %all-to-all-start.2 = ((f32[32,16,400]{2,1,0:T(8,128)}), f32[32,16,400]{2,1,0:T(8,128)}, u32[]{:S(2)}, u32[]{:S(2)}) async-start(f32[32,16,400]{2,1,0:T(8,128)} %bitcast.36), calls=%async_computation.3 | async-start | bytes 2097152 | tf_op jit(solution)/shard_map/all_to_all | solution.py:90
  186.1 345.0 %reduce-scatter.5.cloned.1.call-start = ((), (), s32[]{:S(2)}) async-start(), calls=%async_computation.9 | async-start | bytes 4866048 | tf_op jit(solution)/shard_map/reduce_scatter | solution.py:110
  267.2 3.4 copy-start.4
  309.1 447.5 %reduce-scatter.3.cloned.1.call-start = ((), (), s32[]{:S(2)}) async-start(), calls=%async_computation.7 | async-start | bytes 4866048 | tf_op jit(solution)/shard_map/reduce_scatter | solution.py:110
Sparse Core Ops, SparseCore 0:
  13.9 79.9 all-gather.4
  97.0 76.9 all-gather.6
  309.2 221.8 reduce-scatter.4
  534.9 221.6 reduce-scatter.2
where the time goes:
time: 766 us; the launch traced here: 765 us
  waiting for transfers between devices  569 us (74%)
  blocking collectives  121 us (16%)
  matrix products  24.3 us (3%)
  starting transfers between devices  15.3 us (2%)
  between operations  14.7 us (2%)
  local copies, waits for them, and re-layouts  10.8 us (1%)
  other arithmetic  9.41 us (1%)
    reduce_scatter x2, waiting for transfers between devices, decode_layer(): lax.psum_scatter(jnp.dot(returned, w_out, preferred_element_type=jnp.floa...  405 us
    all_gather x2, waiting for transfers between devices, decode_layer(): partials = project(lax.all_gather(my_slice, 'wide', axis=0, tiled=True))  146 us
    unnamed x1, blocking collectives  51.8 us
    all_to_all x2, blocking collectives, decode_layer(): lax.all_to_all(gathered, 'wide', split_axis=1, concat_axis=0, tiled=True)  42.8 us
    all_gather x2, blocking collectives, decode_layer(): gathered = lax.all_gather(attended, 'narrow', axis=0, tiled=True)  26.1 us
    all_to_all x2, waiting for transfers between devices, decode_layer(): lax.all_to_all(partials, 'wide', split_axis=0, concat_axis=1, tiled=True)  17.9 us
  transfers between devices with their start and end apart: 6, of which 5 were waited for; matrix products, arithmetic and copies ran while one was open for 3% of the time, Pallas kernels for 0%

commit v1 on v0

v1 whole, which is shorter than its diff:
```python
import jax
import jax.numpy as jnp
from jax import lax
from jax.experimental import pallas as pl
from jax.experimental.pallas import tpu as pltpu
from jax.sharding import Mesh, PartitionSpec as P

HEADS = 48
EPSILON = 1e-05
NEG_FILL = -1e30
F32 = jnp.float32
BF16 = jnp.bfloat16


def normalize(inputs, gain, start, width):
    values = inputs.astype(F32)
    average = jnp.mean(values, axis=-1, keepdims=True)
    variance = jnp.mean(values * values, axis=-1, keepdims=True) - average * average
    own = lax.dynamic_slice_in_dim(inputs, start, width, 1).astype(F32)
    own_gain = lax.dynamic_slice_in_dim(gain, start, width, 0)
    return ((own - average) * lax.rsqrt(variance + EPSILON) * own_gain).astype(BF16)


def attend(queries, keyval, cache, lengths):
    steps, seqs, heads, size = queries.shape
    scale = size ** (-0.5)
    rows = queries.transpose(1, 0, 2, 3).reshape(seqs, steps * heads, size)
    keys, values = cache[:, :, :size], cache[:, :, size:]
    new = keyval.transpose(1, 0, 2)
    new_keys, new_values = new[:, :, :size], new[:, :, size:]
    live = (jnp.arange(cache.shape[1])[None, :] < lengths[:, None])[:, None, :]
    step_of = jnp.repeat(jnp.arange(steps), heads)
    new_live = (jnp.arange(steps)[None, :] <= step_of[:, None])[None]
    scores = jnp.einsum("srd,smd->srm", rows, keys, preferred_element_type=F32) * scale
    extra = jnp.einsum("srd,sjd->srj", rows, new_keys, preferred_element_type=F32) * scale
    scores = jnp.where(live, scores, NEG_FILL)
    extra = jnp.where(new_live, extra, NEG_FILL)
    top = jnp.maximum(jnp.max(scores, axis=-1), jnp.max(extra, axis=-1))[..., None]
    weights = jnp.where(live, jnp.exp(scores - top), 0.0)
    extra_weights = jnp.where(new_live, jnp.exp(extra - top), 0.0)
    total = jnp.sum(weights, axis=-1) + jnp.sum(extra_weights, axis=-1)
    out = jnp.einsum("srm,smd->srd", weights.astype(BF16), values, preferred_element_type=F32)
    out = out + jnp.einsum(
        "srj,sjd->srd", extra_weights.astype(BF16), new_values, preferred_element_type=F32
    )
    out = (out / total[..., None]).astype(BF16)
    return out.reshape(seqs, steps, heads * size).transpose(1, 0, 2)


def shift(value, axis, by):
    count = lax.axis_size(axis)
    return lax.ppermute(value, axis, [(i, (i + by) % count) for i in range(count)])


def add(*terms):
    return sum(t.astype(F32) for t in terms).astype(BF16)


def ring_gather(block, axis):
    half = lax.axis_size(axis) // 2
    up, down = [block], [block]
    for _ in range(half - 1):
        up.append(shift(up[-1], axis, 1))
        down.append(shift(down[-1], axis, -1))
    cut = block.shape[0] // 2
    far = jnp.concatenate([shift(up[-1][:cut], axis, 1), shift(down[-1][cut:], axis, -1)])
    return down + [far] + up[:0:-1]


def near_gather(block, axis):
    return [block] + [shift(block, axis, -k) for k in range(1, lax.axis_size(axis))]


def ring_scatter(stack, axis):
    count = lax.axis_size(axis)
    half = count // 2
    here = lax.axis_index(axis)

    def own(k):
        return lax.dynamic_index_in_dim(stack, lax.rem(here + k, count), 0, keepdims=False)

    far = own(half)
    cut = far.shape[0] // 2
    up, down = shift(far[:cut], axis, 1), shift(far[cut:], axis, -1)
    for k in range(half - 1, 0, -1):
        upper, lower = own(k), own(count - k)
        if k == half - 1:
            upper = jnp.concatenate([add(upper[:cut], up), upper[cut:]])
            lower = jnp.concatenate([lower[:cut], add(lower[cut:], down)])
        else:
            upper, lower = add(upper, up), add(lower, down)
        up, down = shift(upper, axis, 1), shift(lower, axis, -1)
    return add(own(0), up, down)


def near_scatter(stack, axis):
    count = lax.axis_size(axis)
    here = lax.axis_index(axis)
    own = [
        lax.dynamic_index_in_dim(stack, lax.rem(here + k, count), 0, keepdims=False)
        for k in range(count)
    ]
    return add(own[0], *(shift(own[k], axis, k) for k in range(1, count)))


def turn(value, dim, by):
    count = value.shape[dim]
    twice = jnp.concatenate([value, value], axis=dim)
    return lax.dynamic_slice_in_dim(twice, lax.rem(count - by, count), count, dim)


def ring_pieces(block, axis):
    half = lax.axis_size(axis) // 2
    up, down = [block], [block]
    for _ in range(half - 1):
        up.append(shift(up[-1], axis, 1))
        down.append(shift(down[-1], axis, -1))
    return down + [shift(up[-1], axis, 1)] + up[:0:-1]


def project_kernel(pieces, blocks, *refs):
    place_ref, refs = refs[0], refs[1:]
    row_refs, refs = refs[:pieces], refs[pieces:]
    weight_refs, refs = refs[:blocks], refs[blocks:]
    keyval_ref, keep_ref, give_ref, rows, sums, kept, given = refs
    here, core = place_ref[0], place_ref[1]
    nx, ny, out_rows, _ = keep_ref.shape
    depth, wide_cols = keyval_ref.shape[0], weight_refs[0].shape[1]
    per = out_rows // pieces
    part = nx * per
    count = row_refs[0].shape[0]
    group = sums.shape[0] // count
    for first in range(0, pieces, group):
        for p in range(group):
            rows[p * count : (p + 1) * count, :] = row_refs[first + p][...]
        for k in range(blocks):
            column = lax.rem(here + blocks - k, blocks) * wide_cols
            sums[:, pl.ds(pl.multiple_of(column, 128), wide_cols)] = jnp.dot(
                rows[...], weight_refs[k][:depth, :], preferred_element_type=F32
            )
        sums[:, blocks * wide_cols :] = jnp.dot(
            rows[...], keyval_ref[...], preferred_element_type=F32
        )
        for p in range(group):
            for y in range(ny):
                at = p * count + y * 2 * part
                mine = sums[pl.ds(pl.multiple_of(at + core * part, 8), part), :]
                theirs = sums[pl.ds(pl.multiple_of(at + (1 - core) * part, 8), part), :]
                slot = (first + p) * per
                for x in range(nx):
                    kept[x, y, slot : slot + per, :] = mine[x * per : (x + 1) * per]
                    given[x, y, slot : slot + per, :] = theirs[x * per : (x + 1) * per]
    for x in range(nx):
        keep_ref[x] = kept[x].astype(BF16)
        give_ref[x] = given[x].astype(BF16)


def project(place, pieces, weights, keyval, nx, per):
    blocks, cols = len(weights), weights[0].shape[1]
    depth = keyval.shape[0]
    count = pieces[0].shape[0]
    total = blocks * cols + keyval.shape[1]
    ny = count // (2 * nx * per)
    shape = (nx, ny, len(pieces) * per, total)
    group = len(pieces) // 2
    whole = pl.BlockSpec(memory_space=pltpu.VMEM)
    return pl.pallas_call(
        lambda *refs: project_kernel(len(pieces), blocks, *refs),
        in_specs=[pl.BlockSpec(memory_space=pltpu.SMEM)] + [whole] * (len(pieces) + blocks + 1),
        out_specs=[whole, whole],
        out_shape=[jax.ShapeDtypeStruct(shape, BF16)] * 2,
        scratch_shapes=[
            pltpu.VMEM((group * count, depth), BF16),
            pltpu.VMEM((group * count, total), F32),
            pltpu.VMEM(shape, F32),
            pltpu.VMEM(shape, F32),
        ],
        compiler_params=pltpu.CompilerParams(vmem_limit_bytes=40 * 2**20),
        cost_estimate=pl.CostEstimate(
            flops=2 * count * len(pieces) * depth * total,
            bytes_accessed=2 * total * (depth + count * len(pieces)),
            transcendentals=0,
        ),
    )(place, *pieces, *weights, keyval)


def shards(step_one, step_two, gain, w_query, w_keyval, w_out, kv_cache, lengths):
    ny, nz, nx, nc = (lax.axis_size(a) for a in ("y", "z", "x", "core"))
    wide, narrow = ny * nz, nx * nc
    here, core = lax.axis_index("y"), lax.axis_index("core")
    width, query_cols = w_query.shape
    pair_cols = w_keyval.shape[1]
    size = kv_cache.shape[2] // 2
    seqs = kv_cache.shape[0]
    per = 2 * seqs
    start = (lax.axis_index("x") * nc + core) * width
    depth = width // ny
    extra = depth * pair_cols // query_cols

    quarters = w_query.reshape(ny, depth, query_cols)
    smalls = w_keyval.reshape(ny, extra, query_cols)

    def quarter(k):
        at = lax.rem(here + k, ny)
        return jnp.concatenate(
            [
                lax.dynamic_index_in_dim(quarters, at, 0, keepdims=False),
                lax.dynamic_index_in_dim(smalls, at, 0, keepdims=False),
            ]
        )

    weights = [quarter(0)] + [shift(quarter(k), "y", k) for k in range(1, ny)]
    smalls = jnp.stack([w[depth:] for w in weights]).reshape(ny, depth, pair_cols)
    smalls = [
        lax.dynamic_index_in_dim(smalls, lax.rem(here + ny - i, ny), 0, keepdims=False)
        for i in range(ny)
    ]
    pad = jnp.zeros((depth, -ny * pair_cols % 128), BF16)
    keyval_weights = jnp.concatenate(smalls + [pad], axis=1)

    both = jnp.stack([normalize(s, gain, start, width) for s in (step_one, step_two)])
    mine = both.reshape(2, nx, nc, seqs, ny, depth).transpose(4, 2, 1, 0, 3, 5)
    mine = mine.reshape(ny, narrow * per, depth)
    column = lax.all_to_all(mine, "y", split_axis=0, concat_axis=0, tiled=True)
    pieces = ring_pieces(column.reshape(ny * narrow * per, depth), "z")
    place = jnp.stack([here, core]).astype(jnp.int32)
    keep, give = project(place, pieces, weights, keyval_weights, nx, per)
    cols = keep.shape[3]
    other = lax.ppermute(give, "core", [(0, 1), (1, 0)])
    pair = add(keep, other).reshape(nx * ny, nz * per, cols)
    terms = lax.all_to_all(pair, ("x", "y"), split_axis=0, concat_axis=0, tiled=True)
    summed = add(*(terms[i] for i in range(nx * ny))).reshape(nz, per, cols)
    summed = turn(summed, 0, lax.axis_index("z"))
    arrived = lax.all_to_all(summed, "z", split_axis=0, concat_axis=0, tiled=True)
    queries = arrived[:, :, : ny * query_cols].reshape(nz, per, ny, query_cols)
    queries = queries.transpose(1, 2, 0, 3).reshape(2, seqs, HEADS, size)
    keyval = arrived[:, :, ny * query_cols : ny * (query_cols + pair_cols)]
    keyval = keyval.reshape(nz, per, ny, pair_cols)
    keyval = keyval.transpose(1, 2, 0, 3).reshape(2, seqs, 2 * size)
    attended = attend(queries, keyval, kv_cache, lengths)
    leaving = attended.reshape(per, wide, query_cols).transpose(1, 0, 2)
    returned = lax.all_to_all(leaving, ("y", "z"), split_axis=0, concat_axis=0, tiled=True)
    returned = returned.reshape(wide * per, query_cols)
    copies = jnp.broadcast_to(returned, (nx, *returned.shape))
    gathered = lax.all_to_all(copies, "x", split_axis=0, concat_axis=0, tiled=True)
    gathered = lax.all_gather(gathered, "core", axis=0, tiled=False)
    gathered = gathered.reshape(nc, nx, ny, nz, per, query_cols).transpose(3, 2, 0, 1, 4, 5)
    gathered = gathered.reshape(wide * narrow * per, query_cols)
    out = jnp.dot(gathered, w_out, preferred_element_type=F32).astype(BF16)
    far = out.shape[1]
    out = lax.psum_scatter(out, "z", scatter_dimension=0, tiled=True)
    out = near_scatter(out.reshape(ny, narrow * per, far), "y")
    out = out.reshape(nc, nx, 2, seqs, far).transpose(2, 1, 0, 3, 4)
    out = out.reshape(2, narrow * seqs, far)
    return (out[0], out[1])


def solution(mesh):
    fine = Mesh(mesh.devices.reshape(4, 8, 4, 2), ("y", "z", "x", "core"))
    wide, narrow = ("y", "z"), ("x", "core")
    return jax.shard_map(
        shards,
        mesh=fine,
        in_specs=(
            P(wide, None),
            P(wide, None),
            P(),
            P(narrow, wide),
            P(narrow, wide),
            P(wide, narrow),
            P(wide + narrow, None, None),
            P(wide + narrow),
        ),
        out_specs=(P(wide, narrow), P(wide, narrow)),
        check_vma=False,
    )
```

time: 766 us -> 240 us (0.31)
  waiting for transfers between devices: 569 us -> 106 us
  blocking collectives: 121 us -> 25.3 us
  starting transfers between devices: 15.3 us -> 40.5 us
  matrix products: 24.3 us -> 7.68 us
  local copies, waits for them, and re-layouts: 10.8 us -> 22.9 us
    reduce_scatter x2 -> x1, waiting for transfers between devices: 405 us -> 54.4 us  [shards(): out = lax.psum_scatter(out, 'z', scatter_dimension=0, tiled=True)]
    all_gather x2 -> x0, waiting for transfers between devices: 146 us -> none  [decode_layer(): partials = project(lax.all_gather(my_slice, 'wide', axis=0, tiled=True))]
    unnamed x1 -> x0, blocking collectives: 51.8 us -> none
    all_gather x2 -> x1, blocking collectives: 26.1 us -> 2.36 us  [shards(): gathered = lax.all_gather(gathered, 'core', axis=0, tiled=False)]
    ppermute x0 -> x14, starting transfers between devices: none -> 23 us  [the longest x13 22.9 us: shift(): lax.ppermute(value, axis, [(i, (i + by) % count) for i in range(count)])]
    all_to_all x2, blocking collectives: 42.8 us -> 23 us  [the longest x1 13.2 us: shards(): lax.all_to_all(leaving, ('y', 'z'), split_axis=0, concat_axis=0, tiled=True)]
    all_to_all x2 -> x3, waiting for transfers between devices: 17.9 us -> 35.9 us  [the longest x1 24.4 us: shards(): lax.all_to_all(pair, ('x', 'y'), split_axis=0, concat_axis=0, tiled=True)]
    dot_general x11 -> x5, matrix products: 24.3 us -> 7.68 us  [the longest x1 4.2 us: shards(): out = jnp.dot(gathered, w_out, preferred_element_type=F32).astype(BF16)]
  transfers between devices with their start and end apart: 6 -> 18, of which waited for: 5 -> 13; matrix products, arithmetic and copies ran while one was open for 3% -> 8% of each run, Pallas kernels for 0% -> 0%
where the time goes in v1:
time: 240 us; the launch traced here: 238 us
  waiting for transfers between devices  106 us (44%)
  starting transfers between devices  40.5 us (17%)
  blocking collectives  25.3 us (11%)
  local copies, waits for them, and re-layouts  22.9 us (10%)
  other arithmetic  14.7 us (6%)
  between operations  14.4 us (6%)
  matrix products  7.68 us (3%)
  Pallas kernels  6.25 us (3%)
    reduce_scatter x1, waiting for transfers between devices, shards(): out = lax.psum_scatter(out, 'z', scatter_dimension=0, tiled=True)  54.4 us
    all_to_all x1, waiting for transfers between devices, shards(): lax.all_to_all(pair, ('x', 'y'), split_axis=0, concat_axis=0, tiled=True)  24.4 us
    ppermute x13, starting transfers between devices, shift(): lax.ppermute(value, axis, [(i, (i + by) % count) for i in range(count)])  22.9 us
    all_to_all x1, blocking collectives, shards(): lax.all_to_all(leaving, ('y', 'z'), split_axis=0, concat_axis=0, tiled=True)  13.2 us
    ppermute x13, waiting for transfers between devices, shift(): lax.ppermute(value, axis, [(i, (i + by) % count) for i in range(count)])  12.6 us
    all_to_all x1, blocking collectives, shards(): lax.all_to_all(copies, 'x', split_axis=0, concat_axis=0, tiled=True)  9.79 us
    all_to_all x1, waiting for transfers between devices, shards(): lax.all_to_all(summed, 'z', split_axis=0, concat_axis=0, tiled=True)  8.76 us
    all_to_all x1, starting transfers between devices, shards(): lax.all_to_all(summed, 'z', split_axis=0, concat_axis=0, tiled=True)  6.42 us
  transfers between devices with their start and end apart: 18, of which 13 were waited for; matrix products, arithmetic and copies ran while one was open for 8% of the time, Pallas kernels for 0%

profile of v1, /device:TPU:8, one launch (start us, length us, event | category | flops | bytes accessed | tf_op | source)
XLA Modules:
  0.0 238.3 jit_solution(8104380711831303782)
XLA Ops:
  7.2 1.3 copy.42
  9.0 2.4 dynamic-slice_bitcast_fusion
  11.3 0.8 pad_maximum_fusion.1
  12.1 1.6 collective-permute-start.7
  13.7 1.3 convert_reduce_fusion.1
  15.0 1.3 convert_reduce_fusion
  17.2 1.0 multiply_convert_fusion.1
  19.6 5.1 %all-to-all-start = ((bf16[4,32,576]{2,1,0:T(8,128)(2,1)}), bf16[4,32,576]{2,1,0:T(8,128)(2,1)S(1)}, u32[]{:S(2)}, u32[]{:S(2)}) async-start(bf16[4,32,576]{2,1,0:T(8,128)(2,1)} %reshape.208), calls=%async_computation | async-start | bytes 327680 | tf_op jit(solution)/shard_map/all_to_all | solution.py:224
  24.7 0.8 pad_maximum_fusion.2
  25.5 2.1 collective-permute-start.8
  27.6 2.7 %all-to-all-done = bf16[4,32,576]{2,1,0:T(8,128)(2,1)S(1)} async-done(((bf16[4,32,576]{2,1,0:T(8,128)(2,1)}), bf16[4,32,576]{2,1,0:T(8,128)(2,1)S(1)}, u32[]{:S(2)}, u32[]{:S(2)}) %all-to-all-start) | async-done | bytes 147488 | tf_op jit(solution)/shard_map/all_to_all | solution.py:224
  30.3 1.1 collective-permute-start.3
  32.2 1.9 collective-permute-start.9
  34.0 3.9 %collective-permute-start = (bf16[128,576]{1,0:T(8,128)(2,1)S(1)}, bf16[128,576]{1,0:T(8,128)(2,1)}, u32[]{:S(2)}, u32[]{:S(2)}) collective-permute-start(bf16[128,576]{1,0:T(8,128)(2,1)S(1)} %bitcast.63), channel_id=1, source_target_pairs={{0,56},{8,0},{16,8},{24,16},{32,24},{40,32},{48,40},{56,48},{1,57}... | collective-permute-start | bytes 442376 | tf_op jit(solution)/shard_map/ppermute | solution.py:52
  38.6 2.2 collective-permute-done.refs_2_
  40.8 3.8 %collective-permute-start.1 = (bf16[128,576]{1,0:T(8,128)(2,1)}, bf16[128,576]{1,0:T(8,128)(2,1)}, u32[]{:S(2)}, u32[]{:S(2)}) collective-permute-start(bf16[128,576]{1,0:T(8,128)(2,1)} %collective-permute-done.refs_2_), channel_id=1, source_target_pairs={{0,56},{8,0},{16,8},{24,16},{32,24},{40,32},{48,40},{56,48},{1,57}... | collective-permute-start | bytes 442376 | tf_op jit(solution)/shard_map/ppermute | solution.py:52
  45.7 1.1 pad_maximum_fusion.refs_9_
  46.8 2.2 collective-permute-done.1.refs_3_
  49.0 3.7 %collective-permute-start.2 = (bf16[128,576]{1,0:T(8,128)(2,1)}, bf16[128,576]{1,0:T(8,128)(2,1)}, u32[]{:S(2)}, u32[]{:S(2)}) collective-permute-start(bf16[128,576]{1,0:T(8,128)(2,1)} %collective-permute-done.1.refs_3_), channel_id=1, source_target_pairs={{0,56},{8,0},{16,8},{24,16},{32,24},{40,32},{48,40},{56,48},{1,57}... | collective-permute-start | bytes 442376 | tf_op jit(solution)/shard_map/ppermute | solution.py:52
  53.3 1.4 slice.112
  54.6 0.9 stack.42
  60.8 1.5 concatenate.24.refs_13_
  63.1 0.9 copy-done.2
  64.0 6.2 %shard_map.95 = (bf16[4,4,32,1664]{3,2,1,0:T(8,128)(2,1)S(1)}, bf16[4,4,32,1664]{3,2,1,0:T(8,128)(2,1)S(1)}) custom-call(s32[2]{0:T(128)S(1)} %pad_add_fusion.refs_0_, bf16[128,576]{1,0:T(8,128)(2,1)S(1)} %bitcast.64, bf16[128,576]{1,0:T(8,128)(2,1)} %collective-permute-done.refs_2_, bf16[128,576]{1,0:T(8,128)(2,1)} %collective-permute-done.1.refs_3_, ...), custom_call_target="tpu_custom_call" | custom-call | flops 1962934272 | bytes 5324800 | tf_op jit(solution)/shard_map/pallas_call | solution.py:167
  70.4 3.6 %collective-permute-done.10 = bf16[4,4,32,1664]{3,2,1,0:T(8,128)(2,1)S(1)} collective-permute-done((bf16[4,4,32,1664]{3,2,1,0:T(8,128)(2,1)S(1)}, bf16[4,4,32,1664]{3,2,1,0:T(8,128)(2,1)S(1)}, u32[]{:S(2)}, u32[]{:S(2)}) %collective-permute-start.10) | collective-permute-done | bytes 1703968 | tf_op jit(solution)/shard_map/ppermute | solution.py:229
  74.0 1.6 add_convert_fusion
  75.6 5.9 %all-to-all-start.1 = ((bf16[16,32,1664]{2,1,0:T(8,128)(2,1)}), bf16[16,32,1664]{2,1,0:T(8,128)(2,1)S(1)}, u32[]{:S(2)}, u32[]{:S(2)}) async-start(bf16[16,32,1664]{2,1,0:T(8,128)(2,1)} %bitcast.17), calls=%async_computation.1 | async-start | bytes 3407872 | tf_op jit(solution)/shard_map/all_to_all | solution.py:231
  81.7 24.4 %all-to-all-done.1 = bf16[16,32,1664]{2,1,0:T(8,128)(2,1)S(1)} async-done(((bf16[16,32,1664]{2,1,0:T(8,128)(2,1)}), bf16[16,32,1664]{2,1,0:T(8,128)(2,1)S(1)}, u32[]{:S(2)}, u32[]{:S(2)}) %all-to-all-start.1) | async-done | bytes 1703968 | tf_op jit(solution)/shard_map/all_to_all | solution.py:231
  106.8 1.7 reshape.236
  108.5 0.9 add_add_fusion
  109.4 1.0 reshape.250
  110.4 1.0 add_convert_fusion.1
  112.1 6.4 %all-to-all-start.2 = ((bf16[8,4,1664]{2,1,0:T(4,128)(2,1)}), bf16[8,4,1664]{2,1,0:T(4,128)(2,1)S(1)}, u32[]{:S(2)}, u32[]{:S(2)}) async-start(bf16[8,4,1664]{2,1,0:T(4,128)(2,1)} %fusion.25), calls=%async_computation.2 | async-start | bytes 212992 | tf_op jit(solution)/shard_map/all_to_all | solution.py:234
  118.6 8.8 %all-to-all-done.2 = bf16[8,4,1664]{2,1,0:T(4,128)(2,1)S(1)} async-done(((bf16[8,4,1664]{2,1,0:T(4,128)(2,1)}), bf16[8,4,1664]{2,1,0:T(4,128)(2,1)S(1)}, u32[]{:S(2)}, u32[]{:S(2)}) %all-to-all-start.2) | async-done | bytes 106528 | tf_op jit(solution)/shard_map/all_to_all | solution.py:234
  127.8 2.6 %fusion.33 = (f32[2,96]{1,0:T(2,128)S(1)}, f32[2,96,2048]{2,1,0:T(8,128)S(1)}) fusion(bf16[2,96,256]{2,1,0:T(8,128)(2,1)S(1)} %bitcast.74, bf16[2,2048,512]{2,1,0:T(8,128)(2,1)} %param.14, pred[2,2048]{1,0:T(4,128)(4,1)S(1)} %iota_compare_fusion), kind=kOutput, calls=%fused_computation.75 | convolution fusion | flops 202506048 | bytes 3773184 | tf_op jit(solution)/shard_map/srd,smd->srm/dot_general | solution.py:34
  132.1 13.2 %all_to_all.25 = bf16[32,4,384]{2,1,0:T(4,128)(2,1)S(1)} all-to-all(bf16[32,4,384]{2,1,0:T(4,128)(2,1)S(1)} %copy.58), channel_id=1, replica_groups=mesh['y'=4,'z'=8,'x'=4,'core'=2] {'y','z'}, dimensions={0} | all-to-all | bytes 196608 | tf_op jit(solution)/shard_map/all_to_all | solution.py:242
  145.4 9.8 %all_to_all.26 = bf16[4,128,384]{2,1,0:T(8,128)(2,1)S(1)} all-to-all(bf16[4,128,384]{2,1,0:T(8,128)(2,1)S(1)} %broadcast_in_dim.70), channel_id=1, replica_groups=mesh['y'=4,'z'=8,'x'=4,'core'=2] {'x'}, dimensions={0} | all-to-all | bytes 786432 | tf_op jit(solution)/shard_map/all_to_all | solution.py:245
  155.2 2.4 all-gather
  158.2 4.2 %convolution_convert_fusion = bf16[1024,2304]{1,0:T(8,128)(2,1)} fusion(bf16[1024,384]{1,0:T(8,128)(2,1)S(1)} %reshape.222, bf16[384,2304]{1,0:T(8,128)(2,1)S(1)} %copy-done), kind=kOutput, calls=%fused_computation | convolution fusion | flops 1814298624 | bytes 7274496 | tf_op jit(solution)/shard_map/dot_general | solution.py:249
  162.4 54.4 %reduce-scatter.2.cloned.1.call-done = bf16[128,2304]{1,0:T(8,128)(2,1)} async-done(((bf16[1024,2304]{1,0:T(8,128)(2,1)}), bf16[128,2304]{1,0:T(8,128)(2,1)}) %reduce-scatter.2.cloned.1.call-update) | async-done | bytes 589840 | tf_op jit(solution)/shard_map/reduce_scatter | solution.py:251
  216.9 1.1 dynamic-slice_bitcast_fusion.6
  217.9 1.6 collective-permute-start.11
  219.5 1.1 collective-permute-start.12
  220.6 2.2 collective-permute-start.13
  222.8 1.5 collective-permute-done.11
  224.3 3.5 %collective-permute-done.12 = bf16[32,2304]{1,0:T(8,128)(2,1)S(1)} collective-permute-done((bf16[32,2304]{1,0:T(8,128)(2,1)S(1)}, bf16[32,2304]{1,0:T(8,128)(2,1)S(1)}, u32[]{:S(2)}, u32[]{:S(2)}) %collective-permute-start.12) | collective-permute-done | bytes 147488 | tf_op jit(solution)/shard_map/ppermute | solution.py:52
  227.8 1.1 collective-permute-done.13
  228.9 1.0 fusion.24
  (88 shorter events, 17.9 us)
Async XLA Ops:
  7.2 151.0 %copy-start = (bf16[384,2304]{1,0:T(8,128)(2,1)S(1)}, bf16[384,2304]{1,0:T(8,128)(2,1)}, u32[]{:S(2)}) copy-start(bf16[384,2304]{1,0:T(8,128)(2,1)} %param.13) | copy-start | bytes 5308420
  12.1 40.5 %collective-permute-start.7 = (bf16[600,384]{1,0:T(8,128)(2,1)}, bf16[600,384]{1,0:T(8,128)(2,1)S(1)}, u32[]{:S(2)}, u32[]{:S(2)}) collective-permute-start(bf16[600,384]{1,0:T(8,128)(2,1)} %pad_maximum_fusion.1), channel_id=1, source_target_pairs={{0,64},{64,128},{128,192},{192,0},{1,65},{65,129},{129,193},{193,1... | collective-permute-start | bytes 1382408 | tf_op jit(solution)/shard_map/ppermute | solution.py:52
  19.6 10.7 %all-to-all-start = ((bf16[4,32,576]{2,1,0:T(8,128)(2,1)}), bf16[4,32,576]{2,1,0:T(8,128)(2,1)S(1)}, u32[]{:S(2)}, u32[]{:S(2)}) async-start(bf16[4,32,576]{2,1,0:T(8,128)(2,1)} %reshape.208), calls=%async_computation | async-start | bytes 327680 | tf_op jit(solution)/shard_map/all_to_all | solution.py:224
  25.5 27.4 %collective-permute-start.8 = (bf16[600,384]{1,0:T(8,128)(2,1)}, bf16[600,384]{1,0:T(8,128)(2,1)S(1)}, u32[]{:S(2)}, u32[]{:S(2)}) collective-permute-start(bf16[600,384]{1,0:T(8,128)(2,1)} %pad_maximum_fusion.2), channel_id=1, source_target_pairs={{0,128},{64,192},{128,0},{192,64},{1,129},{65,193},{129,1},{193,65... | collective-permute-start | bytes 1382408 | tf_op jit(solution)/shard_map/ppermute | solution.py:52
  30.3 8.3 %collective-permute-start.3 = (bf16[128,576]{1,0:T(8,128)(2,1)S(1)}, bf16[128,576]{1,0:T(8,128)(2,1)S(1)}, u32[]{:S(2)}, u32[]{:S(2)}) collective-permute-start(bf16[128,576]{1,0:T(8,128)(2,1)S(1)} %bitcast.62), channel_id=1, source_target_pairs={{0,8},{8,16},{16,24},{24,32},{32,40},{40,48},{48,56},{56,0},{1,9},... | collective-permute-start | bytes 442376 | tf_op jit(solution)/shard_map/ppermute | solution.py:52
  32.2 21.1 %collective-permute-start.9 = (bf16[600,384]{1,0:T(8,128)(2,1)}, bf16[600,384]{1,0:T(8,128)(2,1)}, u32[]{:S(2)}, u32[]{:S(2)}) collective-permute-start(bf16[600,384]{1,0:T(8,128)(2,1)} %pad_maximum_fusion.3), channel_id=1, source_target_pairs={{0,192},{64,0},{128,64},{192,128},{1,193},{65,1},{129,65},{193,129... | collective-permute-start | bytes 1382408 | tf_op jit(solution)/shard_map/ppermute | solution.py:52
  34.0 6.8 %collective-permute-start = (bf16[128,576]{1,0:T(8,128)(2,1)S(1)}, bf16[128,576]{1,0:T(8,128)(2,1)}, u32[]{:S(2)}, u32[]{:S(2)}) collective-permute-start(bf16[128,576]{1,0:T(8,128)(2,1)S(1)} %bitcast.63), channel_id=1, source_target_pairs={{0,56},{8,0},{16,8},{24,16},{32,24},{40,32},{48,40},{56,48},{1,57}... | collective-permute-start | bytes 442376 | tf_op jit(solution)/shard_map/ppermute | solution.py:52
  38.6 7.1 %copy-start.1 = (bf16[128,576]{1,0:T(8,128)(2,1)}, bf16[128,576]{1,0:T(8,128)(2,1)S(1)}, u32[]{:S(2)}) copy-start(bf16[128,576]{1,0:T(8,128)(2,1)S(1)} %collective-permute-done.3.refs_8_) | copy-start | bytes 442372
  38.6 6.8 %collective-permute-start.4 = (bf16[128,576]{1,0:T(8,128)(2,1)S(1)}, bf16[128,576]{1,0:T(8,128)(2,1)}, u32[]{:S(2)}, u32[]{:S(2)}) collective-permute-start(bf16[128,576]{1,0:T(8,128)(2,1)S(1)} %collective-permute-done.3.refs_8_), channel_id=1, source_target_pairs={{0,8},{8,16},{16,24},{24,32},{32,40},{40,48},{48,56},{56,0},{1,9},... | collective-permute-start | bytes 442376 | tf_op jit(solution)/shard_map/ppermute | solution.py:52
  40.8 8.2 %collective-permute-start.1 = (bf16[128,576]{1,0:T(8,128)(2,1)}, bf16[128,576]{1,0:T(8,128)(2,1)}, u32[]{:S(2)}, u32[]{:S(2)}) collective-permute-start(bf16[128,576]{1,0:T(8,128)(2,1)} %collective-permute-done.refs_2_), channel_id=1, source_target_pairs={{0,56},{8,0},{16,8},{24,16},{32,24},{40,32},{48,40},{56,48},{1,57}... | collective-permute-start | bytes 442376 | tf_op jit(solution)/shard_map/ppermute | solution.py:52
  45.3 10.9 %collective-permute-start.5 = (bf16[128,576]{1,0:T(8,128)(2,1)}, bf16[128,576]{1,0:T(8,128)(2,1)}, u32[]{:S(2)}, u32[]{:S(2)}) collective-permute-start(bf16[128,576]{1,0:T(8,128)(2,1)} %collective-permute-done.4.refs_7_), channel_id=1, source_target_pairs={{0,8},{8,16},{16,24},{24,32},{32,40},{40,48},{48,56},{56,0},{1,9},... | collective-permute-start | bytes 442376 | tf_op jit(solution)/shard_map/ppermute | solution.py:52
  49.0 13.3 %collective-permute-start.2 = (bf16[128,576]{1,0:T(8,128)(2,1)}, bf16[128,576]{1,0:T(8,128)(2,1)}, u32[]{:S(2)}, u32[]{:S(2)}) collective-permute-start(bf16[128,576]{1,0:T(8,128)(2,1)} %collective-permute-done.1.refs_3_), channel_id=1, source_target_pairs={{0,56},{8,0},{16,8},{24,16},{32,24},{40,32},{48,40},{56,48},{1,57}... | collective-permute-start | bytes 442376 | tf_op jit(solution)/shard_map/ppermute | solution.py:52
  56.3 6.8 %collective-permute-start.6 = (bf16[128,576]{1,0:T(8,128)(2,1)}, bf16[128,576]{1,0:T(8,128)(2,1)}, u32[]{:S(2)}, u32[]{:S(2)}) collective-permute-start(bf16[128,576]{1,0:T(8,128)(2,1)} %collective-permute-done.5.refs_6_), channel_id=1, source_target_pairs={{0,8},{8,16},{16,24},{24,32},{32,40},{40,48},{48,56},{56,0},{1,9},... | collective-permute-start | bytes 442376 | tf_op jit(solution)/shard_map/ppermute | solution.py:52
  63.1 0.9 copy-start.2
  70.3 3.7 %collective-permute-start.10 = (bf16[4,4,32,1664]{3,2,1,0:T(8,128)(2,1)S(1)}, bf16[4,4,32,1664]{3,2,1,0:T(8,128)(2,1)S(1)}, u32[]{:S(2)}, u32[]{:S(2)}) collective-permute-start(bf16[4,4,32,1664]{3,2,1,0:T(8,128)(2,1)S(1)} %get-tuple-element.5), channel_id=1, source_target_pairs={{0,1},{1,0},{2,3},{3,2},{4,5},{5,4},{6,7},{7,6},{8,9},{9,8},{10,11... | collective-permute-start | bytes 5111816 | tf_op jit(solution)/shard_map/ppermute | solution.py:229
  75.6 6.0 %copy-start.3 = (s32[2]{0:T(128)S(1)}, s32[2]{0:T(128)}, u32[]{:S(2)}) copy-start(s32[2]{0:T(128)} %param.15) | copy-start | bytes 28
  75.6 30.5 %all-to-all-start.1 = ((bf16[16,32,1664]{2,1,0:T(8,128)(2,1)}), bf16[16,32,1664]{2,1,0:T(8,128)(2,1)S(1)}, u32[]{:S(2)}, u32[]{:S(2)}) async-start(bf16[16,32,1664]{2,1,0:T(8,128)(2,1)} %bitcast.17), calls=%async_computation.1 | async-start | bytes 3407872 | tf_op jit(solution)/shard_map/all_to_all | solution.py:231
  112.1 15.2 %all-to-all-start.2 = ((bf16[8,4,1664]{2,1,0:T(4,128)(2,1)}), bf16[8,4,1664]{2,1,0:T(4,128)(2,1)S(1)}, u32[]{:S(2)}, u32[]{:S(2)}) async-start(bf16[8,4,1664]{2,1,0:T(4,128)(2,1)} %fusion.25), calls=%async_computation.2 | async-start | bytes 212992 | tf_op jit(solution)/shard_map/all_to_all | solution.py:234
  118.5 98.3 %reduce-scatter.2.cloned.1.call-start = ((), (), s32[]{:S(2)}) async-start(), calls=%async_computation.6 | async-start | bytes 5308416 | tf_op jit(solution)/shard_map/reduce_scatter | solution.py:251
  127.8 3.5 %copy-start.4 = (bf16[2,2048,512]{2,1,0:T(8,128)(2,1)S(1)}, bf16[2,2048,512]{2,1,0:T(8,128)(2,1)}, u32[]{:S(2)}) copy-start(bf16[2,2048,512]{2,1,0:T(8,128)(2,1)} %param.14) | copy-start | bytes 12582916
  217.9 6.4 %collective-permute-start.11 = (bf16[32,2304]{1,0:T(8,128)(2,1)S(1)}, bf16[32,2304]{1,0:T(8,128)(2,1)S(1)}, u32[]{:S(2)}, u32[]{:S(2)}) collective-permute-start(bf16[32,2304]{1,0:T(8,128)(2,1)S(1)} %get-tuple-element.14), channel_id=1, source_target_pairs={{0,64},{64,128},{128,192},{192,0},{1,65},{65,129},{129,193},{193,1... | collective-permute-start | bytes 442376 | tf_op jit(solution)/shard_map/ppermute | solution.py:52
  219.5 8.3 %collective-permute-start.12 = (bf16[32,2304]{1,0:T(8,128)(2,1)S(1)}, bf16[32,2304]{1,0:T(8,128)(2,1)S(1)}, u32[]{:S(2)}, u32[]{:S(2)}) collective-permute-start(bf16[32,2304]{1,0:T(8,128)(2,1)S(1)} %get-tuple-element.16), channel_id=1, source_target_pairs={{0,128},{64,192},{128,0},{192,64},{1,129},{65,193},{129,1},{193,65... | collective-permute-start | bytes 442376 | tf_op jit(solution)/shard_map/ppermute | solution.py:52
  220.6 8.2 %collective-permute-start.13 = (bf16[32,2304]{1,0:T(8,128)(2,1)S(1)}, bf16[32,2304]{1,0:T(8,128)(2,1)S(1)}, u32[]{:S(2)}, u32[]{:S(2)}) collective-permute-start(bf16[32,2304]{1,0:T(8,128)(2,1)S(1)} %get-tuple-element.15), channel_id=1, source_target_pairs={{0,192},{64,0},{128,64},{192,128},{1,193},{65,1},{129,65},{193,129... | collective-permute-start | bytes 442376 | tf_op jit(solution)/shard_map/ppermute | solution.py:52
Sparse Core Ops, SparseCore 0:
  162.5 54.2 reduce-scatter.1

commit v2 on v1

v2 whole, which is shorter than its diff:
```python
import jax
import jax.numpy as jnp
from jax import lax
from jax.experimental import pallas as pl
from jax.experimental.pallas import tpu as pltpu
from jax.sharding import Mesh, PartitionSpec as P

HEADS = 48
EPSILON = 1e-05
NEG_FILL = -1e30
F32 = jnp.float32
BF16 = jnp.bfloat16


def attend(queries, keyval, cache, lengths):
    steps, seqs, heads, size = queries.shape
    scale = size ** (-0.5)
    rows = queries.transpose(1, 0, 2, 3).reshape(seqs, steps * heads, size)
    keys, values = cache[:, :, :size], cache[:, :, size:]
    new = keyval.transpose(1, 0, 2)
    new_keys, new_values = new[:, :, :size], new[:, :, size:]
    live = (jnp.arange(cache.shape[1])[None, :] < lengths[:, None])[:, None, :]
    step_of = jnp.repeat(jnp.arange(steps), heads)
    new_live = (jnp.arange(steps)[None, :] <= step_of[:, None])[None]
    scores = jnp.einsum("srd,smd->srm", rows, keys, preferred_element_type=F32) * scale
    extra = jnp.einsum("srd,sjd->srj", rows, new_keys, preferred_element_type=F32) * scale
    scores = jnp.where(live, scores, NEG_FILL)
    extra = jnp.where(new_live, extra, NEG_FILL)
    top = jnp.maximum(jnp.max(scores, axis=-1), jnp.max(extra, axis=-1))[..., None]
    weights = jnp.where(live, jnp.exp(scores - top), 0.0)
    extra_weights = jnp.where(new_live, jnp.exp(extra - top), 0.0)
    total = jnp.sum(weights, axis=-1) + jnp.sum(extra_weights, axis=-1)
    out = jnp.einsum("srm,smd->srd", weights.astype(BF16), values, preferred_element_type=F32)
    out = out + jnp.einsum(
        "srj,sjd->srd", extra_weights.astype(BF16), new_values, preferred_element_type=F32
    )
    out = (out / total[..., None]).astype(BF16)
    return out.reshape(seqs, steps, heads * size).transpose(1, 0, 2)


VMEM = pl.BlockSpec(memory_space=pltpu.VMEM)
SMEM = pl.BlockSpec(memory_space=pltpu.SMEM)


def call(kernel, inputs, outputs, scratch, flops=0, mib=40):
    moved = sum(a.size * a.dtype.itemsize for a in (*inputs[1:], *outputs))
    return pl.pallas_call(
        kernel,
        in_specs=[SMEM] + [VMEM] * (len(inputs) - 1),
        out_specs=[VMEM] * len(outputs),
        out_shape=outputs,
        scratch_shapes=scratch,
        compiler_params=pltpu.CompilerParams(vmem_limit_bytes=mib * 2**20),
        cost_estimate=pl.CostEstimate(flops=flops, bytes_accessed=moved, transcendentals=0),
    )(*inputs)


def normalize(start, steps, gain, nx, nc, ny, width):
    count = steps[0].shape[0]
    seqs = count // (nx * nc)
    depth = width // ny

    def kernel(start_ref, one_ref, two_ref, gain_ref, out_ref, rows):
        columns = pl.ds(pl.multiple_of(start_ref[0], 128), width)
        scales = gain_ref[:, columns]
        for t, ref in enumerate((one_ref, two_ref)):
            values = ref[...].astype(F32)
            average = jnp.mean(values, axis=-1, keepdims=True)
            variance = jnp.mean(values * values, axis=-1, keepdims=True) - average * average
            own = ref[:, columns].astype(F32)
            normed = (own - average) * lax.rsqrt(variance + EPSILON) * scales
            for n in range(nx * nc):
                x, c = n // nc, n % nc
                at = ((c * nx + x) * 2 + t) * seqs
                rows[at : at + seqs, :] = normed[n * seqs : (n + 1) * seqs]
        for k in range(ny):
            out_ref[k] = rows[:, k * depth : (k + 1) * depth].astype(BF16)

    return call(
        kernel,
        (start, *steps, gain.reshape(1, -1)),
        [jax.ShapeDtypeStruct((ny, 2 * count, depth), BF16)],
        [pltpu.VMEM((2 * count, width), F32)],
    )[0]


def input_quarters(place, w_query, w_keyval, ny):
    width, cols = w_query.shape
    small = w_keyval.shape[1]
    depth = width // ny

    def kernel(place_ref, query_ref, keyval_ref, *out_refs):
        unit = (
            lax.broadcasted_iota(jnp.int32, (small, small), 0)
            == lax.broadcasted_iota(jnp.int32, (small, small), 1)
        ).astype(BF16)
        for k, out_ref in enumerate(out_refs):
            at = pl.multiple_of(lax.rem(place_ref[0] + k, ny) * depth, 16)
            out_ref[:depth, :] = query_ref[pl.ds(at, depth), :]
            turned = lax.dot_general(
                unit,
                keyval_ref[pl.ds(at, depth), :],
                (((1,), (1,)), ((), ())),
                preferred_element_type=F32,
            ).astype(BF16)
            rest = jnp.zeros((small, 2 * cols - depth), BF16)
            out_ref[depth : depth + small, :] = turned[:, :cols]
            out_ref[depth + small :, :] = jnp.concatenate([turned[:, cols:], rest], axis=1)

    shape = jax.ShapeDtypeStruct((depth + 2 * small, cols), BF16)
    return call(kernel, (place, w_query, w_keyval), [shape] * ny, [])


def output_quarters(place, w_out, ny):
    rows, width = w_out.shape
    depth = width // ny

    def kernel(place_ref, weights_ref, *refs):
        out_refs, quarters = refs[:-1], refs[-1]
        for k in range(ny):
            quarters[k] = weights_ref[:, k * depth : (k + 1) * depth]
        for k, out_ref in enumerate(out_refs):
            out_ref[...] = quarters[lax.rem(place_ref[0] + k, ny)]

    shape = jax.ShapeDtypeStruct((rows, depth), BF16)
    return call(kernel, (place, w_out), [shape] * ny, [pltpu.VMEM((ny, rows, depth), BF16)])


def shift(value, axis, by):
    count = lax.axis_size(axis)
    return lax.ppermute(value, axis, [(i, (i + by) % count) for i in range(count)])


def add(*terms):
    return sum(t.astype(F32) for t in terms).astype(BF16)


def ring_pieces(block, axis):
    half = lax.axis_size(axis) // 2
    up, down = [block], [block]
    for _ in range(half - 1):
        up.append(shift(up[-1], axis, 1))
        down.append(shift(down[-1], axis, -1))
    return down + [shift(up[-1], axis, 1)] + up[:0:-1]


def ring_sum(parts, axis):
    count = len(parts)
    half = count // 2
    up, down = shift(parts[half], axis, 1), None
    for k in range(half - 1, 0, -1):
        upper = add(parts[k], up)
        lower = parts[count - k] if down is None else add(parts[count - k], down)
        up, down = shift(upper, axis, 1), shift(lower, axis, -1)
    return add(parts[0], up, down)


def project(place, pieces, weights, small, nx, per):
    count, depth = pieces[0].shape
    ny, cols = len(weights), weights[0].shape[1]
    nz = len(pieces)
    part = nx * per
    total = ny * cols + 128
    shape = (nx, ny, nz * per, total)
    group = nz // 2

    def kernel(place_ref, *refs):
        row_refs, refs = refs[:nz], refs[nz:]
        weight_refs, refs = refs[:ny], refs[ny:]
        keep_ref, give_ref, rows, smalls, sums, kept, given = refs
        here, core = place_ref[0], place_ref[1]
        smalls[...] = jnp.zeros_like(smalls)
        for k in range(ny):
            to = pl.ds(pl.multiple_of(lax.rem(here + ny - k, ny) * small, 16), small)
            smalls[to, :cols] = weight_refs[k][depth : depth + small, :]
            smalls[to, cols:] = weight_refs[k][depth + small :, : depth - cols]
        for first in range(0, nz, group):
            for p in range(group):
                rows[p * count : (p + 1) * count, :] = row_refs[first + p][...]
            for k in range(ny):
                to = pl.multiple_of(lax.rem(here + ny - k, ny) * cols, 128)
                sums[:, pl.ds(to, cols)] = jnp.dot(
                    rows[...], weight_refs[k][:depth, :], preferred_element_type=F32
                )
            sums[:, ny * cols :] = lax.dot_general(
                rows[...], smalls[...], (((1,), (1,)), ((), ())), preferred_element_type=F32
            )
            for p in range(group):
                for y in range(ny):
                    at = p * count + y * 2 * part
                    mine = sums[pl.ds(pl.multiple_of(at + core * part, 8), part), :]
                    theirs = sums[pl.ds(pl.multiple_of(at + (1 - core) * part, 8), part), :]
                    slot = (first + p) * per
                    for x in range(nx):
                        kept[x, y, slot : slot + per, :] = mine[x * per : (x + 1) * per]
                        given[x, y, slot : slot + per, :] = theirs[x * per : (x + 1) * per]
        for x in range(nx):
            keep_ref[x] = kept[x].astype(BF16)
            give_ref[x] = given[x].astype(BF16)

    return call(
        kernel,
        (place, *pieces, *weights),
        [jax.ShapeDtypeStruct(shape, BF16)] * 2,
        [
            pltpu.VMEM((group * count, depth), BF16),
            pltpu.VMEM((128, depth), BF16),
            pltpu.VMEM((group * count, total), F32),
            pltpu.VMEM(shape, F32),
            pltpu.VMEM(shape, F32),
        ],
        flops=2 * count * nz * depth * total,
    )


def sum_terms(place, terms, per):
    def kernel(place_ref, terms_ref, out_ref):
        total = terms_ref[0].astype(F32)
        for i in range(1, terms_ref.shape[0]):
            total = total + terms_ref[i].astype(F32)
        out_ref[...] = pltpu.roll(total, place_ref[2] * per, 0).astype(BF16)

    return call(kernel, (place, terms), [jax.ShapeDtypeStruct(terms.shape[1:], BF16)], [])[0]


def project_out(place, own, other, weights, nx, nc, seqs):
    groups, count, width = own.shape
    ny = len(weights)
    rows, depth = weights[0].shape
    per = 2 * seqs
    nz = count // per
    block = ny * 2 * nx * nc * seqs

    def kernel(place_ref, own_ref, other_ref, *refs):
        weight_refs, refs = refs[:ny], refs[ny:]
        out_refs, (sums, slots) = refs[:nz], refs[nz:]
        here, core, depth_at = place_ref[0], place_ref[1], place_ref[2]
        for c in range(nc):
            for k in range(ny):
                at = pl.ds(pl.multiple_of(lax.rem(here + ny - k, ny) * rows, 128), rows)
                piece = jnp.where(core == c, own_ref[:, :, at], other_ref[:, :, at])
                term = jnp.dot(
                    piece.reshape(groups * count, rows),
                    weight_refs[k][...],
                    preferred_element_type=F32,
                )
                if k == 0:
                    sums[...] = term
                else:
                    sums[...] += term
            for x in range(nx):
                for y in range(ny):
                    for z in range(nz):
                        for t in range(2):
                            at = (x * ny + y) * count + z * per + t * seqs
                            to = ((y * 2 + t) * nx * nc + x * nc + c) * seqs
                            slots[z, to : to + seqs, :] = sums[at : at + seqs, :]
        for k in range(nz):
            out_refs[k][...] = slots[lax.rem(depth_at + k, nz)].astype(BF16)

    return call(
        kernel,
        (place, own, other, *weights),
        [jax.ShapeDtypeStruct((block, depth), BF16)] * nz,
        [pltpu.VMEM((groups * count, depth), F32), pltpu.VMEM((nz, block, depth), F32)],
        flops=2 * nc * groups * count * width * depth,
    )


def join_columns(place, blocks):
    count, rows, depth = blocks.shape

    def kernel(place_ref, blocks_ref, one_ref, two_ref, joined):
        for k in range(count):
            joined[:, k * depth : (k + 1) * depth] = blocks_ref[k].astype(F32)
        one_ref[...] = joined[: rows // 2, :].astype(BF16)
        two_ref[...] = joined[rows // 2 :, :].astype(BF16)

    shape = jax.ShapeDtypeStruct((rows // 2, count * depth), BF16)
    return call(kernel, (place, blocks), [shape] * 2, [pltpu.VMEM((rows, count * depth), F32)])


def shards(step_one, step_two, gain, w_query, w_keyval, w_out, kv_cache, lengths):
    ny, nz, nx, nc = (lax.axis_size(a) for a in ("y", "z", "x", "core"))
    narrow = nx * nc
    places = [lax.axis_index(a) for a in ("y", "core", "z", "x")]
    place = jnp.stack(places).astype(jnp.int32)
    width, query_cols = w_query.shape
    pair_cols = w_keyval.shape[1]
    size = kv_cache.shape[2] // 2
    seqs = kv_cache.shape[0]
    per = 2 * seqs
    depth = width // ny

    quarters = input_quarters(place, w_query, w_keyval, ny)
    weights = [quarters[0]] + [shift(quarters[k], "y", k) for k in range(1, ny)]

    quarters = output_quarters(place, w_out, ny)
    out_weights = [quarters[0]] + [shift(quarters[k], "y", k) for k in range(1, ny)]

    start = ((places[3] * nc + places[1]) * width).astype(jnp.int32).reshape(1)
    mine = normalize(start, (step_one, step_two), gain, nx, nc, ny, width)
    column = lax.all_to_all(mine, "y", split_axis=0, concat_axis=0, tiled=True)
    pieces = ring_pieces(column.reshape(ny * narrow * per, depth), "z")
    keep, give = project(place, pieces, weights, pair_cols, nx, per)
    cols = keep.shape[3]
    other = lax.ppermute(give, "core", [(0, 1), (1, 0)])
    pair = add(keep, other).reshape(nx * ny, nz * per, cols)
    pair, out_weights = lax.optimization_barrier((pair, out_weights))
    terms = lax.all_to_all(pair, ("x", "y"), split_axis=0, concat_axis=0, tiled=True)
    summed = sum_terms(place, terms, per)
    arrived = lax.all_to_all(
        summed.reshape(nz, per, cols), "z", split_axis=0, concat_axis=0, tiled=True
    )
    queries = arrived[:, :, : ny * query_cols].reshape(nz, per, ny, query_cols)
    queries = queries.transpose(1, 2, 0, 3).reshape(2, seqs, HEADS, size)
    keyval = arrived[:, :, ny * query_cols : ny * (query_cols + pair_cols)]
    keyval = keyval.reshape(nz, per, ny, pair_cols)
    keyval = keyval.transpose(1, 2, 0, 3).reshape(2, seqs, 2 * size)
    attended = attend(queries, keyval, kv_cache, lengths)
    leaving = attended.reshape(per, ny, nz, query_cols).transpose(2, 0, 1, 3)
    leaving = leaving.reshape(nz, per, ny * query_cols)
    returned = lax.all_to_all(leaving, "z", split_axis=0, concat_axis=0, tiled=True)
    returned = returned.reshape(nz * per, ny * query_cols)
    copies = jnp.broadcast_to(returned, (nx * ny, *returned.shape))
    gathered = lax.all_to_all(copies, ("x", "y"), split_axis=0, concat_axis=0, tiled=True)
    other = lax.ppermute(gathered, "core", [(0, 1), (1, 0)])
    parts = project_out(place, gathered, other, out_weights, nx, nc, seqs)
    out = ring_sum(parts, "z").reshape(ny, narrow * per, depth)
    out = lax.all_to_all(out, "y", split_axis=0, concat_axis=0, tiled=True)
    return tuple(join_columns(place, out))


def solution(mesh):
    fine = Mesh(mesh.devices.reshape(4, 8, 4, 2), ("y", "z", "x", "core"))
    wide, narrow = ("y", "z"), ("x", "core")
    return jax.shard_map(
        shards,
        mesh=fine,
        in_specs=(
            P(wide, None),
            P(wide, None),
            P(),
            P(narrow, wide),
            P(narrow, wide),
            P(wide, narrow),
            P(wide + narrow, None, None),
            P(wide + narrow),
        ),
        out_specs=(P(wide, narrow), P(wide, narrow)),
        check_vma=False,
    )
```

time: 240 us -> 211 us (0.88)
  blocking collectives: 25.3 us -> 50.4 us
  waiting for transfers between devices: 106 us -> 86.5 us
  local copies, waits for them, and re-layouts: 22.9 us -> 6.74 us
  between operations: 14.4 us -> 0.97 us
  other arithmetic: 14.7 us -> 2.57 us
  Pallas kernels: 6.25 us -> 14.8 us
  starting transfers between devices: 40.5 us -> 45.3 us
  matrix products: 7.68 us -> 3.47 us
    reduce_scatter x1 -> x0, waiting for transfers between devices: 54.4 us -> none  [shards(): out = lax.psum_scatter(out, 'z', scatter_dimension=0, tiled=True)]
    ppermute x13 -> x20, waiting for transfers between devices: 12.6 us -> 51 us  [shift(): lax.ppermute(value, axis, [(i, (i + by) % count) for i in range(count)])]
    all_to_all x2 -> x4, blocking collectives: 23 us -> 50.4 us  [the longest x1 21.4 us: shards(): lax.all_to_all(copies, ('x', 'y'), split_axis=0, concat_axis=0, tiled=True)]
    pallas_call x1 -> x7, Pallas kernels: 6.25 us -> 14.8 us  [call(): pl.pallas_call(kernel, in_specs=[SMEM] + [VMEM] * (len(inputs) - 1), out_...]
    ppermute x13 -> x20, starting transfers between devices: 22.9 us -> 31.4 us  [shift(): lax.ppermute(value, axis, [(i, (i + by) % count) for i in range(count)])]
    all_to_all x2 -> x1, starting transfers between devices: 11.5 us -> 6.41 us  [shards(): lax.all_to_all(summed.reshape(nz, per, cols), 'z', split_axis=0, concat_a...]
    squeeze x5 -> x0, local copies, waits for them, and re-layouts: 4.77 us -> none  [the longest x1 2.35 us: quarter(): lax.dynamic_index_in_dim(quarters, at, 0, keepdims=False)]
    concatenate x5 -> x0, other arithmetic: 4.33 us -> none  [the longest x4 3.55 us: quarter(): jnp.concatenate([lax.dynamic_index_in_dim(quarters, at, 0, keepdims=False...]
  transfers between devices with their start and end apart: 18 -> 24, of which waited for: 13 -> 16; matrix products, arithmetic and copies ran while one was open for 8% -> 2% of each run, Pallas kernels for 0% -> 1%
where the time goes in v2:
time: 211 us
  waiting for transfers between devices  86.5 us (41%)
  blocking collectives  50.4 us (24%)
  starting transfers between devices  45.3 us (21%)
  Pallas kernels  14.8 us (7%)
  local copies, waits for them, and re-layouts  6.74 us (3%)
  matrix products  3.47 us (2%)
  other arithmetic  2.57 us (1%)
    ppermute x20, waiting for transfers between devices, shift(): lax.ppermute(value, axis, [(i, (i + by) % count) for i in range(count)])  51 us
    ppermute x20, starting transfers between devices, shift(): lax.ppermute(value, axis, [(i, (i + by) % count) for i in range(count)])  31.4 us
    all_to_all x1, waiting for transfers between devices, shards(): lax.all_to_all(pair, ('x', 'y'), split_axis=0, concat_axis=0, tiled=True)  23.3 us
    all_to_all x1, blocking collectives, shards(): lax.all_to_all(copies, ('x', 'y'), split_axis=0, concat_axis=0, tiled=True)  21.4 us
    pallas_call x7, Pallas kernels, call(): pl.pallas_call(kernel, in_specs=[SMEM] + [VMEM] * (len(inputs) - 1), out_...  14.8 us
    all_to_all x1, blocking collectives, shards(): lax.all_to_all(leaving, 'z', split_axis=0, concat_axis=0, tiled=True)  11.1 us
    all_to_all x1, blocking collectives, shards(): column = lax.all_to_all(mine, 'y', split_axis=0, concat_axis=0, tiled=True)  9.4 us
    all_to_all x1, waiting for transfers between devices, shards(): lax.all_to_all(summed.reshape(nz, per, cols), 'z', split_axis=0, concat_a...  8.81 us
  transfers between devices with their start and end apart: 24, of which 16 were waited for; matrix products, arithmetic and copies ran while one was open for 2% of the time, Pallas kernels for 1%

profile of v2, /device:TPU:8, one launch (start us, length us, event | category | flops | bytes accessed | tf_op | source)
XLA Modules:
  0.0 210.7 jit_solution(51130085318190674)
XLA Ops:
  0.7 1.2 copy-done.2
  1.8 1.1 copy-done.3
  2.9 0.9 copy-done.4
  3.8 0.6 shard_map.95
  4.4 9.4 %all_to_all.30 = bf16[4,32,576]{2,1,0:T(8,128)(2,1)S(1)} all-to-all(bf16[4,32,576]{2,1,0:T(8,128)(2,1)S(1)} %shard_map.95), channel_id=1, replica_groups=mesh['y'=4,'z'=8,'x'=4,'core'=2] {'y'}, dimensions={0} | all-to-all | bytes 294912 | tf_op jit(solution)/shard_map/all_to_all | solution.py:303
  13.8 1.9 collective-permute-start.3
  15.7 1.2 copy.30.keyval_ref
  17.0 0.9 shard_map.96
  18.4 3.1 %collective-permute-start.8 = (bf16[608,384]{1,0:T(8,128)(2,1)S(1)}, bf16[608,384]{1,0:T(8,128)(2,1)S(1)}, u32[]{:S(2)}, u32[]{:S(2)}) collective-permute-start(bf16[608,384]{1,0:T(8,128)(2,1)S(1)} %get-tuple-element.27), channel_id=1, source_target_pairs={{0,128},{64,192},{128,0},{192,64},{1,129},{65,193},{129,1},{193,65... | collective-permute-start | bytes 1400840 | tf_op jit(solution)/shard_map/ppermute | solution.py:131
  22.0 3.9 %collective-permute-start = (bf16[128,576]{1,0:T(8,128)(2,1)S(1)}, bf16[128,576]{1,0:T(8,128)(2,1)S(1)}, u32[]{:S(2)}, u32[]{:S(2)}) collective-permute-start(bf16[128,576]{1,0:T(8,128)(2,1)S(1)} %bitcast.32), channel_id=1, source_target_pairs={{0,56},{8,0},{16,8},{24,16},{32,24},{40,32},{48,40},{56,48},{1,57}... | collective-permute-start | bytes 442376 | tf_op jit(solution)/shard_map/ppermute | solution.py:131
  26.0 2.8 %collective-permute-done.refs_1_ = bf16[128,576]{1,0:T(8,128)(2,1)S(1)} collective-permute-done((bf16[128,576]{1,0:T(8,128)(2,1)S(1)}, bf16[128,576]{1,0:T(8,128)(2,1)S(1)}, u32[]{:S(2)}, u32[]{:S(2)}) %collective-permute-start) | collective-permute-done | bytes 147488 | tf_op jit(solution)/shard_map/ppermute | solution.py:131
  28.8 3.7 %collective-permute-start.1 = (bf16[128,576]{1,0:T(8,128)(2,1)S(1)}, bf16[128,576]{1,0:T(8,128)(2,1)S(1)}, u32[]{:S(2)}, u32[]{:S(2)}) collective-permute-start(bf16[128,576]{1,0:T(8,128)(2,1)S(1)} %collective-permute-done.refs_1_), channel_id=1, source_target_pairs={{0,56},{8,0},{16,8},{24,16},{32,24},{40,32},{48,40},{56,48},{1,57}... | collective-permute-start | bytes 442376 | tf_op jit(solution)/shard_map/ppermute | solution.py:131
  32.5 3.5 %collective-permute-done.1.refs_2_ = bf16[128,576]{1,0:T(8,128)(2,1)S(1)} collective-permute-done((bf16[128,576]{1,0:T(8,128)(2,1)S(1)}, bf16[128,576]{1,0:T(8,128)(2,1)S(1)}, u32[]{:S(2)}, u32[]{:S(2)}) %collective-permute-start.1) | collective-permute-done | bytes 147488 | tf_op jit(solution)/shard_map/ppermute | solution.py:131
  36.0 3.7 %collective-permute-start.2 = (bf16[128,576]{1,0:T(8,128)(2,1)S(1)}, bf16[128,576]{1,0:T(8,128)(2,1)S(1)}, u32[]{:S(2)}, u32[]{:S(2)}) collective-permute-start(bf16[128,576]{1,0:T(8,128)(2,1)S(1)} %collective-permute-done.1.refs_2_), channel_id=1, source_target_pairs={{0,56},{8,0},{16,8},{24,16},{32,24},{40,32},{48,40},{56,48},{1,57}... | collective-permute-start | bytes 442376 | tf_op jit(solution)/shard_map/ppermute | solution.py:131
  40.0 0.7 collective-permute-done.9.refs_11_
  40.7 1.8 collective-permute-done.2.refs_3_
  42.5 4.0 %collective-permute-done.6.refs_4_ = bf16[128,576]{1,0:T(8,128)(2,1)S(1)} collective-permute-done((bf16[128,576]{1,0:T(8,128)(2,1)S(1)}, bf16[128,576]{1,0:T(8,128)(2,1)S(1)}, u32[]{:S(2)}, u32[]{:S(2)}) %collective-permute-start.6) | collective-permute-done | bytes 147488 | tf_op jit(solution)/shard_map/ppermute | solution.py:131
  46.5 5.4 %shard_map.97 = (bf16[4,4,32,1664]{3,2,1,0:T(8,128)(2,1)S(1)}, bf16[4,4,32,1664]{3,2,1,0:T(8,128)(2,1)S(1)}) custom-call(s32[4]{0:T(128)S(1)} %pad_add_fusion.place_ref, bf16[128,576]{1,0:T(8,128)(2,1)S(1)} %bitcast.33, bf16[128,576]{1,0:T(8,128)(2,1)S(1)} %collective-permute-done.refs_1_, bf16[128,576]{1,0:T(8,128)(2,1)S(1)} %collective-permute-done.1.refs_2_, ...), custom_call_target="tpu_custom_call" | custom-call | flops 1962934272 | bytes 6455296 | tf_op jit(solution)/shard_map/pallas_call | solution.py:47
  52.0 1.2 shard_map.98
  53.2 1.6 collective-permute-start.11
  54.9 0.9 collective-permute-start.12
  55.8 1.3 collective-permute-start.13
  57.1 1.6 add_convert_fusion
  58.7 8.6 %collective-permute-done.11.refs_1_ = bf16[384,576]{1,0:T(8,128)(2,1)S(1)} collective-permute-done((bf16[384,576]{1,0:T(8,128)(2,1)S(1)}, bf16[384,576]{1,0:T(8,128)(2,1)S(1)}, u32[]{:S(2)}, u32[]{:S(2)}) %collective-permute-start.11) | collective-permute-done | bytes 442400 | tf_op jit(solution)/shard_map/ppermute | solution.py:131
  67.3 3.2 %collective-permute-done.12.refs_2_ = bf16[384,576]{1,0:T(8,128)(2,1)S(1)} collective-permute-done((bf16[384,576]{1,0:T(8,128)(2,1)S(1)}, bf16[384,576]{1,0:T(8,128)(2,1)S(1)}, u32[]{:S(2)}, u32[]{:S(2)}) %collective-permute-start.12) | collective-permute-done | bytes 442400 | tf_op jit(solution)/shard_map/ppermute | solution.py:131
  70.5 8.9 %collective-permute-done.13.refs_3_ = bf16[384,576]{1,0:T(8,128)(2,1)S(1)} collective-permute-done((bf16[384,576]{1,0:T(8,128)(2,1)S(1)}, bf16[384,576]{1,0:T(8,128)(2,1)S(1)}, u32[]{:S(2)}, u32[]{:S(2)}) %collective-permute-start.13) | collective-permute-done | bytes 442400 | tf_op jit(solution)/shard_map/ppermute | solution.py:131
  79.4 0.8 copy-done.5
  80.2 7.4 %all-to-all-start.1 = ((bf16[16,32,1664]{2,1,0:T(8,128)(2,1)}), bf16[16,32,1664]{2,1,0:T(8,128)(2,1)S(1)}, u32[]{:S(2)}, u32[]{:S(2)}) async-start(bf16[16,32,1664]{2,1,0:T(8,128)(2,1)} %bitcast.35), calls=%async_computation.1 | async-start | bytes 3407872 | tf_op jit(solution)/shard_map/all_to_all | solution.py:310
  87.8 23.3 %all-to-all-done.1.terms_ref = bf16[16,32,1664]{2,1,0:T(8,128)(2,1)S(1)} async-done(((bf16[16,32,1664]{2,1,0:T(8,128)(2,1)}), bf16[16,32,1664]{2,1,0:T(8,128)(2,1)S(1)}, u32[]{:S(2)}, u32[]{:S(2)}) %all-to-all-start.1) | async-done | bytes 1703968 | tf_op jit(solution)/shard_map/all_to_all | solution.py:310
  111.1 0.8 shard_map.99
  111.9 0.7 reshape.101
  112.6 6.4 %all-to-all-start.2 = ((bf16[8,4,1664]{2,1,0:T(4,128)(2,1)}), bf16[8,4,1664]{2,1,0:T(4,128)(2,1)S(1)}, u32[]{:S(2)}, u32[]{:S(2)}) async-start(bf16[8,4,1664]{2,1,0:T(4,128)(2,1)} %reshape.101), calls=%async_computation.2 | async-start | bytes 212992 | tf_op jit(solution)/shard_map/all_to_all | solution.py:312
  119.0 8.8 %all-to-all-done.2 = bf16[8,4,1664]{2,1,0:T(4,128)(2,1)S(1)} async-done(((bf16[8,4,1664]{2,1,0:T(4,128)(2,1)}), bf16[8,4,1664]{2,1,0:T(4,128)(2,1)S(1)}, u32[]{:S(2)}, u32[]{:S(2)}) %all-to-all-start.2) | async-done | bytes 106528 | tf_op jit(solution)/shard_map/all_to_all | solution.py:312
  128.2 2.6 %fusion.26 = (f32[2,96]{1,0:T(2,128)S(1)}, f32[2,96,2048]{2,1,0:T(8,128)S(1)}) fusion(bf16[2,96,256]{2,1,0:T(8,128)(2,1)S(1)} %bitcast.37, bf16[2,2048,512]{2,1,0:T(8,128)(2,1)} %param.14, pred[2,2048]{1,0:T(4,128)(4,1)S(1)} %iota_compare_fusion), kind=kOutput, calls=%fused_computation.35 | convolution fusion | flops 202506048 | bytes 3773184 | tf_op jit(solution)/shard_map/srd,smd->srm/dot_general | solution.py:25
  132.5 11.1 %all_to_all.31 = bf16[8,4,1536]{2,1,0:T(4,128)(2,1)S(1)} all-to-all(bf16[8,4,1536]{2,1,0:T(4,128)(2,1)S(1)} %copy.38), channel_id=1, replica_groups=mesh['y'=4,'z'=8,'x'=4,'core'=2] {'z'}, dimensions={0} | all-to-all | bytes 196608 | tf_op jit(solution)/shard_map/all_to_all | solution.py:323
  143.8 21.4 %all_to_all.32.own_ref = bf16[16,32,1536]{2,1,0:T(8,128)(2,1)S(1)} all-to-all(bf16[16,32,1536]{2,1,0:T(8,128)(2,1)S(1)} %broadcast_in_dim.60), channel_id=1, replica_groups=mesh['y'=4,'z'=8,'x'=4,'core'=2] {'x','y'}, dimensions={0} | all-to-all | bytes 3145728 | tf_op jit(solution)/shard_map/all_to_all | solution.py:326
  165.2 3.4 %collective-permute-done.14.other_ref = bf16[16,32,1536]{2,1,0:T(8,128)(2,1)S(1)} collective-permute-done((bf16[16,32,1536]{2,1,0:T(8,128)(2,1)S(1)}, bf16[16,32,1536]{2,1,0:T(8,128)(2,1)S(1)}, u32[]{:S(2)}, u32[]{:S(2)}) %collective-permute-start.14) | collective-permute-done | bytes 1572896 | tf_op jit(solution)/shard_map/ppermute | solution.py:327
  168.6 4.6 %shard_map.100 = (bf16[128,576]{1,0:T(8,128)(2,1)S(1)}, bf16[128,576]{1,0:T(8,128)(2,1)S(1)}, bf16[128,576]{1,0:T(8,128)(2,1)S(1)}, bf16[128,576]{1,0:T(8,128)(2...) custom-call(s32[4]{0:T(128)S(1)} %pad_add_fusion.place_ref, ...), custom_call_target="tpu_custom_call" | custom-call | flops 1811939328 | bytes 6094848 | tf_op jit(solution)/shard_map/pallas_call | solution.py:47
  173.3 0.6 collective-permute-start.15
  173.9 2.7 %collective-permute-start.19 = (bf16[128,576]{1,0:T(8,128)(2,1)S(1)}, bf16[128,576]{1,0:T(8,128)(2,1)S(1)}, u32[]{:S(2)}, u32[]{:S(2)}) collective-permute-start(bf16[128,576]{1,0:T(8,128)(2,1)S(1)} %get-tuple-element.47), channel_id=1, source_target_pairs={{0,56},{8,0},{16,8},{24,16},{32,24},{40,32},{48,40},{56,48},{1,57}... | collective-permute-start | bytes 442376 | tf_op jit(solution)/shard_map/ppermute | solution.py:131
  176.6 4.2 %collective-permute-done.15 = bf16[128,576]{1,0:T(8,128)(2,1)S(1)} collective-permute-done((bf16[128,576]{1,0:T(8,128)(2,1)S(1)}, bf16[128,576]{1,0:T(8,128)(2,1)S(1)}, u32[]{:S(2)}, u32[]{:S(2)}) %collective-permute-start.15) | collective-permute-done | bytes 147488 | tf_op jit(solution)/shard_map/ppermute | solution.py:131
  181.0 3.3 %collective-permute-start.20 = (bf16[128,576]{1,0:T(8,128)(2,1)S(1)}, bf16[128,576]{1,0:T(8,128)(2,1)S(1)}, u32[]{:S(2)}, u32[]{:S(2)}) collective-permute-start(bf16[128,576]{1,0:T(8,128)(2,1)S(1)} %add_convert_fusion.3), channel_id=1, source_target_pairs={{0,56},{8,0},{16,8},{24,16},{32,24},{40,32},{48,40},{56,48},{1,57}... | collective-permute-start | bytes 442376 | tf_op jit(solution)/shard_map/ppermute | solution.py:131
  184.3 3.3 %collective-permute-done.16 = bf16[128,576]{1,0:T(8,128)(2,1)S(1)} collective-permute-done((bf16[128,576]{1,0:T(8,128)(2,1)S(1)}, bf16[128,576]{1,0:T(8,128)(2,1)S(1)}, u32[]{:S(2)}, u32[]{:S(2)}) %collective-permute-start.16) | collective-permute-done | bytes 147488 | tf_op jit(solution)/shard_map/ppermute | solution.py:131
  187.7 3.3 %collective-permute-start.21 = (bf16[128,576]{1,0:T(8,128)(2,1)S(1)}, bf16[128,576]{1,0:T(8,128)(2,1)S(1)}, u32[]{:S(2)}, u32[]{:S(2)}) collective-permute-start(bf16[128,576]{1,0:T(8,128)(2,1)S(1)} %add_convert_fusion.2), channel_id=1, source_target_pairs={{0,56},{8,0},{16,8},{24,16},{32,24},{40,32},{48,40},{56,48},{1,57}... | collective-permute-start | bytes 442376 | tf_op jit(solution)/shard_map/ppermute | solution.py:131
  191.0 3.2 %collective-permute-done.17 = bf16[128,576]{1,0:T(8,128)(2,1)S(1)} collective-permute-done((bf16[128,576]{1,0:T(8,128)(2,1)S(1)}, bf16[128,576]{1,0:T(8,128)(2,1)S(1)}, u32[]{:S(2)}, u32[]{:S(2)}) %collective-permute-start.17) | collective-permute-done | bytes 147488 | tf_op jit(solution)/shard_map/ppermute | solution.py:131
  194.3 6.5 %collective-permute-done.18 = bf16[128,576]{1,0:T(8,128)(2,1)S(1)} collective-permute-done((bf16[128,576]{1,0:T(8,128)(2,1)S(1)}, bf16[128,576]{1,0:T(8,128)(2,1)S(1)}, u32[]{:S(2)}, u32[]{:S(2)}) %collective-permute-start.18) | collective-permute-done | bytes 147488 | tf_op jit(solution)/shard_map/ppermute | solution.py:131
  200.9 8.5 %all_to_all.33.blocks_ref = bf16[4,32,576]{2,1,0:T(8,128)(2,1)S(1)} all-to-all(bf16[4,32,576]{2,1,0:T(8,128)(2,1)S(1)} %bitcast.36), channel_id=1, replica_groups=mesh['y'=4,'z'=8,'x'=4,'core'=2] {'y'}, dimensions={0} | all-to-all | bytes 294912 | tf_op jit(solution)/shard_map/all_to_all | solution.py:330
  209.4 1.3 shard_map.101
  (68 shorter events, 4.6 us)
Async XLA Ops:
  0.6 16.4 %copy-start = (bf16[2304,384]{1,0:T(8,128)(2,1)S(1)}, bf16[2304,384]{1,0:T(8,128)(2,1)}, u32[]{:S(2)}) copy-start(bf16[2304,384]{1,0:T(8,128)(2,1)} %query_ref.1) | copy-start | bytes 5308420
  0.6 1.2 copy-start.2
  1.8 1.1 copy-start.3
  2.9 0.9 copy-start.4
  13.8 12.2 %collective-permute-start.3 = (bf16[128,576]{1,0:T(8,128)(2,1)S(1)}, bf16[128,576]{1,0:T(8,128)(2,1)S(1)}, u32[]{:S(2)}, u32[]{:S(2)}) collective-permute-start(bf16[128,576]{1,0:T(8,128)(2,1)S(1)} %bitcast.31), channel_id=1, source_target_pairs={{0,8},{8,16},{16,24},{24,32},{32,40},{40,48},{48,56},{56,0},{1,9},... | collective-permute-start | bytes 442376 | tf_op jit(solution)/shard_map/ppermute | solution.py:131
  17.9 22.1 %collective-permute-start.7 = (bf16[608,384]{1,0:T(8,128)(2,1)S(1)}, bf16[608,384]{1,0:T(8,128)(2,1)S(1)}, u32[]{:S(2)}, u32[]{:S(2)}) collective-permute-start(bf16[608,384]{1,0:T(8,128)(2,1)S(1)} %get-tuple-element.26), channel_id=1, source_target_pairs={{0,64},{64,128},{128,192},{192,0},{1,65},{65,129},{129,193},{193,1... | collective-permute-start | bytes 1400840 | tf_op jit(solution)/shard_map/ppermute | solution.py:131
  18.4 21.6 %collective-permute-start.8 = (bf16[608,384]{1,0:T(8,128)(2,1)S(1)}, bf16[608,384]{1,0:T(8,128)(2,1)S(1)}, u32[]{:S(2)}, u32[]{:S(2)}) collective-permute-start(bf16[608,384]{1,0:T(8,128)(2,1)S(1)} %get-tuple-element.27), channel_id=1, source_target_pairs={{0,128},{64,192},{128,0},{192,64},{1,129},{65,193},{129,1},{193,65... | collective-permute-start | bytes 1400840 | tf_op jit(solution)/shard_map/ppermute | solution.py:131
  21.5 19.2 %collective-permute-start.9 = (bf16[608,384]{1,0:T(8,128)(2,1)S(1)}, bf16[608,384]{1,0:T(8,128)(2,1)S(1)}, u32[]{:S(2)}, u32[]{:S(2)}) collective-permute-start(bf16[608,384]{1,0:T(8,128)(2,1)S(1)} %get-tuple-element.28), channel_id=1, source_target_pairs={{0,192},{64,0},{128,64},{192,128},{1,193},{65,1},{129,65},{193,129... | collective-permute-start | bytes 1400840 | tf_op jit(solution)/shard_map/ppermute | solution.py:131
  22.0 6.8 %collective-permute-start = (bf16[128,576]{1,0:T(8,128)(2,1)S(1)}, bf16[128,576]{1,0:T(8,128)(2,1)S(1)}, u32[]{:S(2)}, u32[]{:S(2)}) collective-permute-start(bf16[128,576]{1,0:T(8,128)(2,1)S(1)} %bitcast.32), channel_id=1, source_target_pairs={{0,56},{8,0},{16,8},{24,16},{32,24},{40,32},{48,40},{56,48},{1,57}... | collective-permute-start | bytes 442376 | tf_op jit(solution)/shard_map/ppermute | solution.py:131
  26.0 6.5 %collective-permute-start.4 = (bf16[128,576]{1,0:T(8,128)(2,1)S(1)}, bf16[128,576]{1,0:T(8,128)(2,1)S(1)}, u32[]{:S(2)}, u32[]{:S(2)}) collective-permute-start(bf16[128,576]{1,0:T(8,128)(2,1)S(1)} %collective-permute-done.3.refs_7_), channel_id=1, source_target_pairs={{0,8},{8,16},{16,24},{24,32},{32,40},{40,48},{48,56},{56,0},{1,9},... | collective-permute-start | bytes 442376 | tf_op jit(solution)/shard_map/ppermute | solution.py:131
  28.8 7.2 %collective-permute-start.1 = (bf16[128,576]{1,0:T(8,128)(2,1)S(1)}, bf16[128,576]{1,0:T(8,128)(2,1)S(1)}, u32[]{:S(2)}, u32[]{:S(2)}) collective-permute-start(bf16[128,576]{1,0:T(8,128)(2,1)S(1)} %collective-permute-done.refs_1_), channel_id=1, source_target_pairs={{0,56},{8,0},{16,8},{24,16},{32,24},{40,32},{48,40},{56,48},{1,57}... | collective-permute-start | bytes 442376 | tf_op jit(solution)/shard_map/ppermute | solution.py:131
  32.5 7.5 %collective-permute-start.5 = (bf16[128,576]{1,0:T(8,128)(2,1)S(1)}, bf16[128,576]{1,0:T(8,128)(2,1)S(1)}, u32[]{:S(2)}, u32[]{:S(2)}) collective-permute-start(bf16[128,576]{1,0:T(8,128)(2,1)S(1)} %collective-permute-done.4.refs_6_), channel_id=1, source_target_pairs={{0,8},{8,16},{16,24},{24,32},{32,40},{40,48},{48,56},{56,0},{1,9},... | collective-permute-start | bytes 442376 | tf_op jit(solution)/shard_map/ppermute | solution.py:131
  36.0 6.5 %collective-permute-start.2 = (bf16[128,576]{1,0:T(8,128)(2,1)S(1)}, bf16[128,576]{1,0:T(8,128)(2,1)S(1)}, u32[]{:S(2)}, u32[]{:S(2)}) collective-permute-start(bf16[128,576]{1,0:T(8,128)(2,1)S(1)} %collective-permute-done.1.refs_2_), channel_id=1, source_target_pairs={{0,56},{8,0},{16,8},{24,16},{32,24},{40,32},{48,40},{56,48},{1,57}... | collective-permute-start | bytes 442376 | tf_op jit(solution)/shard_map/ppermute | solution.py:131
  40.0 6.5 %collective-permute-start.6 = (bf16[128,576]{1,0:T(8,128)(2,1)S(1)}, bf16[128,576]{1,0:T(8,128)(2,1)S(1)}, u32[]{:S(2)}, u32[]{:S(2)}) collective-permute-start(bf16[128,576]{1,0:T(8,128)(2,1)S(1)} %collective-permute-done.5.refs_5_), channel_id=1, source_target_pairs={{0,8},{8,16},{16,24},{24,32},{32,40},{40,48},{48,56},{56,0},{1,9},... | collective-permute-start | bytes 442376 | tf_op jit(solution)/shard_map/ppermute | solution.py:131
  46.5 5.5 %copy-start.1 = (bf16[384,2304]{1,0:T(8,128)(2,1)S(1)}, bf16[384,2304]{1,0:T(8,128)(2,1)}, u32[]{:S(2)}) copy-start(bf16[384,2304]{1,0:T(8,128)(2,1)} %weights_ref.1) | copy-start | bytes 5308420
  51.9 5.2 %collective-permute-start.10 = (bf16[4,4,32,1664]{3,2,1,0:T(8,128)(2,1)S(1)}, bf16[4,4,32,1664]{3,2,1,0:T(8,128)(2,1)S(1)}, u32[]{:S(2)}, u32[]{:S(2)}) collective-permute-start(bf16[4,4,32,1664]{3,2,1,0:T(8,128)(2,1)S(1)} %get-tuple-element.30), channel_id=1, source_target_pairs={{0,1},{1,0},{2,3},{3,2},{4,5},{5,4},{6,7},{7,6},{8,9},{9,8},{10,11... | collective-permute-start | bytes 5111816 | tf_op jit(solution)/shard_map/ppermute | solution.py:307
  53.2 14.1 %collective-permute-start.11 = (bf16[384,576]{1,0:T(8,128)(2,1)S(1)}, bf16[384,576]{1,0:T(8,128)(2,1)S(1)}, u32[]{:S(2)}, u32[]{:S(2)}) collective-permute-start(bf16[384,576]{1,0:T(8,128)(2,1)S(1)} %get-tuple-element.32), channel_id=1, source_target_pairs={{0,64},{64,128},{128,192},{192,0},{1,65},{65,129},{129,193},{193,1... | collective-permute-start | bytes 1327112 | tf_op jit(solution)/shard_map/ppermute | solution.py:131
  54.9 15.6 %collective-permute-start.12 = (bf16[384,576]{1,0:T(8,128)(2,1)S(1)}, bf16[384,576]{1,0:T(8,128)(2,1)S(1)}, u32[]{:S(2)}, u32[]{:S(2)}) collective-permute-start(bf16[384,576]{1,0:T(8,128)(2,1)S(1)} %get-tuple-element.33), channel_id=1, source_target_pairs={{0,128},{64,192},{128,0},{192,64},{1,129},{65,193},{129,1},{193,65... | collective-permute-start | bytes 1327112 | tf_op jit(solution)/shard_map/ppermute | solution.py:131
  55.8 23.6 %collective-permute-start.13 = (bf16[384,576]{1,0:T(8,128)(2,1)S(1)}, bf16[384,576]{1,0:T(8,128)(2,1)S(1)}, u32[]{:S(2)}, u32[]{:S(2)}) collective-permute-start(bf16[384,576]{1,0:T(8,128)(2,1)S(1)} %get-tuple-element.34), channel_id=1, source_target_pairs={{0,192},{64,0},{128,64},{192,128},{1,193},{65,1},{129,65},{193,129... | collective-permute-start | bytes 1327112 | tf_op jit(solution)/shard_map/ppermute | solution.py:131
  79.4 0.8 copy-start.5
  80.2 7.5 %copy-start.7 = (s32[2]{0:T(128)S(1)}, s32[2]{0:T(128)}, u32[]{:S(2)}) copy-start(s32[2]{0:T(128)} %param.15) | copy-start | bytes 28
  80.2 30.9 %all-to-all-start.1 = ((bf16[16,32,1664]{2,1,0:T(8,128)(2,1)}), bf16[16,32,1664]{2,1,0:T(8,128)(2,1)S(1)}, u32[]{:S(2)}, u32[]{:S(2)}) async-start(bf16[16,32,1664]{2,1,0:T(8,128)(2,1)} %bitcast.35), calls=%async_computation.1 | async-start | bytes 3407872 | tf_op jit(solution)/shard_map/all_to_all | solution.py:310
  112.6 15.2 %all-to-all-start.2 = ((bf16[8,4,1664]{2,1,0:T(4,128)(2,1)}), bf16[8,4,1664]{2,1,0:T(4,128)(2,1)S(1)}, u32[]{:S(2)}, u32[]{:S(2)}) async-start(bf16[8,4,1664]{2,1,0:T(4,128)(2,1)} %reshape.101), calls=%async_computation.2 | async-start | bytes 212992 | tf_op jit(solution)/shard_map/all_to_all | solution.py:312
  128.2 3.5 %copy-start.8 = (bf16[2,2048,512]{2,1,0:T(8,128)(2,1)S(1)}, bf16[2,2048,512]{2,1,0:T(8,128)(2,1)}, u32[]{:S(2)}) copy-start(bf16[2,2048,512]{2,1,0:T(8,128)(2,1)} %param.14) | copy-start | bytes 12582916
  143.8 24.8 %copy-start.6 = (bf16[384,576]{1,0:T(8,128)(2,1)S(1)}, bf16[384,576]{1,0:T(8,128)(2,1)}, u32[]{:S(2)}) copy-start(bf16[384,576]{1,0:T(8,128)(2,1)} %copy-done.5) | copy-start | bytes 1327108
  165.2 3.4 %collective-permute-start.14 = (bf16[16,32,1536]{2,1,0:T(8,128)(2,1)S(1)}, bf16[16,32,1536]{2,1,0:T(8,128)(2,1)S(1)}, u32[]{:S(2)}, u32[]{:S(2)}) collective-permute-start(bf16[16,32,1536]{2,1,0:T(8,128)(2,1)S(1)} %all_to_all.32.own_ref), channel_id=1, source_target_pairs={{0,1},{1,0},{2,3},{3,2},{4,5},{5,4},{6,7},{7,6},{8,9},{9,8},{10,11... | collective-permute-start | bytes 4718600 | tf_op jit(solution)/shard_map/ppermute | solution.py:327
  173.3 7.5 %collective-permute-start.15 = (bf16[128,576]{1,0:T(8,128)(2,1)S(1)}, bf16[128,576]{1,0:T(8,128)(2,1)S(1)}, u32[]{:S(2)}, u32[]{:S(2)}) collective-permute-start(bf16[128,576]{1,0:T(8,128)(2,1)S(1)} %get-tuple-element.44), channel_id=1, source_target_pairs={{0,8},{8,16},{16,24},{24,32},{32,40},{40,48},{48,56},{56,0},{1,9},... | collective-permute-start | bytes 442376 | tf_op jit(solution)/shard_map/ppermute | solution.py:131
  173.9 7.0 %collective-permute-start.19 = (bf16[128,576]{1,0:T(8,128)(2,1)S(1)}, bf16[128,576]{1,0:T(8,128)(2,1)S(1)}, u32[]{:S(2)}, u32[]{:S(2)}) collective-permute-start(bf16[128,576]{1,0:T(8,128)(2,1)S(1)} %get-tuple-element.47), channel_id=1, source_target_pairs={{0,56},{8,0},{16,8},{24,16},{32,24},{40,32},{48,40},{56,48},{1,57}... | collective-permute-start | bytes 442376 | tf_op jit(solution)/shard_map/ppermute | solution.py:131
  180.8 6.7 %collective-permute-start.16 = (bf16[128,576]{1,0:T(8,128)(2,1)S(1)}, bf16[128,576]{1,0:T(8,128)(2,1)S(1)}, u32[]{:S(2)}, u32[]{:S(2)}) collective-permute-start(bf16[128,576]{1,0:T(8,128)(2,1)S(1)} %add_convert_fusion.6), channel_id=1, source_target_pairs={{0,8},{8,16},{16,24},{24,32},{32,40},{40,48},{48,56},{56,0},{1,9},... | collective-permute-start | bytes 442376 | tf_op jit(solution)/shard_map/ppermute | solution.py:131
  181.0 6.7 %collective-permute-start.20 = (bf16[128,576]{1,0:T(8,128)(2,1)S(1)}, bf16[128,576]{1,0:T(8,128)(2,1)S(1)}, u32[]{:S(2)}, u32[]{:S(2)}) collective-permute-start(bf16[128,576]{1,0:T(8,128)(2,1)S(1)} %add_convert_fusion.3), channel_id=1, source_target_pairs={{0,56},{8,0},{16,8},{24,16},{32,24},{40,32},{48,40},{56,48},{1,57}... | collective-permute-start | bytes 442376 | tf_op jit(solution)/shard_map/ppermute | solution.py:131
  187.6 6.6 %collective-permute-start.17 = (bf16[128,576]{1,0:T(8,128)(2,1)S(1)}, bf16[128,576]{1,0:T(8,128)(2,1)S(1)}, u32[]{:S(2)}, u32[]{:S(2)}) collective-permute-start(bf16[128,576]{1,0:T(8,128)(2,1)S(1)} %add_convert_fusion.5), channel_id=1, source_target_pairs={{0,8},{8,16},{16,24},{24,32},{32,40},{40,48},{48,56},{56,0},{1,9},... | collective-permute-start | bytes 442376 | tf_op jit(solution)/shard_map/ppermute | solution.py:131
  187.7 6.6 %collective-permute-start.21 = (bf16[128,576]{1,0:T(8,128)(2,1)S(1)}, bf16[128,576]{1,0:T(8,128)(2,1)S(1)}, u32[]{:S(2)}, u32[]{:S(2)}) collective-permute-start(bf16[128,576]{1,0:T(8,128)(2,1)S(1)} %add_convert_fusion.2), channel_id=1, source_target_pairs={{0,56},{8,0},{16,8},{24,16},{32,24},{40,32},{48,40},{56,48},{1,57}... | collective-permute-start | bytes 442376 | tf_op jit(solution)/shard_map/ppermute | solution.py:131
  194.2 6.6 %collective-permute-start.18 = (bf16[128,576]{1,0:T(8,128)(2,1)S(1)}, bf16[128,576]{1,0:T(8,128)(2,1)S(1)}, u32[]{:S(2)}, u32[]{:S(2)}) collective-permute-start(bf16[128,576]{1,0:T(8,128)(2,1)S(1)} %add_convert_fusion.4), channel_id=1, source_target_pairs={{0,8},{8,16},{16,24},{24,32},{32,40},{40,48},{48,56},{56,0},{1,9},... | collective-permute-start | bytes 442376 | tf_op jit(solution)/shard_map/ppermute | solution.py:131

commit v3 on v2

--- a/solution.py
+++ b/solution.py
@@ -81,6 +81,7 @@
         (start, *steps, gain.reshape(1, -1)),
         [jax.ShapeDtypeStruct((ny, 2 * count, depth), BF16)],
         [pltpu.VMEM((2 * count, width), F32)],
+        mib=58,
     )[0]
 
 
@@ -295,9 +296,6 @@
     quarters = input_quarters(place, w_query, w_keyval, ny)
     weights = [quarters[0]] + [shift(quarters[k], "y", k) for k in range(1, ny)]
 
-    quarters = output_quarters(place, w_out, ny)
-    out_weights = [quarters[0]] + [shift(quarters[k], "y", k) for k in range(1, ny)]
-
     start = ((places[3] * nc + places[1]) * width).astype(jnp.int32).reshape(1)
     mine = normalize(start, (step_one, step_two), gain, nx, nc, ny, width)
     column = lax.all_to_all(mine, "y", split_axis=0, concat_axis=0, tiled=True)
@@ -306,11 +304,15 @@
     cols = keep.shape[3]
     other = lax.ppermute(give, "core", [(0, 1), (1, 0)])
     pair = add(keep, other).reshape(nx * ny, nz * per, cols)
-    pair, out_weights = lax.optimization_barrier((pair, out_weights))
     terms = lax.all_to_all(pair, ("x", "y"), split_axis=0, concat_axis=0, tiled=True)
     summed = sum_terms(place, terms, per)
+    summed, *quarters = lax.optimization_barrier((summed, *output_quarters(place, w_out, ny)))
+    out_weights = [quarters[0]] + [shift(quarters[k], "y", k) for k in range(1, ny)]
     arrived = lax.all_to_all(
         summed.reshape(nz, per, cols), "z", split_axis=0, concat_axis=0, tiled=True
+    )
+    arrived, out_weights[1], out_weights[-1] = lax.optimization_barrier(
+        (arrived, out_weights[1], out_weights[-1])
     )
     queries = arrived[:, :, : ny * query_cols].reshape(nz, per, ny, query_cols)
     queries = queries.transpose(1, 2, 0, 3).reshape(2, seqs, HEADS, size)
@@ -322,6 +324,7 @@
     leaving = leaving.reshape(nz, per, ny * query_cols)
     returned = lax.all_to_all(leaving, "z", split_axis=0, concat_axis=0, tiled=True)
     returned = returned.reshape(nz * per, ny * query_cols)
+    returned, out_weights = lax.optimization_barrier((returned, out_weights))
     copies = jnp.broadcast_to(returned, (nx * ny, *returned.shape))
     gathered = lax.all_to_all(copies, ("x", "y"), split_axis=0, concat_axis=0, tiled=True)
     other = lax.ppermute(gathered, "core", [(0, 1), (1, 0)])

time: 211 us -> 198 us (0.938)
  waiting for transfers between devices: 86.5 us -> 65.7 us
  blocking collectives: 50.4 us -> 58.6 us
  Pallas kernels: 14.8 us -> 18.1 us
  local copies, waits for them, and re-layouts: 6.74 us -> 3.52 us
    ppermute x20, waiting for transfers between devices: 51 us -> 30.7 us  [shift(): lax.ppermute(value, axis, [(i, (i + by) % count) for i in range(count)])]
    all_to_all x1, blocking collectives: 21.4 us -> 28.8 us  [shards(): lax.all_to_all(copies, ('x', 'y'), split_axis=0, concat_axis=0, tiled=True)]
    ppermute x1, waiting for transfers between devices: 0.01 us -> 3.58 us  [shards(): other = lax.ppermute(give, 'core', [(0, 1), (1, 0)])]
    pallas_call x7, Pallas kernels: 14.8 us -> 18.1 us  [call(): pl.pallas_call(kernel, in_specs=[SMEM] + [VMEM] * (len(inputs) - 1), out_...]
    unnamed x19, local copies, waits for them, and re-layouts: 5.14 us -> 1.92 us
    all_to_all x1, waiting for transfers between devices: 23.3 us -> 20.8 us  [shards(): lax.all_to_all(pair, ('x', 'y'), split_axis=0, concat_axis=0, tiled=True)]
  transfers between devices with their start and end apart: 24 -> 24, of which waited for: 16 -> 15; matrix products, arithmetic and copies ran while one was open for 2% -> 3% of each run, Pallas kernels for 1% -> 2%
where the time goes in v3:
time: 198 us
  waiting for transfers between devices  65.7 us (33%)
  blocking collectives  58.6 us (30%)
  starting transfers between devices  44.5 us (22%)
  Pallas kernels  18.1 us (9%)
  local copies, waits for them, and re-layouts  3.52 us (2%)
  matrix products  3.48 us (2%)
  other arithmetic  2.56 us (1%)
    ppermute x20, waiting for transfers between devices, shift(): lax.ppermute(value, axis, [(i, (i + by) % count) for i in range(count)])  30.7 us
    ppermute x20, starting transfers between devices, shift(): lax.ppermute(value, axis, [(i, (i + by) % count) for i in range(count)])  30.7 us
    all_to_all x1, blocking collectives, shards(): lax.all_to_all(copies, ('x', 'y'), split_axis=0, concat_axis=0, tiled=True)  28.8 us
    all_to_all x1, waiting for transfers between devices, shards(): lax.all_to_all(pair, ('x', 'y'), split_axis=0, concat_axis=0, tiled=True)  20.8 us
    pallas_call x7, Pallas kernels, call(): pl.pallas_call(kernel, in_specs=[SMEM] + [VMEM] * (len(inputs) - 1), out_...  18.1 us
    all_to_all x1, blocking collectives, shards(): lax.all_to_all(leaving, 'z', split_axis=0, concat_axis=0, tiled=True)  11.1 us
    all_to_all x1, blocking collectives, shards(): column = lax.all_to_all(mine, 'y', split_axis=0, concat_axis=0, tiled=True)  10.2 us
    all_to_all x1, blocking collectives, shards(): out = lax.all_to_all(out, 'y', split_axis=0, concat_axis=0, tiled=True)  8.5 us
  transfers between devices with their start and end apart: 24, of which 15 were waited for; matrix products, arithmetic and copies ran while one was open for 3% of the time, Pallas kernels for 2%

profile of v3, /device:TPU:8, one launch (start us, length us, event | category | flops | bytes accessed | tf_op | source)
XLA Modules:
  0.0 197.6 jit_solution(12633311079037807608)
XLA Ops:
  0.7 2.6 %shard_map.95 = bf16[4,32,576]{2,1,0:T(8,128)(2,1)} custom-call(s32[1]{0:T(128)} %bitcast.4.start_ref, bf16[16,18432]{1,0:T(8,128)(2,1)} %one_ref.1, bf16[16,18432]{1,0:T(8,128)(2,1)} %two_ref.1, f32[1,18432]{1,0:T(1,128)} %bitcast.43), custom_call_target="tpu_custom_call" | custom-call | bytes 1400832 | tf_op jit(solution)/shard_map/pallas_call | solution.py:47
  3.3 10.2 %all_to_all.30 = bf16[4,32,576]{2,1,0:T(8,128)(2,1)S(1)} all-to-all(bf16[4,32,576]{2,1,0:T(8,128)(2,1)} %shard_map.95), channel_id=1, replica_groups=mesh['y'=4,'z'=8,'x'=4,'core'=2] {'y'}, dimensions={0} | all-to-all | bytes 294912 | tf_op jit(solution)/shard_map/all_to_all | solution.py:301
  13.5 1.3 collective-permute-start.3
  14.8 0.3 copy.30.keyval_ref
  15.2 0.9 shard_map.96
  16.1 0.6 collective-permute-start.7
  16.6 3.1 %collective-permute-start.8 = (bf16[608,384]{1,0:T(8,128)(2,1)S(1)}, bf16[608,384]{1,0:T(8,128)(2,1)S(1)}, u32[]{:S(2)}, u32[]{:S(2)}) collective-permute-start(bf16[608,384]{1,0:T(8,128)(2,1)S(1)} %get-tuple-element.35), channel_id=1, source_target_pairs={{0,128},{64,192},{128,0},{192,64},{1,129},{65,193},{129,1},{193,65... | collective-permute-start | bytes 1400840 | tf_op jit(solution)/shard_map/ppermute | solution.py:132
  19.7 0.6 collective-permute-start.9
  20.2 3.9 %collective-permute-start = (bf16[128,576]{1,0:T(8,128)(2,1)S(1)}, bf16[128,576]{1,0:T(8,128)(2,1)S(1)}, u32[]{:S(2)}, u32[]{:S(2)}) collective-permute-start(bf16[128,576]{1,0:T(8,128)(2,1)S(1)} %bitcast.32), channel_id=1, source_target_pairs={{0,56},{8,0},{16,8},{24,16},{32,24},{40,32},{48,40},{56,48},{1,57}... | collective-permute-start | bytes 442376 | tf_op jit(solution)/shard_map/ppermute | solution.py:132
  24.2 2.8 %collective-permute-done.refs_1_ = bf16[128,576]{1,0:T(8,128)(2,1)S(1)} collective-permute-done((bf16[128,576]{1,0:T(8,128)(2,1)S(1)}, bf16[128,576]{1,0:T(8,128)(2,1)S(1)}, u32[]{:S(2)}, u32[]{:S(2)}) %collective-permute-start) | collective-permute-done | bytes 147488 | tf_op jit(solution)/shard_map/ppermute | solution.py:132
  27.0 3.7 %collective-permute-start.1 = (bf16[128,576]{1,0:T(8,128)(2,1)S(1)}, bf16[128,576]{1,0:T(8,128)(2,1)S(1)}, u32[]{:S(2)}, u32[]{:S(2)}) collective-permute-start(bf16[128,576]{1,0:T(8,128)(2,1)S(1)} %collective-permute-done.refs_1_), channel_id=1, source_target_pairs={{0,56},{8,0},{16,8},{24,16},{32,24},{40,32},{48,40},{56,48},{1,57}... | collective-permute-start | bytes 442376 | tf_op jit(solution)/shard_map/ppermute | solution.py:132
  30.9 3.3 %collective-permute-done.1.refs_2_ = bf16[128,576]{1,0:T(8,128)(2,1)S(1)} collective-permute-done((bf16[128,576]{1,0:T(8,128)(2,1)S(1)}, bf16[128,576]{1,0:T(8,128)(2,1)S(1)}, u32[]{:S(2)}, u32[]{:S(2)}) %collective-permute-start.1) | collective-permute-done | bytes 147488 | tf_op jit(solution)/shard_map/ppermute | solution.py:132
  34.2 3.7 %collective-permute-start.2 = (bf16[128,576]{1,0:T(8,128)(2,1)S(1)}, bf16[128,576]{1,0:T(8,128)(2,1)S(1)}, u32[]{:S(2)}, u32[]{:S(2)}) collective-permute-start(bf16[128,576]{1,0:T(8,128)(2,1)S(1)} %collective-permute-done.1.refs_2_), channel_id=1, source_target_pairs={{0,56},{8,0},{16,8},{24,16},{32,24},{40,32},{48,40},{56,48},{1,57}... | collective-permute-start | bytes 442376 | tf_op jit(solution)/shard_map/ppermute | solution.py:132
  37.9 0.7 collective-permute-done.5.refs_5_
  38.6 0.3 collective-permute-done.9.refs_11_
  38.9 1.8 collective-permute-done.2.refs_3_
  40.7 4.4 %collective-permute-done.6.refs_4_ = bf16[128,576]{1,0:T(8,128)(2,1)S(1)} collective-permute-done((bf16[128,576]{1,0:T(8,128)(2,1)S(1)}, bf16[128,576]{1,0:T(8,128)(2,1)S(1)}, u32[]{:S(2)}, u32[]{:S(2)}) %collective-permute-start.6) | collective-permute-done | bytes 147488 | tf_op jit(solution)/shard_map/ppermute | solution.py:132
  45.1 5.7 %shard_map.97 = (bf16[4,4,32,1664]{3,2,1,0:T(8,128)(2,1)S(1)}, bf16[4,4,32,1664]{3,2,1,0:T(8,128)(2,1)S(1)}) custom-call(s32[4]{0:T(128)S(1)} %pad_add_fusion.place_ref, bf16[128,576]{1,0:T(8,128)(2,1)S(1)} %bitcast.33, bf16[128,576]{1,0:T(8,128)(2,1)S(1)} %collective-permute-done.refs_1_, bf16[128,576]{1,0:T(8,128)(2,1)S(1)} %collective-permute-done.1.refs_2_, ...), custom_call_target="tpu_custom_call" | custom-call | flops 1962934272 | bytes 6455296 | tf_op jit(solution)/shard_map/pallas_call | solution.py:47
  51.0 3.6 %collective-permute-done.10 = bf16[4,4,32,1664]{3,2,1,0:T(8,128)(2,1)S(1)} collective-permute-done((bf16[4,4,32,1664]{3,2,1,0:T(8,128)(2,1)S(1)}, bf16[4,4,32,1664]{3,2,1,0:T(8,128)(2,1)S(1)}, u32[]{:S(2)}, u32[]{:S(2)}) %collective-permute-start.10) | collective-permute-done | bytes 1703968 | tf_op jit(solution)/shard_map/ppermute | solution.py:305
  54.5 1.6 add_convert_fusion
  56.2 7.4 %all-to-all-start.1 = ((bf16[16,32,1664]{2,1,0:T(8,128)(2,1)}), bf16[16,32,1664]{2,1,0:T(8,128)(2,1)S(1)}, u32[]{:S(2)}, u32[]{:S(2)}) async-start(bf16[16,32,1664]{2,1,0:T(8,128)(2,1)} %bitcast.34), calls=%async_computation.1 | async-start | bytes 3407872 | tf_op jit(solution)/shard_map/all_to_all | solution.py:307
  63.5 2.2 %shard_map.99 = (bf16[384,576]{1,0:T(8,128)(2,1)S(1)}, bf16[384,576]{1,0:T(8,128)(2,1)}, bf16[384,576]{1,0:T(8,128)(2,1)S(1)}, bf16[384,576]{1,0:T(8,128)(2,1)}) custom-call(s32[4]{0:T(128)S(1)} %pad_add_fusion.place_ref, bf16[384,2304]{1,0:T(8,128)(2,1)S(1)} %copy-done.1), custom_call_target="tpu_custom_call" | custom-call | bytes 3538944 | tf_op jit(solution)/shard_map/pallas_call | solution.py:47
  65.8 0.8 copy-done.2
  66.5 0.8 copy-done.4
  67.3 20.8 %all-to-all-done.1.terms_ref = bf16[16,32,1664]{2,1,0:T(8,128)(2,1)S(1)} async-done(((bf16[16,32,1664]{2,1,0:T(8,128)(2,1)}), bf16[16,32,1664]{2,1,0:T(8,128)(2,1)S(1)}, u32[]{:S(2)}, u32[]{:S(2)}) %all-to-all-start.1) | async-done | bytes 1703968 | tf_op jit(solution)/shard_map/all_to_all | solution.py:307
  88.1 0.8 shard_map.98
  89.0 2.0 %collective-permute-start.12 = (bf16[384,576]{1,0:T(8,128)(2,1)}, bf16[384,576]{1,0:T(8,128)(2,1)S(1)}, u32[]{:S(2)}, u32[]{:S(2)}) collective-permute-start(bf16[384,576]{1,0:T(8,128)(2,1)} %get-tuple-element.45), channel_id=1, source_target_pairs={{0,192},{64,0},{128,64},{192,128},{1,193},{65,1},{129,65},{193,129... | collective-permute-start | bytes 1327112 | tf_op jit(solution)/shard_map/ppermute | solution.py:132
  91.2 0.7 reshape.101
  91.9 6.4 %all-to-all-start.2 = ((bf16[8,4,1664]{2,1,0:T(4,128)(2,1)}), bf16[8,4,1664]{2,1,0:T(4,128)(2,1)S(1)}, u32[]{:S(2)}, u32[]{:S(2)}) async-start(bf16[8,4,1664]{2,1,0:T(4,128)(2,1)} %reshape.101), calls=%async_computation.2 | async-start | bytes 212992 | tf_op jit(solution)/shard_map/all_to_all | solution.py:311
  98.4 1.6 collective-permute-start.13
  100.0 7.2 %all-to-all-done.2 = bf16[8,4,1664]{2,1,0:T(4,128)(2,1)S(1)} async-done(((bf16[8,4,1664]{2,1,0:T(4,128)(2,1)}), bf16[8,4,1664]{2,1,0:T(4,128)(2,1)S(1)}, u32[]{:S(2)}, u32[]{:S(2)}) %all-to-all-start.2) | async-done | bytes 106528 | tf_op jit(solution)/shard_map/all_to_all | solution.py:311
  107.6 2.6 %fusion.26 = (f32[2,96]{1,0:T(2,128)S(1)}, f32[2,96,2048]{2,1,0:T(8,128)S(1)}) fusion(bf16[2,96,256]{2,1,0:T(8,128)(2,1)S(1)} %bitcast.36, bf16[2,2048,512]{2,1,0:T(8,128)(2,1)} %param.14, pred[2,2048]{1,0:T(4,128)(4,1)S(1)} %iota_compare_fusion), kind=kOutput, calls=%fused_computation.35 | convolution fusion | flops 202506048 | bytes 3773184 | tf_op jit(solution)/shard_map/srd,smd->srm/dot_general | solution.py:25
  110.7 0.4 fusion.4
  111.1 0.5 fusion.12
  111.9 11.1 %all_to_all.31 = bf16[8,4,1536]{2,1,0:T(4,128)(2,1)S(1)} all-to-all(bf16[8,4,1536]{2,1,0:T(4,128)(2,1)S(1)} %copy.38), channel_id=1, replica_groups=mesh['y'=4,'z'=8,'x'=4,'core'=2] {'z'}, dimensions={0} | all-to-all | bytes 196608 | tf_op jit(solution)/shard_map/all_to_all | solution.py:325
  123.2 28.8 %all_to_all.32.own_ref = bf16[16,32,1536]{2,1,0:T(8,128)(2,1)S(1)} all-to-all(bf16[16,32,1536]{2,1,0:T(8,128)(2,1)S(1)} %broadcast_in_dim.60), channel_id=1, replica_groups=mesh['y'=4,'z'=8,'x'=4,'core'=2] {'x','y'}, dimensions={0} | all-to-all | bytes 3145728 | tf_op jit(solution)/shard_map/all_to_all | solution.py:329
  152.1 3.4 %collective-permute-done.14.other_ref = bf16[16,32,1536]{2,1,0:T(8,128)(2,1)S(1)} collective-permute-done((bf16[16,32,1536]{2,1,0:T(8,128)(2,1)S(1)}, bf16[16,32,1536]{2,1,0:T(8,128)(2,1)S(1)}, u32[]{:S(2)}, u32[]{:S(2)}) %collective-permute-start.14) | collective-permute-done | bytes 1572896 | tf_op jit(solution)/shard_map/ppermute | solution.py:330
  155.5 4.6 %shard_map.100 = (bf16[128,576]{1,0:T(8,128)(2,1)S(1)}, bf16[128,576]{1,0:T(8,128)(2,1)S(1)}, bf16[128,576]{1,0:T(8,128)(2,1)S(1)}, bf16[128,576]{1,0:T(8,128)(2...) custom-call(s32[4]{0:T(128)S(1)} %pad_add_fusion.place_ref, ...), custom_call_target="tpu_custom_call" | custom-call | flops 1811939328 | bytes 6094848 | tf_op jit(solution)/shard_map/pallas_call | solution.py:47
  160.1 0.6 collective-permute-start.15
  160.7 2.7 %collective-permute-start.19 = (bf16[128,576]{1,0:T(8,128)(2,1)S(1)}, bf16[128,576]{1,0:T(8,128)(2,1)S(1)}, u32[]{:S(2)}, u32[]{:S(2)}) collective-permute-start(bf16[128,576]{1,0:T(8,128)(2,1)S(1)} %get-tuple-element.63), channel_id=1, source_target_pairs={{0,56},{8,0},{16,8},{24,16},{32,24},{40,32},{48,40},{56,48},{1,57}... | collective-permute-start | bytes 442376 | tf_op jit(solution)/shard_map/ppermute | solution.py:132
  163.4 4.2 %collective-permute-done.15 = bf16[128,576]{1,0:T(8,128)(2,1)S(1)} collective-permute-done((bf16[128,576]{1,0:T(8,128)(2,1)S(1)}, bf16[128,576]{1,0:T(8,128)(2,1)S(1)}, u32[]{:S(2)}, u32[]{:S(2)}) %collective-permute-start.15) | collective-permute-done | bytes 147488 | tf_op jit(solution)/shard_map/ppermute | solution.py:132
  167.8 3.3 %collective-permute-start.20 = (bf16[128,576]{1,0:T(8,128)(2,1)S(1)}, bf16[128,576]{1,0:T(8,128)(2,1)S(1)}, u32[]{:S(2)}, u32[]{:S(2)}) collective-permute-start(bf16[128,576]{1,0:T(8,128)(2,1)S(1)} %add_convert_fusion.3), channel_id=1, source_target_pairs={{0,56},{8,0},{16,8},{24,16},{32,24},{40,32},{48,40},{56,48},{1,57}... | collective-permute-start | bytes 442376 | tf_op jit(solution)/shard_map/ppermute | solution.py:132
  171.1 3.3 %collective-permute-done.16 = bf16[128,576]{1,0:T(8,128)(2,1)S(1)} collective-permute-done((bf16[128,576]{1,0:T(8,128)(2,1)S(1)}, bf16[128,576]{1,0:T(8,128)(2,1)S(1)}, u32[]{:S(2)}, u32[]{:S(2)}) %collective-permute-start.16) | collective-permute-done | bytes 147488 | tf_op jit(solution)/shard_map/ppermute | solution.py:132
  174.6 3.3 %collective-permute-start.21 = (bf16[128,576]{1,0:T(8,128)(2,1)S(1)}, bf16[128,576]{1,0:T(8,128)(2,1)S(1)}, u32[]{:S(2)}, u32[]{:S(2)}) collective-permute-start(bf16[128,576]{1,0:T(8,128)(2,1)S(1)} %add_convert_fusion.2), channel_id=1, source_target_pairs={{0,56},{8,0},{16,8},{24,16},{32,24},{40,32},{48,40},{56,48},{1,57}... | collective-permute-start | bytes 442376 | tf_op jit(solution)/shard_map/ppermute | solution.py:132
  177.9 3.2 %collective-permute-done.17 = bf16[128,576]{1,0:T(8,128)(2,1)S(1)} collective-permute-done((bf16[128,576]{1,0:T(8,128)(2,1)S(1)}, bf16[128,576]{1,0:T(8,128)(2,1)S(1)}, u32[]{:S(2)}, u32[]{:S(2)}) %collective-permute-start.17) | collective-permute-done | bytes 147488 | tf_op jit(solution)/shard_map/ppermute | solution.py:132
  181.2 6.5 %collective-permute-done.18 = bf16[128,576]{1,0:T(8,128)(2,1)S(1)} collective-permute-done((bf16[128,576]{1,0:T(8,128)(2,1)S(1)}, bf16[128,576]{1,0:T(8,128)(2,1)S(1)}, u32[]{:S(2)}, u32[]{:S(2)}) %collective-permute-start.18) | collective-permute-done | bytes 147488 | tf_op jit(solution)/shard_map/ppermute | solution.py:132
  187.8 8.5 %all_to_all.33.blocks_ref = bf16[4,32,576]{2,1,0:T(8,128)(2,1)S(1)} all-to-all(bf16[4,32,576]{2,1,0:T(8,128)(2,1)S(1)} %bitcast.35), channel_id=1, replica_groups=mesh['y'=4,'z'=8,'x'=4,'core'=2] {'y'}, dimensions={0} | all-to-all | bytes 294912 | tf_op jit(solution)/shard_map/all_to_all | solution.py:333
  196.3 1.3 shard_map.101
  (68 shorter events, 2.5 us)
Async XLA Ops:
  0.6 14.2 %copy-start.6 = (bf16[2304,16]{0,1:T(8,128)(2,1)S(1)}, bf16[2304,16]{0,1:T(8,128)(2,1)}, u32[]{:S(2)}) copy-start(bf16[2304,16]{0,1:T(8,128)(2,1)} %param.12) | copy-start | bytes 221188
  0.6 14.6 %copy-start = (bf16[2304,384]{1,0:T(8,128)(2,1)S(1)}, bf16[2304,384]{1,0:T(8,128)(2,1)}, u32[]{:S(2)}) copy-start(bf16[2304,384]{1,0:T(8,128)(2,1)} %query_ref.1) | copy-start | bytes 5308420
  13.5 10.7 %collective-permute-start.3 = (bf16[128,576]{1,0:T(8,128)(2,1)S(1)}, bf16[128,576]{1,0:T(8,128)(2,1)}, u32[]{:S(2)}, u32[]{:S(2)}) collective-permute-start(bf16[128,576]{1,0:T(8,128)(2,1)S(1)} %bitcast.31), channel_id=1, source_target_pairs={{0,8},{8,16},{16,24},{24,32},{32,40},{40,48},{48,56},{56,0},{1,9},... | collective-permute-start | bytes 442376 | tf_op jit(solution)/shard_map/ppermute | solution.py:132
  16.1 22.5 %collective-permute-start.7 = (bf16[608,384]{1,0:T(8,128)(2,1)S(1)}, bf16[608,384]{1,0:T(8,128)(2,1)S(1)}, u32[]{:S(2)}, u32[]{:S(2)}) collective-permute-start(bf16[608,384]{1,0:T(8,128)(2,1)S(1)} %get-tuple-element.34), channel_id=1, source_target_pairs={{0,64},{64,128},{128,192},{192,0},{1,65},{65,129},{129,193},{193,1... | collective-permute-start | bytes 1400840 | tf_op jit(solution)/shard_map/ppermute | solution.py:132
  16.6 22.0 %collective-permute-start.8 = (bf16[608,384]{1,0:T(8,128)(2,1)S(1)}, bf16[608,384]{1,0:T(8,128)(2,1)S(1)}, u32[]{:S(2)}, u32[]{:S(2)}) collective-permute-start(bf16[608,384]{1,0:T(8,128)(2,1)S(1)} %get-tuple-element.35), channel_id=1, source_target_pairs={{0,128},{64,192},{128,0},{192,64},{1,129},{65,193},{129,1},{193,65... | collective-permute-start | bytes 1400840 | tf_op jit(solution)/shard_map/ppermute | solution.py:132
  19.7 19.2 %collective-permute-start.9 = (bf16[608,384]{1,0:T(8,128)(2,1)S(1)}, bf16[608,384]{1,0:T(8,128)(2,1)S(1)}, u32[]{:S(2)}, u32[]{:S(2)}) collective-permute-start(bf16[608,384]{1,0:T(8,128)(2,1)S(1)} %get-tuple-element.36), channel_id=1, source_target_pairs={{0,192},{64,0},{128,64},{192,128},{1,193},{65,1},{129,65},{193,129... | collective-permute-start | bytes 1400840 | tf_op jit(solution)/shard_map/ppermute | solution.py:132
  20.2 6.8 %collective-permute-start = (bf16[128,576]{1,0:T(8,128)(2,1)S(1)}, bf16[128,576]{1,0:T(8,128)(2,1)S(1)}, u32[]{:S(2)}, u32[]{:S(2)}) collective-permute-start(bf16[128,576]{1,0:T(8,128)(2,1)S(1)} %bitcast.32), channel_id=1, source_target_pairs={{0,56},{8,0},{16,8},{24,16},{32,24},{40,32},{48,40},{56,48},{1,57}... | collective-permute-start | bytes 442376 | tf_op jit(solution)/shard_map/ppermute | solution.py:132
  24.2 6.7 %collective-permute-start.4 = (bf16[128,576]{1,0:T(8,128)(2,1)}, bf16[128,576]{1,0:T(8,128)(2,1)S(1)}, u32[]{:S(2)}, u32[]{:S(2)}) collective-permute-start(bf16[128,576]{1,0:T(8,128)(2,1)} %collective-permute-done.3.refs_7_), channel_id=1, source_target_pairs={{0,8},{8,16},{16,24},{24,32},{32,40},{40,48},{48,56},{56,0},{1,9},... | collective-permute-start | bytes 442376 | tf_op jit(solution)/shard_map/ppermute | solution.py:132
  27.0 7.2 %collective-permute-start.1 = (bf16[128,576]{1,0:T(8,128)(2,1)S(1)}, bf16[128,576]{1,0:T(8,128)(2,1)S(1)}, u32[]{:S(2)}, u32[]{:S(2)}) collective-permute-start(bf16[128,576]{1,0:T(8,128)(2,1)S(1)} %collective-permute-done.refs_1_), channel_id=1, source_target_pairs={{0,56},{8,0},{16,8},{24,16},{32,24},{40,32},{48,40},{56,48},{1,57}... | collective-permute-start | bytes 442376 | tf_op jit(solution)/shard_map/ppermute | solution.py:132
  30.9 7.6 %collective-permute-start.5 = (bf16[128,576]{1,0:T(8,128)(2,1)S(1)}, bf16[128,576]{1,0:T(8,128)(2,1)S(1)}, u32[]{:S(2)}, u32[]{:S(2)}) collective-permute-start(bf16[128,576]{1,0:T(8,128)(2,1)S(1)} %collective-permute-done.4.refs_6_), channel_id=1, source_target_pairs={{0,8},{8,16},{16,24},{24,32},{32,40},{40,48},{48,56},{56,0},{1,9},... | collective-permute-start | bytes 442376 | tf_op jit(solution)/shard_map/ppermute | solution.py:132
  34.2 6.5 %collective-permute-start.2 = (bf16[128,576]{1,0:T(8,128)(2,1)S(1)}, bf16[128,576]{1,0:T(8,128)(2,1)S(1)}, u32[]{:S(2)}, u32[]{:S(2)}) collective-permute-start(bf16[128,576]{1,0:T(8,128)(2,1)S(1)} %collective-permute-done.1.refs_2_), channel_id=1, source_target_pairs={{0,56},{8,0},{16,8},{24,16},{32,24},{40,32},{48,40},{56,48},{1,57}... | collective-permute-start | bytes 442376 | tf_op jit(solution)/shard_map/ppermute | solution.py:132
  38.6 6.5 %collective-permute-start.6 = (bf16[128,576]{1,0:T(8,128)(2,1)S(1)}, bf16[128,576]{1,0:T(8,128)(2,1)S(1)}, u32[]{:S(2)}, u32[]{:S(2)}) collective-permute-start(bf16[128,576]{1,0:T(8,128)(2,1)S(1)} %collective-permute-done.5.refs_5_), channel_id=1, source_target_pairs={{0,8},{8,16},{16,24},{24,32},{32,40},{40,48},{48,56},{56,0},{1,9},... | collective-permute-start | bytes 442376 | tf_op jit(solution)/shard_map/ppermute | solution.py:132
  50.9 3.7 %collective-permute-start.10 = (bf16[4,4,32,1664]{3,2,1,0:T(8,128)(2,1)S(1)}, bf16[4,4,32,1664]{3,2,1,0:T(8,128)(2,1)S(1)}, u32[]{:S(2)}, u32[]{:S(2)}) collective-permute-start(bf16[4,4,32,1664]{3,2,1,0:T(8,128)(2,1)S(1)} %get-tuple-element.38), channel_id=1, source_target_pairs={{0,1},{1,0},{2,3},{3,2},{4,5},{5,4},{6,7},{7,6},{8,9},{9,8},{10,11... | collective-permute-start | bytes 5111816 | tf_op jit(solution)/shard_map/ppermute | solution.py:305
  56.2 7.4 %copy-start.1 = (bf16[384,2304]{1,0:T(8,128)(2,1)S(1)}, bf16[384,2304]{1,0:T(8,128)(2,1)}, u32[]{:S(2)}) copy-start(bf16[384,2304]{1,0:T(8,128)(2,1)} %weights_ref.1) | copy-start | bytes 5308420
  56.2 32.0 %all-to-all-start.1 = ((bf16[16,32,1664]{2,1,0:T(8,128)(2,1)}), bf16[16,32,1664]{2,1,0:T(8,128)(2,1)S(1)}, u32[]{:S(2)}, u32[]{:S(2)}) async-start(bf16[16,32,1664]{2,1,0:T(8,128)(2,1)} %bitcast.34), calls=%async_computation.1 | async-start | bytes 3407872 | tf_op jit(solution)/shard_map/all_to_all | solution.py:307
  63.5 27.5 %copy-start.7 = (s32[2]{0:T(128)S(1)}, s32[2]{0:T(128)}, u32[]{:S(2)}) copy-start(s32[2]{0:T(128)} %param.15) | copy-start | bytes 28
  65.8 0.8 copy-start.2
  66.5 0.8 copy-start.4
  88.1 10.2 %copy-start.5 = (bf16[384,576]{1,0:T(8,128)(2,1)S(1)}, bf16[384,576]{1,0:T(8,128)(2,1)}, u32[]{:S(2)}) copy-start(bf16[384,576]{1,0:T(8,128)(2,1)} %copy-done.4) | copy-start | bytes 1327108
  88.9 18.2 %collective-permute-start.11 = (bf16[384,576]{1,0:T(8,128)(2,1)}, bf16[384,576]{1,0:T(8,128)(2,1)S(1)}, u32[]{:S(2)}, u32[]{:S(2)}) collective-permute-start(bf16[384,576]{1,0:T(8,128)(2,1)} %get-tuple-element.44), channel_id=1, source_target_pairs={{0,64},{64,128},{128,192},{192,0},{1,65},{65,129},{129,193},{193,1... | collective-permute-start | bytes 1327112 | tf_op jit(solution)/shard_map/ppermute | solution.py:132
  89.0 18.1 %collective-permute-start.12 = (bf16[384,576]{1,0:T(8,128)(2,1)}, bf16[384,576]{1,0:T(8,128)(2,1)S(1)}, u32[]{:S(2)}, u32[]{:S(2)}) collective-permute-start(bf16[384,576]{1,0:T(8,128)(2,1)} %get-tuple-element.45), channel_id=1, source_target_pairs={{0,192},{64,0},{128,64},{192,128},{1,193},{65,1},{129,65},{193,129... | collective-permute-start | bytes 1327112 | tf_op jit(solution)/shard_map/ppermute | solution.py:132
  91.9 15.3 %all-to-all-start.2 = ((bf16[8,4,1664]{2,1,0:T(4,128)(2,1)}), bf16[8,4,1664]{2,1,0:T(4,128)(2,1)S(1)}, u32[]{:S(2)}, u32[]{:S(2)}) async-start(bf16[8,4,1664]{2,1,0:T(4,128)(2,1)} %reshape.101), calls=%async_computation.2 | async-start | bytes 212992 | tf_op jit(solution)/shard_map/all_to_all | solution.py:311
  98.4 24.7 %collective-permute-start.13 = (bf16[384,576]{1,0:T(8,128)(2,1)S(1)}, bf16[384,576]{1,0:T(8,128)(2,1)S(1)}, u32[]{:S(2)}, u32[]{:S(2)}) collective-permute-start(bf16[384,576]{1,0:T(8,128)(2,1)S(1)} %copy-done.5), channel_id=1, source_target_pairs={{0,128},{64,192},{128,0},{192,64},{1,129},{65,193},{129,1},{193,65... | collective-permute-start | bytes 1327112 | tf_op jit(solution)/shard_map/ppermute | solution.py:132
  107.6 3.5 %copy-start.8 = (bf16[2,2048,512]{2,1,0:T(8,128)(2,1)S(1)}, bf16[2,2048,512]{2,1,0:T(8,128)(2,1)}, u32[]{:S(2)}) copy-start(bf16[2,2048,512]{2,1,0:T(8,128)(2,1)} %param.14) | copy-start | bytes 12582916
  123.2 32.3 %copy-start.3 = (bf16[384,576]{1,0:T(8,128)(2,1)S(1)}, bf16[384,576]{1,0:T(8,128)(2,1)}, u32[]{:S(2)}) copy-start(bf16[384,576]{1,0:T(8,128)(2,1)} %copy-done.2) | copy-start | bytes 1327108
  152.1 3.4 %collective-permute-start.14 = (bf16[16,32,1536]{2,1,0:T(8,128)(2,1)S(1)}, bf16[16,32,1536]{2,1,0:T(8,128)(2,1)S(1)}, u32[]{:S(2)}, u32[]{:S(2)}) collective-permute-start(bf16[16,32,1536]{2,1,0:T(8,128)(2,1)S(1)} %all_to_all.32.own_ref), channel_id=1, source_target_pairs={{0,1},{1,0},{2,3},{3,2},{4,5},{5,4},{6,7},{7,6},{8,9},{9,8},{10,11... | collective-permute-start | bytes 4718600 | tf_op jit(solution)/shard_map/ppermute | solution.py:330
  160.1 7.5 %collective-permute-start.15 = (bf16[128,576]{1,0:T(8,128)(2,1)S(1)}, bf16[128,576]{1,0:T(8,128)(2,1)S(1)}, u32[]{:S(2)}, u32[]{:S(2)}) collective-permute-start(bf16[128,576]{1,0:T(8,128)(2,1)S(1)} %get-tuple-element.60), channel_id=1, source_target_pairs={{0,8},{8,16},{16,24},{24,32},{32,40},{40,48},{48,56},{56,0},{1,9},... | collective-permute-start | bytes 442376 | tf_op jit(solution)/shard_map/ppermute | solution.py:132
  160.7 7.0 %collective-permute-start.19 = (bf16[128,576]{1,0:T(8,128)(2,1)S(1)}, bf16[128,576]{1,0:T(8,128)(2,1)S(1)}, u32[]{:S(2)}, u32[]{:S(2)}) collective-permute-start(bf16[128,576]{1,0:T(8,128)(2,1)S(1)} %get-tuple-element.63), channel_id=1, source_target_pairs={{0,56},{8,0},{16,8},{24,16},{32,24},{40,32},{48,40},{56,48},{1,57}... | collective-permute-start | bytes 442376 | tf_op jit(solution)/shard_map/ppermute | solution.py:132
  167.7 6.7 %collective-permute-start.16 = (bf16[128,576]{1,0:T(8,128)(2,1)S(1)}, bf16[128,576]{1,0:T(8,128)(2,1)S(1)}, u32[]{:S(2)}, u32[]{:S(2)}) collective-permute-start(bf16[128,576]{1,0:T(8,128)(2,1)S(1)} %add_convert_fusion.6), channel_id=1, source_target_pairs={{0,8},{8,16},{16,24},{24,32},{32,40},{40,48},{48,56},{56,0},{1,9},... | collective-permute-start | bytes 442376 | tf_op jit(solution)/shard_map/ppermute | solution.py:132
  167.8 6.7 %collective-permute-start.20 = (bf16[128,576]{1,0:T(8,128)(2,1)S(1)}, bf16[128,576]{1,0:T(8,128)(2,1)S(1)}, u32[]{:S(2)}, u32[]{:S(2)}) collective-permute-start(bf16[128,576]{1,0:T(8,128)(2,1)S(1)} %add_convert_fusion.3), channel_id=1, source_target_pairs={{0,56},{8,0},{16,8},{24,16},{32,24},{40,32},{48,40},{56,48},{1,57}... | collective-permute-start | bytes 442376 | tf_op jit(solution)/shard_map/ppermute | solution.py:132
  174.4 6.6 %collective-permute-start.17 = (bf16[128,576]{1,0:T(8,128)(2,1)S(1)}, bf16[128,576]{1,0:T(8,128)(2,1)S(1)}, u32[]{:S(2)}, u32[]{:S(2)}) collective-permute-start(bf16[128,576]{1,0:T(8,128)(2,1)S(1)} %add_convert_fusion.5), channel_id=1, source_target_pairs={{0,8},{8,16},{16,24},{24,32},{32,40},{40,48},{48,56},{56,0},{1,9},... | collective-permute-start | bytes 442376 | tf_op jit(solution)/shard_map/ppermute | solution.py:132
  174.6 6.6 %collective-permute-start.21 = (bf16[128,576]{1,0:T(8,128)(2,1)S(1)}, bf16[128,576]{1,0:T(8,128)(2,1)S(1)}, u32[]{:S(2)}, u32[]{:S(2)}) collective-permute-start(bf16[128,576]{1,0:T(8,128)(2,1)S(1)} %add_convert_fusion.2), channel_id=1, source_target_pairs={{0,56},{8,0},{16,8},{24,16},{32,24},{40,32},{48,40},{56,48},{1,57}... | collective-permute-start | bytes 442376 | tf_op jit(solution)/shard_map/ppermute | solution.py:132
  181.1 6.6 %collective-permute-start.18 = (bf16[128,576]{1,0:T(8,128)(2,1)S(1)}, bf16[128,576]{1,0:T(8,128)(2,1)S(1)}, u32[]{:S(2)}, u32[]{:S(2)}) collective-permute-start(bf16[128,576]{1,0:T(8,128)(2,1)S(1)} %add_convert_fusion.4), channel_id=1, source_target_pairs={{0,8},{8,16},{16,24},{24,32},{32,40},{40,48},{48,56},{56,0},{1,9},... | collective-permute-start | bytes 442376 | tf_op jit(solution)/shard_map/ppermute | solution.py:132

commit v4 on v3

--- a/solution.py
+++ b/solution.py
@@ -163,7 +163,7 @@
     part = nx * per
     total = ny * cols + 128
     shape = (nx, ny, nz * per, total)
-    group = nz // 2
+    group = min(nz, 4)
 
     def kernel(place_ref, *refs):
         row_refs, refs = refs[:nz], refs[nz:]
@@ -214,12 +214,29 @@
     )
 
 
-def sum_terms(place, terms, per):
+def add_halves(place, ones, others):
+    nx, ny, rows, cols = ones[0].shape
+    count = len(ones)
+
+    def kernel(place_ref, *refs):
+        out_ref = refs[-1]
+        for h in range(count):
+            for x in range(nx):
+                for y in range(ny):
+                    total = refs[h][x, y].astype(F32) + refs[count + h][x, y].astype(F32)
+                    out_ref[x * ny + y, h * rows : (h + 1) * rows, :] = total.astype(BF16)
+
+    shape = jax.ShapeDtypeStruct((nx * ny, count * rows, cols), BF16)
+    return call(kernel, (place, *ones, *others), [shape], [])[0]
+
+
+def sum_terms(place, terms, per, first):
     def kernel(place_ref, terms_ref, out_ref):
         total = terms_ref[0].astype(F32)
         for i in range(1, terms_ref.shape[0]):
             total = total + terms_ref[i].astype(F32)
-        out_ref[...] = pltpu.roll(total, place_ref[2] * per, 0).astype(BF16)
+        by = lax.rem(place_ref[2] + first, total.shape[0] // per) * per
+        out_ref[...] = pltpu.roll(total, by, 0).astype(BF16)
 
     return call(kernel, (place, terms), [jax.ShapeDtypeStruct(terms.shape[1:], BF16)], [])[0]
 
@@ -293,26 +310,28 @@
     per = 2 * seqs
     depth = width // ny
 
-    quarters = input_quarters(place, w_query, w_keyval, ny)
-    weights = [quarters[0]] + [shift(quarters[k], "y", k) for k in range(1, ny)]
-
     start = ((places[3] * nc + places[1]) * width).astype(jnp.int32).reshape(1)
     mine = normalize(start, (step_one, step_two), gain, nx, nc, ny, width)
     column = lax.all_to_all(mine, "y", split_axis=0, concat_axis=0, tiled=True)
+    w_query, column = lax.optimization_barrier((w_query, column))
+    quarters = input_quarters(place, w_query, w_keyval, ny)
+    weights = [quarters[0]] + [shift(quarters[k], "y", k) for k in range(1, ny)]
     pieces = ring_pieces(column.reshape(ny * narrow * per, depth), "z")
-    keep, give = project(place, pieces, weights, pair_cols, nx, per)
-    cols = keep.shape[3]
-    other = lax.ppermute(give, "core", [(0, 1), (1, 0)])
-    pair = add(keep, other).reshape(nx * ny, nz * per, cols)
+    first = nz - nz // 4
+    turned = pieces[first:] + pieces[:first]
+    halves = [
+        project(place, half, weights, pair_cols, nx, per)
+        for half in (turned[: nz // 2], turned[nz // 2 :])
+    ]
+    cols = halves[0][0].shape[3]
+    others = [lax.ppermute(give, "core", [(0, 1), (1, 0)]) for _, give in halves]
+    pair = add_halves(place, [keep for keep, _ in halves], others)
     terms = lax.all_to_all(pair, ("x", "y"), split_axis=0, concat_axis=0, tiled=True)
-    summed = sum_terms(place, terms, per)
+    summed = sum_terms(place, terms, per, first)
     summed, *quarters = lax.optimization_barrier((summed, *output_quarters(place, w_out, ny)))
     out_weights = [quarters[0]] + [shift(quarters[k], "y", k) for k in range(1, ny)]
     arrived = lax.all_to_all(
         summed.reshape(nz, per, cols), "z", split_axis=0, concat_axis=0, tiled=True
-    )
-    arrived, out_weights[1], out_weights[-1] = lax.optimization_barrier(
-        (arrived, out_weights[1], out_weights[-1])
     )
     queries = arrived[:, :, : ny * query_cols].reshape(nz, per, ny, query_cols)
     queries = queries.transpose(1, 2, 0, 3).reshape(2, seqs, HEADS, size)

time: 198 us -> 190 us (0.960)
  blocking collectives: 58.6 us -> 45.3 us
  starting transfers between devices: 44.5 us -> 50.2 us
  waiting for transfers between devices: 65.7 us -> 62.6 us
  Pallas kernels: 18.1 us -> 20.7 us
    all_to_all x1 -> x0, blocking collectives: 10.2 us -> none  [shards(): column = lax.all_to_all(mine, 'y', split_axis=0, concat_axis=0, tiled=True)]
    all_to_all x0 -> x1, starting transfers between devices: none -> 5.5 us  [shards(): column = lax.all_to_all(mine, 'y', split_axis=0, concat_axis=0, tiled=True)]
    all_to_all x0 -> x1, waiting for transfers between devices: none -> 4.7 us  [shards(): column = lax.all_to_all(mine, 'y', split_axis=0, concat_axis=0, tiled=True)]
    ppermute x20, waiting for transfers between devices: 30.7 us -> 27 us  [shift(): lax.ppermute(value, axis, [(i, (i + by) % count) for i in range(count)])]
    all_to_all x1, blocking collectives: 28.8 us -> 25.5 us  [shards(): lax.all_to_all(copies, ('x', 'y'), split_axis=0, concat_axis=0, tiled=True)]
    pallas_call x7 -> x9, Pallas kernels: 18.1 us -> 20.7 us  [call(): pl.pallas_call(kernel, in_specs=[SMEM] + [VMEM] * (len(inputs) - 1), out_...]
    all_to_all x1, waiting for transfers between devices: 7.2 us -> 5.19 us  [shards(): lax.all_to_all(summed.reshape(nz, per, cols), 'z', split_axis=0, concat_a...]
  transfers between devices with their start and end apart: 24 -> 26, of which waited for: 15 -> 14; matrix products, arithmetic and copies ran while one was open for 3% -> 3% of each run, Pallas kernels for 2% -> 5%
where the time goes in v4:
time: 190 us; the launch traced here: 189 us
  waiting for transfers between devices  62.6 us (33%)
  starting transfers between devices  50.2 us (26%)
  blocking collectives  45.3 us (24%)
  Pallas kernels  20.7 us (11%)
  local copies, waits for them, and re-layouts  5.18 us (3%)
  matrix products  3.47 us (2%)
    ppermute x20, starting transfers between devices, shift(): lax.ppermute(value, axis, [(i, (i + by) % count) for i in range(count)])  30.6 us
    ppermute x20, waiting for transfers between devices, shift(): lax.ppermute(value, axis, [(i, (i + by) % count) for i in range(count)])  27 us
    all_to_all x1, blocking collectives, shards(): lax.all_to_all(copies, ('x', 'y'), split_axis=0, concat_axis=0, tiled=True)  25.5 us
    pallas_call x9, Pallas kernels, call(): pl.pallas_call(kernel, in_specs=[SMEM] + [VMEM] * (len(inputs) - 1), out_...  20.7 us
    all_to_all x1, waiting for transfers between devices, shards(): lax.all_to_all(pair, ('x', 'y'), split_axis=0, concat_axis=0, tiled=True)  20 us
    all_to_all x1, blocking collectives, shards(): lax.all_to_all(leaving, 'z', split_axis=0, concat_axis=0, tiled=True)  11.1 us
    all_to_all x1, blocking collectives, shards(): out = lax.all_to_all(out, 'y', split_axis=0, concat_axis=0, tiled=True)  8.71 us
    all_to_all x1, starting transfers between devices, shards(): lax.all_to_all(pair, ('x', 'y'), split_axis=0, concat_axis=0, tiled=True)  7.34 us
  transfers between devices with their start and end apart: 26, of which 14 were waited for; matrix products, arithmetic and copies ran while one was open for 3% of the time, Pallas kernels for 5%

profile of v4, /device:TPU:8, one launch (start us, length us, event | category | flops | bytes accessed | tf_op | source)
XLA Modules:
  0.0 189.4 jit_solution(10862769261802969045)
XLA Ops:
  0.6 2.6 %shard_map.95 = bf16[4,32,576]{2,1,0:T(8,128)(2,1)} custom-call(s32[1]{0:T(128)} %bitcast.4.start_ref, bf16[16,18432]{1,0:T(8,128)(2,1)} %one_ref.1, bf16[16,18432]{1,0:T(8,128)(2,1)} %two_ref.1, f32[1,18432]{1,0:T(1,128)} %bitcast.41), custom_call_target="tpu_custom_call" | custom-call | bytes 1400832 | tf_op jit(solution)/shard_map/pallas_call | solution.py:47
  3.3 5.5 %all-to-all-start = ((bf16[4,32,576]{2,1,0:T(8,128)(2,1)}), bf16[4,32,576]{2,1,0:T(8,128)(2,1)S(1)}, u32[]{:S(2)}, u32[]{:S(2)}) async-start(bf16[4,32,576]{2,1,0:T(8,128)(2,1)} %shard_map.95), calls=%async_computation | async-start | bytes 327680 | tf_op jit(solution)/shard_map/all_to_all | solution.py:315
  8.8 4.7 %all-to-all-done = bf16[4,32,576]{2,1,0:T(8,128)(2,1)S(1)} async-done(((bf16[4,32,576]{2,1,0:T(8,128)(2,1)}), bf16[4,32,576]{2,1,0:T(8,128)(2,1)S(1)}, u32[]{:S(2)}, u32[]{:S(2)}) %all-to-all-start) | async-done | bytes 147488 | tf_op jit(solution)/shard_map/all_to_all | solution.py:315
  13.4 1.3 collective-permute-start
  14.9 1.2 copy.30.keyval_ref
  16.1 0.9 shard_map.96
  17.1 3.4 %collective-permute-start.4 = (bf16[608,384]{1,0:T(8,128)(2,1)S(1)}, bf16[608,384]{1,0:T(8,128)(2,1)S(1)}, u32[]{:S(2)}, u32[]{:S(2)}) collective-permute-start(bf16[608,384]{1,0:T(8,128)(2,1)S(1)} %get-tuple-element.38), channel_id=1, source_target_pairs={{0,128},{64,192},{128,0},{192,64},{1,129},{65,193},{129,1},{193,65... | collective-permute-start | bytes 1400840 | tf_op jit(solution)/shard_map/ppermute | solution.py:132
  20.5 0.6 collective-permute-start.5
  21.1 3.9 %collective-permute-start.2 = (bf16[128,576]{1,0:T(8,128)(2,1)S(1)}, bf16[128,576]{1,0:T(8,128)(2,1)S(1)}, u32[]{:S(2)}, u32[]{:S(2)}) collective-permute-start(bf16[128,576]{1,0:T(8,128)(2,1)S(1)} %bitcast.31), channel_id=1, source_target_pairs={{0,56},{8,0},{16,8},{24,16},{32,24},{40,32},{48,40},{56,48},{1,57}... | collective-permute-start | bytes 442376 | tf_op jit(solution)/shard_map/ppermute | solution.py:132
  25.1 2.8 %collective-permute-done.2.refs_3_ = bf16[128,576]{1,0:T(8,128)(2,1)S(1)} collective-permute-done((bf16[128,576]{1,0:T(8,128)(2,1)S(1)}, bf16[128,576]{1,0:T(8,128)(2,1)S(1)}, u32[]{:S(2)}, u32[]{:S(2)}) %collective-permute-start.2) | collective-permute-done | bytes 147488 | tf_op jit(solution)/shard_map/ppermute | solution.py:132
  27.9 3.7 %collective-permute-start.6 = (bf16[128,576]{1,0:T(8,128)(2,1)S(1)}, bf16[128,576]{1,0:T(8,128)(2,1)S(1)}, u32[]{:S(2)}, u32[]{:S(2)}) collective-permute-start(bf16[128,576]{1,0:T(8,128)(2,1)S(1)} %collective-permute-done.2.refs_3_), channel_id=1, source_target_pairs={{0,56},{8,0},{16,8},{24,16},{32,24},{40,32},{48,40},{56,48},{1,57}... | collective-permute-start | bytes 442376 | tf_op jit(solution)/shard_map/ppermute | solution.py:132
  31.8 3.3 %collective-permute-done.6.refs_0_ = bf16[128,576]{1,0:T(8,128)(2,1)S(1)} collective-permute-done((bf16[128,576]{1,0:T(8,128)(2,1)S(1)}, bf16[128,576]{1,0:T(8,128)(2,1)S(1)}, u32[]{:S(2)}, u32[]{:S(2)}) %collective-permute-start.6) | collective-permute-done | bytes 147488 | tf_op jit(solution)/shard_map/ppermute | solution.py:132
  35.1 3.7 %collective-permute-start.7 = (bf16[128,576]{1,0:T(8,128)(2,1)S(1)}, bf16[128,576]{1,0:T(8,128)(2,1)S(1)}, u32[]{:S(2)}, u32[]{:S(2)}) collective-permute-start(bf16[128,576]{1,0:T(8,128)(2,1)S(1)} %collective-permute-done.6.refs_0_), channel_id=1, source_target_pairs={{0,56},{8,0},{16,8},{24,16},{32,24},{40,32},{48,40},{56,48},{1,57}... | collective-permute-start | bytes 442376 | tf_op jit(solution)/shard_map/ppermute | solution.py:132
  38.7 0.7 collective-permute-done.8.refs_3_
  39.5 3.4 %shard_map.97 = (bf16[4,4,16,1664]{3,2,1,0:T(8,128)(2,1)S(1)}, bf16[4,4,16,1664]{3,2,1,0:T(8,128)(2,1)S(1)}) custom-call(s32[4]{0:T(128)S(1)} %pad_add_fusion.place_ref, bf16[128,576]{1,0:T(8,128)(2,1)S(1)} %collective-permute-done.1.refs_0_, bf16[128,576]{1,0:T(8,128)(2,1)} %collective-permute-done.refs_1_, bf16[128,576]{1,0:T(8,128)(2,1)S(1)} %bitcast.32, ...), custom_call_target="tpu_custom_call" | custom-call | flops 981467136 | bytes 4161536 | tf_op jit(solution)/shard_map/pallas_call | solution.py:47
  42.9 0.3 collective-permute-start.10
  43.2 2.8 %collective-permute-done.9.refs_2_ = bf16[128,576]{1,0:T(8,128)(2,1)S(1)} collective-permute-done((bf16[128,576]{1,0:T(8,128)(2,1)S(1)}, bf16[128,576]{1,0:T(8,128)(2,1)S(1)}, u32[]{:S(2)}, u32[]{:S(2)}) %collective-permute-start.9) | collective-permute-done | bytes 147488 | tf_op jit(solution)/shard_map/ppermute | solution.py:132
  46.0 3.0 %shard_map.98 = (bf16[4,4,16,1664]{3,2,1,0:T(8,128)(2,1)S(1)}, bf16[4,4,16,1664]{3,2,1,0:T(8,128)(2,1)S(1)}) custom-call(s32[4]{0:T(128)S(1)} %pad_add_fusion.place_ref, bf16[128,576]{1,0:T(8,128)(2,1)S(1)} %collective-permute-done.6.refs_0_, bf16[128,576]{1,0:T(8,128)(2,1)S(1)} %collective-permute-done.7.refs_1_, ...), custom_call_target="tpu_custom_call" | custom-call | flops 981467136 | bytes 4161536 | tf_op jit(solution)/shard_map/pallas_call | solution.py:47
  49.1 2.4 %collective-permute-done.11.refs_3_ = bf16[4,4,16,1664]{3,2,1,0:T(8,128)(2,1)S(1)} collective-permute-done((bf16[4,4,16,1664]{3,2,1,0:T(8,128)(2,1)S(1)}, bf16[4,4,16,1664]{3,2,1,0:T(8,128)(2,1)S(1)}, u32[]{:S(2)}, u32[]{:S(2)}) %collective-permute-start.11) | collective-permute-done | bytes 852000 | tf_op jit(solution)/shard_map/ppermute | solution.py:327
  51.5 2.1 %shard_map.99 = bf16[16,32,1664]{2,1,0:T(8,128)(2,1)} custom-call(s32[4]{0:T(128)S(1)} %pad_add_fusion.place_ref, bf16[4,4,16,1664]{3,2,1,0:T(8,128)(2,1)S(1)} %get-tuple-element.40.refs_0_, bf16[4,4,16,1664]{3,2,1,0:T(8,128)(2,1)S(1)} %get-tuple-element.41.refs_1_, bf16[4,4,16,1664]{3,2,1,0:T(8,128)(2,1)S(1)} %collective-permute-done.10.refs_2_, ...), custom_call_target="tpu_custom_call" | custom-call | bytes 5111808 | tf_op jit(solution)/shard_map/pallas_call | solution.py:47
  53.6 7.3 %all-to-all-start.1 = ((bf16[16,32,1664]{2,1,0:T(8,128)(2,1)}), bf16[16,32,1664]{2,1,0:T(8,128)(2,1)S(1)}, u32[]{:S(2)}, u32[]{:S(2)}) async-start(bf16[16,32,1664]{2,1,0:T(8,128)(2,1)} %shard_map.99), calls=%async_computation.1 | async-start | bytes 3407872 | tf_op jit(solution)/shard_map/all_to_all | solution.py:329
  61.1 2.0 %shard_map.101 = (bf16[384,576]{1,0:T(8,128)(2,1)S(1)}, bf16[384,576]{1,0:T(8,128)(2,1)}, bf16[384,576]{1,0:T(8,128)(2,1)S(1)}, bf16[384,576]{1,0:T(8,128)(2,1)S(1)}) custom-call(s32[4]{0:T(128)S(1)} %pad_add_fusion.place_ref, bf16[384,2304]{1,0:T(8,128)(2,1)S(1)} %copy-done.1), custom_call_target="tpu_custom_call" | custom-call | bytes 3538944 | tf_op jit(solution)/shard_map/pallas_call | solution.py:47
  63.1 0.8 copy-done.2
  63.9 0.8 copy-done.4
  64.7 0.8 copy-done.6
  65.6 20.0 %all-to-all-done.1.terms_ref = bf16[16,32,1664]{2,1,0:T(8,128)(2,1)S(1)} async-done(((bf16[16,32,1664]{2,1,0:T(8,128)(2,1)}), bf16[16,32,1664]{2,1,0:T(8,128)(2,1)S(1)}, u32[]{:S(2)}, u32[]{:S(2)}) %all-to-all-start.1) | async-done | bytes 1703968 | tf_op jit(solution)/shard_map/all_to_all | solution.py:329
  85.6 0.8 shard_map.100
  86.4 0.7 reshape.97
  87.0 6.4 %all-to-all-start.2 = ((bf16[8,4,1664]{2,1,0:T(4,128)(2,1)}), bf16[8,4,1664]{2,1,0:T(4,128)(2,1)S(1)}, u32[]{:S(2)}, u32[]{:S(2)}) async-start(bf16[8,4,1664]{2,1,0:T(4,128)(2,1)} %reshape.97), calls=%async_computation.2 | async-start | bytes 212992 | tf_op jit(solution)/shard_map/all_to_all | solution.py:333
  93.6 3.5 %collective-permute-start.13 = (bf16[384,576]{1,0:T(8,128)(2,1)S(1)}, bf16[384,576]{1,0:T(8,128)(2,1)S(1)}, u32[]{:S(2)}, u32[]{:S(2)}) collective-permute-start(bf16[384,576]{1,0:T(8,128)(2,1)S(1)} %copy-done.7), channel_id=1, source_target_pairs={{0,128},{64,192},{128,0},{192,64},{1,129},{65,193},{129,1},{193,65... | collective-permute-start | bytes 1327112 | tf_op jit(solution)/shard_map/ppermute | solution.py:132
  97.1 5.2 %all-to-all-done.2 = bf16[8,4,1664]{2,1,0:T(4,128)(2,1)S(1)} async-done(((bf16[8,4,1664]{2,1,0:T(4,128)(2,1)}), bf16[8,4,1664]{2,1,0:T(4,128)(2,1)S(1)}, u32[]{:S(2)}, u32[]{:S(2)}) %all-to-all-start.2) | async-done | bytes 106528 | tf_op jit(solution)/shard_map/all_to_all | solution.py:333
  102.9 2.6 %fusion.26 = (f32[2,96]{1,0:T(2,128)S(1)}, f32[2,96,2048]{2,1,0:T(8,128)S(1)}) fusion(bf16[2,96,256]{2,1,0:T(8,128)(2,1)S(1)} %bitcast.35, bf16[2,2048,512]{2,1,0:T(8,128)(2,1)} %param.14, pred[2,2048]{1,0:T(4,128)(4,1)S(1)} %iota_compare_fusion), kind=kOutput, calls=%fused_computation.34 | convolution fusion | flops 202506048 | bytes 3773184 | tf_op jit(solution)/shard_map/srd,smd->srm/dot_general | solution.py:25
  105.8 0.4 fusion.4
  106.2 0.5 fusion.12
  107.0 11.1 %all_to_all.30 = bf16[8,4,1536]{2,1,0:T(4,128)(2,1)S(1)} all-to-all(bf16[8,4,1536]{2,1,0:T(4,128)(2,1)S(1)} %copy.38), channel_id=1, replica_groups=mesh['y'=4,'z'=8,'x'=4,'core'=2] {'z'}, dimensions={0} | all-to-all | bytes 196608 | tf_op jit(solution)/shard_map/all_to_all | solution.py:344
  118.4 25.5 %all_to_all.31.own_ref = bf16[16,32,1536]{2,1,0:T(8,128)(2,1)S(1)} all-to-all(bf16[16,32,1536]{2,1,0:T(8,128)(2,1)S(1)} %broadcast_in_dim.60), channel_id=1, replica_groups=mesh['y'=4,'z'=8,'x'=4,'core'=2] {'x','y'}, dimensions={0} | all-to-all | bytes 3145728 | tf_op jit(solution)/shard_map/all_to_all | solution.py:348
  143.8 3.4 %collective-permute-done.15.other_ref = bf16[16,32,1536]{2,1,0:T(8,128)(2,1)S(1)} collective-permute-done((bf16[16,32,1536]{2,1,0:T(8,128)(2,1)S(1)}, bf16[16,32,1536]{2,1,0:T(8,128)(2,1)S(1)}, u32[]{:S(2)}, u32[]{:S(2)}) %collective-permute-start.15) | collective-permute-done | bytes 1572896 | tf_op jit(solution)/shard_map/ppermute | solution.py:349
  147.3 4.5 %shard_map.102 = (bf16[128,576]{1,0:T(8,128)(2,1)S(1)}, bf16[128,576]{1,0:T(8,128)(2,1)S(1)}, bf16[128,576]{1,0:T(8,128)(2,1)S(1)}, bf16[128,576]{1,0:T(8,128)(2...) custom-call(s32[4]{0:T(128)S(1)} %pad_add_fusion.place_ref, ...), custom_call_target="tpu_custom_call" | custom-call | flops 1811939328 | bytes 6094848 | tf_op jit(solution)/shard_map/pallas_call | solution.py:47
  151.8 1.5 collective-permute-start.16
  153.3 1.8 collective-permute-start.20
  155.1 4.2 %collective-permute-done.16 = bf16[128,576]{1,0:T(8,128)(2,1)S(1)} collective-permute-done((bf16[128,576]{1,0:T(8,128)(2,1)S(1)}, bf16[128,576]{1,0:T(8,128)(2,1)S(1)}, u32[]{:S(2)}, u32[]{:S(2)}) %collective-permute-start.16) | collective-permute-done | bytes 147488 | tf_op jit(solution)/shard_map/ppermute | solution.py:132
  159.7 3.1 %collective-permute-start.21 = (bf16[128,576]{1,0:T(8,128)(2,1)S(1)}, bf16[128,576]{1,0:T(8,128)(2,1)S(1)}, u32[]{:S(2)}, u32[]{:S(2)}) collective-permute-start(bf16[128,576]{1,0:T(8,128)(2,1)S(1)} %add_convert_fusion.2), channel_id=1, source_target_pairs={{0,56},{8,0},{16,8},{24,16},{32,24},{40,32},{48,40},{56,48},{1,57}... | collective-permute-start | bytes 442376 | tf_op jit(solution)/shard_map/ppermute | solution.py:132
  162.8 3.3 %collective-permute-done.17 = bf16[128,576]{1,0:T(8,128)(2,1)S(1)} collective-permute-done((bf16[128,576]{1,0:T(8,128)(2,1)S(1)}, bf16[128,576]{1,0:T(8,128)(2,1)S(1)}, u32[]{:S(2)}, u32[]{:S(2)}) %collective-permute-start.17) | collective-permute-done | bytes 147488 | tf_op jit(solution)/shard_map/ppermute | solution.py:132
  166.3 3.3 %collective-permute-start.22 = (bf16[128,576]{1,0:T(8,128)(2,1)S(1)}, bf16[128,576]{1,0:T(8,128)(2,1)S(1)}, u32[]{:S(2)}, u32[]{:S(2)}) collective-permute-start(bf16[128,576]{1,0:T(8,128)(2,1)S(1)} %add_convert_fusion.1), channel_id=1, source_target_pairs={{0,56},{8,0},{16,8},{24,16},{32,24},{40,32},{48,40},{56,48},{1,57}... | collective-permute-start | bytes 442376 | tf_op jit(solution)/shard_map/ppermute | solution.py:132
  169.6 3.2 %collective-permute-done.18 = bf16[128,576]{1,0:T(8,128)(2,1)S(1)} collective-permute-done((bf16[128,576]{1,0:T(8,128)(2,1)S(1)}, bf16[128,576]{1,0:T(8,128)(2,1)S(1)}, u32[]{:S(2)}, u32[]{:S(2)}) %collective-permute-start.18) | collective-permute-done | bytes 147488 | tf_op jit(solution)/shard_map/ppermute | solution.py:132
  172.9 6.5 %collective-permute-done.19 = bf16[128,576]{1,0:T(8,128)(2,1)S(1)} collective-permute-done((bf16[128,576]{1,0:T(8,128)(2,1)S(1)}, bf16[128,576]{1,0:T(8,128)(2,1)S(1)}, u32[]{:S(2)}, u32[]{:S(2)}) %collective-permute-start.19) | collective-permute-done | bytes 147488 | tf_op jit(solution)/shard_map/ppermute | solution.py:132
  179.4 8.7 %all_to_all.32.blocks_ref = bf16[4,32,576]{2,1,0:T(8,128)(2,1)S(1)} all-to-all(bf16[4,32,576]{2,1,0:T(8,128)(2,1)S(1)} %bitcast.33), channel_id=1, replica_groups=mesh['y'=4,'z'=8,'x'=4,'core'=2] {'y'}, dimensions={0} | all-to-all | bytes 294912 | tf_op jit(solution)/shard_map/all_to_all | solution.py:352
  188.2 1.3 shard_map.103
  (74 shorter events, 2.9 us)
Async XLA Ops:
  0.6 15.4 %copy-start = (bf16[2304,384]{1,0:T(8,128)(2,1)S(1)}, bf16[2304,384]{1,0:T(8,128)(2,1)}, u32[]{:S(2)}) copy-start(bf16[2304,384]{1,0:T(8,128)(2,1)} %query_ref) | copy-start | bytes 5308420
  3.3 10.2 %all-to-all-start = ((bf16[4,32,576]{2,1,0:T(8,128)(2,1)}), bf16[4,32,576]{2,1,0:T(8,128)(2,1)S(1)}, u32[]{:S(2)}, u32[]{:S(2)}) async-start(bf16[4,32,576]{2,1,0:T(8,128)(2,1)} %shard_map.95), calls=%async_computation | async-start | bytes 327680 | tf_op jit(solution)/shard_map/all_to_all | solution.py:315
  13.4 11.6 %collective-permute-start = (bf16[128,576]{1,0:T(8,128)(2,1)S(1)}, bf16[128,576]{1,0:T(8,128)(2,1)}, u32[]{:S(2)}, u32[]{:S(2)}) collective-permute-start(bf16[128,576]{1,0:T(8,128)(2,1)S(1)} %bitcast.30), channel_id=1, source_target_pairs={{0,8},{8,16},{16,24},{24,32},{32,40},{40,48},{48,56},{56,0},{1,9},... | collective-permute-start | bytes 442376 | tf_op jit(solution)/shard_map/ppermute | solution.py:132
  16.9 22.5 %collective-permute-start.3 = (bf16[608,384]{1,0:T(8,128)(2,1)S(1)}, bf16[608,384]{1,0:T(8,128)(2,1)S(1)}, u32[]{:S(2)}, u32[]{:S(2)}) collective-permute-start(bf16[608,384]{1,0:T(8,128)(2,1)S(1)} %get-tuple-element.37), channel_id=1, source_target_pairs={{0,64},{64,128},{128,192},{192,0},{1,65},{65,129},{129,193},{193,1... | collective-permute-start | bytes 1400840 | tf_op jit(solution)/shard_map/ppermute | solution.py:132
  17.1 22.3 %collective-permute-start.4 = (bf16[608,384]{1,0:T(8,128)(2,1)S(1)}, bf16[608,384]{1,0:T(8,128)(2,1)S(1)}, u32[]{:S(2)}, u32[]{:S(2)}) collective-permute-start(bf16[608,384]{1,0:T(8,128)(2,1)S(1)} %get-tuple-element.38), channel_id=1, source_target_pairs={{0,128},{64,192},{128,0},{192,64},{1,129},{65,193},{129,1},{193,65... | collective-permute-start | bytes 1400840 | tf_op jit(solution)/shard_map/ppermute | solution.py:132
  20.5 18.9 %collective-permute-start.5 = (bf16[608,384]{1,0:T(8,128)(2,1)S(1)}, bf16[608,384]{1,0:T(8,128)(2,1)S(1)}, u32[]{:S(2)}, u32[]{:S(2)}) collective-permute-start(bf16[608,384]{1,0:T(8,128)(2,1)S(1)} %get-tuple-element.39), channel_id=1, source_target_pairs={{0,192},{64,0},{128,64},{192,128},{1,193},{65,1},{129,65},{193,129... | collective-permute-start | bytes 1400840 | tf_op jit(solution)/shard_map/ppermute | solution.py:132
  21.1 6.8 %collective-permute-start.2 = (bf16[128,576]{1,0:T(8,128)(2,1)S(1)}, bf16[128,576]{1,0:T(8,128)(2,1)S(1)}, u32[]{:S(2)}, u32[]{:S(2)}) collective-permute-start(bf16[128,576]{1,0:T(8,128)(2,1)S(1)} %bitcast.31), channel_id=1, source_target_pairs={{0,56},{8,0},{16,8},{24,16},{32,24},{40,32},{48,40},{56,48},{1,57}... | collective-permute-start | bytes 442376 | tf_op jit(solution)/shard_map/ppermute | solution.py:132
  25.1 6.7 %collective-permute-start.1 = (bf16[128,576]{1,0:T(8,128)(2,1)}, bf16[128,576]{1,0:T(8,128)(2,1)S(1)}, u32[]{:S(2)}, u32[]{:S(2)}) collective-permute-start(bf16[128,576]{1,0:T(8,128)(2,1)} %collective-permute-done.refs_1_), channel_id=1, source_target_pairs={{0,8},{8,16},{16,24},{24,32},{32,40},{40,48},{48,56},{56,0},{1,9},... | collective-permute-start | bytes 442376 | tf_op jit(solution)/shard_map/ppermute | solution.py:132
  27.9 7.2 %collective-permute-start.6 = (bf16[128,576]{1,0:T(8,128)(2,1)S(1)}, bf16[128,576]{1,0:T(8,128)(2,1)S(1)}, u32[]{:S(2)}, u32[]{:S(2)}) collective-permute-start(bf16[128,576]{1,0:T(8,128)(2,1)S(1)} %collective-permute-done.2.refs_3_), channel_id=1, source_target_pairs={{0,56},{8,0},{16,8},{24,16},{32,24},{40,32},{48,40},{56,48},{1,57}... | collective-permute-start | bytes 442376 | tf_op jit(solution)/shard_map/ppermute | solution.py:132
  31.8 7.6 %collective-permute-start.8 = (bf16[128,576]{1,0:T(8,128)(2,1)S(1)}, bf16[128,576]{1,0:T(8,128)(2,1)S(1)}, u32[]{:S(2)}, u32[]{:S(2)}) collective-permute-start(bf16[128,576]{1,0:T(8,128)(2,1)S(1)} %collective-permute-done.1.refs_0_), channel_id=1, source_target_pairs={{0,8},{8,16},{16,24},{24,32},{32,40},{40,48},{48,56},{56,0},{1,9},... | collective-permute-start | bytes 442376 | tf_op jit(solution)/shard_map/ppermute | solution.py:132
  35.1 8.1 %collective-permute-start.7 = (bf16[128,576]{1,0:T(8,128)(2,1)S(1)}, bf16[128,576]{1,0:T(8,128)(2,1)S(1)}, u32[]{:S(2)}, u32[]{:S(2)}) collective-permute-start(bf16[128,576]{1,0:T(8,128)(2,1)S(1)} %collective-permute-done.6.refs_0_), channel_id=1, source_target_pairs={{0,56},{8,0},{16,8},{24,16},{32,24},{40,32},{48,40},{56,48},{1,57}... | collective-permute-start | bytes 442376 | tf_op jit(solution)/shard_map/ppermute | solution.py:132
  39.4 6.5 %collective-permute-start.9 = (bf16[128,576]{1,0:T(8,128)(2,1)S(1)}, bf16[128,576]{1,0:T(8,128)(2,1)S(1)}, u32[]{:S(2)}, u32[]{:S(2)}) collective-permute-start(bf16[128,576]{1,0:T(8,128)(2,1)S(1)} %collective-permute-done.8.refs_3_), channel_id=1, source_target_pairs={{0,8},{8,16},{16,24},{24,32},{32,40},{40,48},{48,56},{56,0},{1,9},... | collective-permute-start | bytes 442376 | tf_op jit(solution)/shard_map/ppermute | solution.py:132
  42.9 6.2 %collective-permute-start.10 = (bf16[4,4,16,1664]{3,2,1,0:T(8,128)(2,1)S(1)}, bf16[4,4,16,1664]{3,2,1,0:T(8,128)(2,1)S(1)}, u32[]{:S(2)}, u32[]{:S(2)}) collective-permute-start(bf16[4,4,16,1664]{3,2,1,0:T(8,128)(2,1)S(1)} %get-tuple-element.42), channel_id=1, source_target_pairs={{0,1},{1,0},{2,3},{3,2},{4,5},{5,4},{6,7},{7,6},{8,9},{9,8},{10,11... | collective-permute-start | bytes 2555912 | tf_op jit(solution)/shard_map/ppermute | solution.py:327
  49.0 2.5 %collective-permute-start.11 = (bf16[4,4,16,1664]{3,2,1,0:T(8,128)(2,1)S(1)}, bf16[4,4,16,1664]{3,2,1,0:T(8,128)(2,1)S(1)}, u32[]{:S(2)}, u32[]{:S(2)}) collective-permute-start(bf16[4,4,16,1664]{3,2,1,0:T(8,128)(2,1)S(1)} %get-tuple-element.43), channel_id=1, source_target_pairs={{0,1},{1,0},{2,3},{3,2},{4,5},{5,4},{6,7},{7,6},{8,9},{9,8},{10,11... | collective-permute-start | bytes 2555912 | tf_op jit(solution)/shard_map/ppermute | solution.py:327
  53.6 7.4 %copy-start.1 = (bf16[384,2304]{1,0:T(8,128)(2,1)S(1)}, bf16[384,2304]{1,0:T(8,128)(2,1)}, u32[]{:S(2)}) copy-start(bf16[384,2304]{1,0:T(8,128)(2,1)} %weights_ref.1) | copy-start | bytes 5308420
  53.6 32.0 %all-to-all-start.1 = ((bf16[16,32,1664]{2,1,0:T(8,128)(2,1)}), bf16[16,32,1664]{2,1,0:T(8,128)(2,1)S(1)}, u32[]{:S(2)}, u32[]{:S(2)}) async-start(bf16[16,32,1664]{2,1,0:T(8,128)(2,1)} %shard_map.99), calls=%async_computation.1 | async-start | bytes 3407872 | tf_op jit(solution)/shard_map/all_to_all | solution.py:329
  61.0 4.5 %copy-start.8 = (s32[2]{0:T(128)S(1)}, s32[2]{0:T(128)}, u32[]{:S(2)}) copy-start(s32[2]{0:T(128)} %param.15) | copy-start | bytes 28
  63.1 0.8 copy-start.2
  63.9 0.8 copy-start.4
  64.7 0.8 copy-start.6
  65.5 28.0 %copy-start.7 = (bf16[384,576]{1,0:T(8,128)(2,1)S(1)}, bf16[384,576]{1,0:T(8,128)(2,1)}, u32[]{:S(2)}) copy-start(bf16[384,576]{1,0:T(8,128)(2,1)} %copy-done.6) | copy-start | bytes 1327108
  65.6 31.5 %copy-start.5 = (bf16[384,576]{1,0:T(8,128)(2,1)S(1)}, bf16[384,576]{1,0:T(8,128)(2,1)}, u32[]{:S(2)}) copy-start(bf16[384,576]{1,0:T(8,128)(2,1)} %copy-done.4) | copy-start | bytes 1327108
  87.0 15.3 %all-to-all-start.2 = ((bf16[8,4,1664]{2,1,0:T(4,128)(2,1)}), bf16[8,4,1664]{2,1,0:T(4,128)(2,1)S(1)}, u32[]{:S(2)}, u32[]{:S(2)}) async-start(bf16[8,4,1664]{2,1,0:T(4,128)(2,1)} %reshape.97), calls=%async_computation.2 | async-start | bytes 212992 | tf_op jit(solution)/shard_map/all_to_all | solution.py:333
  93.5 24.7 %collective-permute-start.12 = (bf16[384,576]{1,0:T(8,128)(2,1)}, bf16[384,576]{1,0:T(8,128)(2,1)S(1)}, u32[]{:S(2)}, u32[]{:S(2)}) collective-permute-start(bf16[384,576]{1,0:T(8,128)(2,1)} %get-tuple-element.50), channel_id=1, source_target_pairs={{0,64},{64,128},{128,192},{192,0},{1,65},{65,129},{129,193},{193,1... | collective-permute-start | bytes 1327112 | tf_op jit(solution)/shard_map/ppermute | solution.py:132
  93.6 24.6 %collective-permute-start.13 = (bf16[384,576]{1,0:T(8,128)(2,1)S(1)}, bf16[384,576]{1,0:T(8,128)(2,1)S(1)}, u32[]{:S(2)}, u32[]{:S(2)}) collective-permute-start(bf16[384,576]{1,0:T(8,128)(2,1)S(1)} %copy-done.7), channel_id=1, source_target_pairs={{0,128},{64,192},{128,0},{192,64},{1,129},{65,193},{129,1},{193,65... | collective-permute-start | bytes 1327112 | tf_op jit(solution)/shard_map/ppermute | solution.py:132
  97.1 21.1 %collective-permute-start.14 = (bf16[384,576]{1,0:T(8,128)(2,1)S(1)}, bf16[384,576]{1,0:T(8,128)(2,1)S(1)}, u32[]{:S(2)}, u32[]{:S(2)}) collective-permute-start(bf16[384,576]{1,0:T(8,128)(2,1)S(1)} %copy-done.5), channel_id=1, source_target_pairs={{0,192},{64,0},{128,64},{192,128},{1,193},{65,1},{129,65},{193,129... | collective-permute-start | bytes 1327112 | tf_op jit(solution)/shard_map/ppermute | solution.py:132
  102.9 3.3 %copy-start.9 = (bf16[2,2048,512]{2,1,0:T(8,128)(2,1)S(1)}, bf16[2,2048,512]{2,1,0:T(8,128)(2,1)}, u32[]{:S(2)}) copy-start(bf16[2,2048,512]{2,1,0:T(8,128)(2,1)} %param.14) | copy-start | bytes 12582916
  118.4 28.9 %copy-start.3 = (bf16[384,576]{1,0:T(8,128)(2,1)S(1)}, bf16[384,576]{1,0:T(8,128)(2,1)}, u32[]{:S(2)}) copy-start(bf16[384,576]{1,0:T(8,128)(2,1)} %copy-done.2) | copy-start | bytes 1327108
  143.8 3.4 %collective-permute-start.15 = (bf16[16,32,1536]{2,1,0:T(8,128)(2,1)S(1)}, bf16[16,32,1536]{2,1,0:T(8,128)(2,1)S(1)}, u32[]{:S(2)}, u32[]{:S(2)}) collective-permute-start(bf16[16,32,1536]{2,1,0:T(8,128)(2,1)S(1)} %all_to_all.31.own_ref), channel_id=1, source_target_pairs={{0,1},{1,0},{2,3},{3,2},{4,5},{5,4},{6,7},{7,6},{8,9},{9,8},{10,11... | collective-permute-start | bytes 4718600 | tf_op jit(solution)/shard_map/ppermute | solution.py:349
  151.8 7.5 %collective-permute-start.16 = (bf16[128,576]{1,0:T(8,128)(2,1)S(1)}, bf16[128,576]{1,0:T(8,128)(2,1)S(1)}, u32[]{:S(2)}, u32[]{:S(2)}) collective-permute-start(bf16[128,576]{1,0:T(8,128)(2,1)S(1)} %get-tuple-element.62), channel_id=1, source_target_pairs={{0,8},{8,16},{16,24},{24,32},{32,40},{40,48},{48,56},{56,0},{1,9},... | collective-permute-start | bytes 442376 | tf_op jit(solution)/shard_map/ppermute | solution.py:132
  153.3 6.4 %collective-permute-start.20 = (bf16[128,576]{1,0:T(8,128)(2,1)S(1)}, bf16[128,576]{1,0:T(8,128)(2,1)S(1)}, u32[]{:S(2)}, u32[]{:S(2)}) collective-permute-start(bf16[128,576]{1,0:T(8,128)(2,1)S(1)} %get-tuple-element.65), channel_id=1, source_target_pairs={{0,56},{8,0},{16,8},{24,16},{32,24},{40,32},{48,40},{56,48},{1,57}... | collective-permute-start | bytes 442376 | tf_op jit(solution)/shard_map/ppermute | solution.py:132
  159.4 6.7 %collective-permute-start.17 = (bf16[128,576]{1,0:T(8,128)(2,1)S(1)}, bf16[128,576]{1,0:T(8,128)(2,1)S(1)}, u32[]{:S(2)}, u32[]{:S(2)}) collective-permute-start(bf16[128,576]{1,0:T(8,128)(2,1)S(1)} %add_convert_fusion.5), channel_id=1, source_target_pairs={{0,8},{8,16},{16,24},{24,32},{32,40},{40,48},{48,56},{56,0},{1,9},... | collective-permute-start | bytes 442376 | tf_op jit(solution)/shard_map/ppermute | solution.py:132
  159.7 6.5 %collective-permute-start.21 = (bf16[128,576]{1,0:T(8,128)(2,1)S(1)}, bf16[128,576]{1,0:T(8,128)(2,1)S(1)}, u32[]{:S(2)}, u32[]{:S(2)}) collective-permute-start(bf16[128,576]{1,0:T(8,128)(2,1)S(1)} %add_convert_fusion.2), channel_id=1, source_target_pairs={{0,56},{8,0},{16,8},{24,16},{32,24},{40,32},{48,40},{56,48},{1,57}... | collective-permute-start | bytes 442376 | tf_op jit(solution)/shard_map/ppermute | solution.py:132
  166.1 6.6 %collective-permute-start.18 = (bf16[128,576]{1,0:T(8,128)(2,1)S(1)}, bf16[128,576]{1,0:T(8,128)(2,1)S(1)}, u32[]{:S(2)}, u32[]{:S(2)}) collective-permute-start(bf16[128,576]{1,0:T(8,128)(2,1)S(1)} %add_convert_fusion.4), channel_id=1, source_target_pairs={{0,8},{8,16},{16,24},{24,32},{32,40},{40,48},{48,56},{56,0},{1,9},... | collective-permute-start | bytes 442376 | tf_op jit(solution)/shard_map/ppermute | solution.py:132
  166.3 6.6 %collective-permute-start.22 = (bf16[128,576]{1,0:T(8,128)(2,1)S(1)}, bf16[128,576]{1,0:T(8,128)(2,1)S(1)}, u32[]{:S(2)}, u32[]{:S(2)}) collective-permute-start(bf16[128,576]{1,0:T(8,128)(2,1)S(1)} %add_convert_fusion.1), channel_id=1, source_target_pairs={{0,56},{8,0},{16,8},{24,16},{32,24},{40,32},{48,40},{56,48},{1,57}... | collective-permute-start | bytes 442376 | tf_op jit(solution)/shard_map/ppermute | solution.py:132
  172.8 6.6 %collective-permute-start.19 = (bf16[128,576]{1,0:T(8,128)(2,1)S(1)}, bf16[128,576]{1,0:T(8,128)(2,1)S(1)}, u32[]{:S(2)}, u32[]{:S(2)}) collective-permute-start(bf16[128,576]{1,0:T(8,128)(2,1)S(1)} %add_convert_fusion.3), channel_id=1, source_target_pairs={{0,8},{8,16},{16,24},{24,32},{32,40},{40,48},{48,56},{56,0},{1,9},... | collective-permute-start | bytes 442376 | tf_op jit(solution)/shard_map/ppermute | solution.py:132

commit v5 on v4

--- a/solution.py
+++ b/solution.py
@@ -241,47 +241,59 @@
     return call(kernel, (place, terms), [jax.ShapeDtypeStruct(terms.shape[1:], BF16)], [])[0]
 
 
-def project_out(place, own, other, weights, nx, nc, seqs):
-    groups, count, width = own.shape
+def multiply_rows(place, gathered, weights):
+    groups, count, width = gathered.shape
     ny = len(weights)
     rows, depth = weights[0].shape
+
+    def kernel(place_ref, rows_ref, *refs):
+        weight_refs, out_ref = refs[:ny], refs[ny]
+        for k in range(ny):
+            at = pl.multiple_of(lax.rem(place_ref[0] + ny - k, ny) * rows, 128)
+            piece = rows_ref[:, :, pl.ds(at, rows)].reshape(groups * count, rows)
+            term = jnp.dot(piece, weight_refs[k][...], preferred_element_type=F32)
+            if k == 0:
+                out_ref[...] = term
+            else:
+                out_ref[...] += term
+
+    return call(
+        kernel,
+        (place, gathered, *weights),
+        [jax.ShapeDtypeStruct((groups * count, depth), F32)],
+        [],
+        flops=2 * groups * count * width * depth,
+    )[0]
+
+
+def arrange(place, own, other, nx, ny, nc, nz, seqs):
+    depth = own.shape[1]
     per = 2 * seqs
-    nz = count // per
     block = ny * 2 * nx * nc * seqs
 
     def kernel(place_ref, own_ref, other_ref, *refs):
-        weight_refs, refs = refs[:ny], refs[ny:]
-        out_refs, (sums, slots) = refs[:nz], refs[nz:]
-        here, core, depth_at = place_ref[0], place_ref[1], place_ref[2]
-        for c in range(nc):
-            for k in range(ny):
-                at = pl.ds(pl.multiple_of(lax.rem(here + ny - k, ny) * rows, 128), rows)
-                piece = jnp.where(core == c, own_ref[:, :, at], other_ref[:, :, at])
-                term = jnp.dot(
-                    piece.reshape(groups * count, rows),
-                    weight_refs[k][...],
-                    preferred_element_type=F32,
-                )
-                if k == 0:
-                    sums[...] = term
-                else:
-                    sums[...] += term
-            for x in range(nx):
-                for y in range(ny):
+        out_refs, slots = refs[:nz], refs[nz]
+        core, here = place_ref[1], place_ref[2]
+        for x in range(nx):
+            for y in range(ny):
+                at = (x * ny + y) * nz * per
+                one = own_ref[at : at + nz * per, :]
+                two = other_ref[at : at + nz * per, :]
+                for c in range(nc):
+                    rows = jnp.where(core == c, one, two)
                     for z in range(nz):
                         for t in range(2):
-                            at = (x * ny + y) * count + z * per + t * seqs
+                            start = z * per + t * seqs
                             to = ((y * 2 + t) * nx * nc + x * nc + c) * seqs
-                            slots[z, to : to + seqs, :] = sums[at : at + seqs, :]
+                            slots[z, to : to + seqs, :] = rows[start : start + seqs]
         for k in range(nz):
-            out_refs[k][...] = slots[lax.rem(depth_at + k, nz)].astype(BF16)
+            out_refs[k][...] = slots[lax.rem(here + k, nz)].astype(BF16)
 
     return call(
         kernel,
-        (place, own, other, *weights),
+        (place, own, other),
         [jax.ShapeDtypeStruct((block, depth), BF16)] * nz,
-        [pltpu.VMEM((groups * count, depth), F32), pltpu.VMEM((nz, block, depth), F32)],
-        flops=2 * nc * groups * count * width * depth,
+        [pltpu.VMEM((nz, block, depth), F32)],
     )
 
 
@@ -347,7 +359,9 @@
     copies = jnp.broadcast_to(returned, (nx * ny, *returned.shape))
     gathered = lax.all_to_all(copies, ("x", "y"), split_axis=0, concat_axis=0, tiled=True)
     other = lax.ppermute(gathered, "core", [(0, 1), (1, 0)])
-    parts = project_out(place, gathered, other, out_weights, nx, nc, seqs)
+    own = multiply_rows(place, gathered, out_weights)
+    other = multiply_rows(place, other, out_weights)
+    parts = arrange(place, own, other, nx, ny, nc, nz, seqs)
     out = ring_sum(parts, "z").reshape(ny, narrow * per, depth)
     out = lax.all_to_all(out, "y", split_axis=0, concat_axis=0, tiled=True)
     return tuple(join_columns(place, out))

time: 190 us -> 189 us (level)
    ppermute x1, waiting for transfers between devices: 3.41 us -> 1.17 us  [shards(): other = lax.ppermute(gathered, 'core', [(0, 1), (1, 0)])]
    pallas_call x9 -> x11, Pallas kernels: 20.7 us -> 20.9 us  [call(): pl.pallas_call(kernel, in_specs=[SMEM] + [VMEM] * (len(inputs) - 1), out_...]
  transfers between devices with their start and end apart: 26 -> 26, of which waited for: 14 -> 14; matrix products, arithmetic and copies ran while one was open for 3% -> 3% of each run, Pallas kernels for 5% -> 6%
where the time goes in v5:
time: 189 us; the launch traced here: 188 us
  waiting for transfers between devices  61.3 us (32%)
  starting transfers between devices  50.3 us (27%)
  blocking collectives  45.2 us (24%)
  Pallas kernels  20.9 us (11%)
  local copies, waits for them, and re-layouts  5.07 us (3%)
  matrix products  3.48 us (2%)
    ppermute x20, starting transfers between devices, shift(): lax.ppermute(value, axis, [(i, (i + by) % count) for i in range(count)])  30.6 us
    ppermute x20, waiting for transfers between devices, shift(): lax.ppermute(value, axis, [(i, (i + by) % count) for i in range(count)])  27 us
    all_to_all x1, blocking collectives, shards(): lax.all_to_all(copies, ('x', 'y'), split_axis=0, concat_axis=0, tiled=True)  25.3 us
    all_to_all x1, waiting for transfers between devices, shards(): lax.all_to_all(pair, ('x', 'y'), split_axis=0, concat_axis=0, tiled=True)  20.9 us
    pallas_call x11, Pallas kernels, call(): pl.pallas_call(kernel, in_specs=[SMEM] + [VMEM] * (len(inputs) - 1), out_...  20.9 us
    all_to_all x1, blocking collectives, shards(): lax.all_to_all(leaving, 'z', split_axis=0, concat_axis=0, tiled=True)  11.1 us
    all_to_all x1, blocking collectives, shards(): out = lax.all_to_all(out, 'y', split_axis=0, concat_axis=0, tiled=True)  8.71 us
    all_to_all x1, starting transfers between devices, shards(): lax.all_to_all(pair, ('x', 'y'), split_axis=0, concat_axis=0, tiled=True)  7.37 us
  transfers between devices with their start and end apart: 26, of which 14 were waited for; matrix products, arithmetic and copies ran while one was open for 3% of the time, Pallas kernels for 6%

profile of v5, /device:TPU:8, one launch (start us, length us, event | category | flops | bytes accessed | tf_op | source)
XLA Modules:
  0.0 188.1 jit_solution(5754468961589917751)
XLA Ops:
  0.6 2.6 %shard_map.95 = bf16[4,32,576]{2,1,0:T(8,128)(2,1)} custom-call(s32[1]{0:T(128)} %bitcast.4.start_ref, bf16[16,18432]{1,0:T(8,128)(2,1)} %one_ref.1, bf16[16,18432]{1,0:T(8,128)(2,1)} %two_ref.1, f32[1,18432]{1,0:T(1,128)} %bitcast.41), custom_call_target="tpu_custom_call" | custom-call | bytes 1400832 | tf_op jit(solution)/shard_map/pallas_call | solution.py:47
  3.3 5.5 %all-to-all-start = ((bf16[4,32,576]{2,1,0:T(8,128)(2,1)}), bf16[4,32,576]{2,1,0:T(8,128)(2,1)S(1)}, u32[]{:S(2)}, u32[]{:S(2)}) async-start(bf16[4,32,576]{2,1,0:T(8,128)(2,1)} %shard_map.95), calls=%async_computation | async-start | bytes 327680 | tf_op jit(solution)/shard_map/all_to_all | solution.py:327
  8.8 4.7 %all-to-all-done = bf16[4,32,576]{2,1,0:T(8,128)(2,1)S(1)} async-done(((bf16[4,32,576]{2,1,0:T(8,128)(2,1)}), bf16[4,32,576]{2,1,0:T(8,128)(2,1)S(1)}, u32[]{:S(2)}, u32[]{:S(2)}) %all-to-all-start) | async-done | bytes 147488 | tf_op jit(solution)/shard_map/all_to_all | solution.py:327
  13.5 1.3 collective-permute-start
  14.9 1.2 copy.30.keyval_ref
  16.1 0.9 shard_map.96
  17.1 3.4 %collective-permute-start.4 = (bf16[608,384]{1,0:T(8,128)(2,1)S(1)}, bf16[608,384]{1,0:T(8,128)(2,1)S(1)}, u32[]{:S(2)}, u32[]{:S(2)}) collective-permute-start(bf16[608,384]{1,0:T(8,128)(2,1)S(1)} %get-tuple-element.38), channel_id=1, source_target_pairs={{0,128},{64,192},{128,0},{192,64},{1,129},{65,193},{129,1},{193,65... | collective-permute-start | bytes 1400840 | tf_op jit(solution)/shard_map/ppermute | solution.py:132
  20.6 0.6 collective-permute-start.5
  21.1 3.9 %collective-permute-start.2 = (bf16[128,576]{1,0:T(8,128)(2,1)S(1)}, bf16[128,576]{1,0:T(8,128)(2,1)S(1)}, u32[]{:S(2)}, u32[]{:S(2)}) collective-permute-start(bf16[128,576]{1,0:T(8,128)(2,1)S(1)} %bitcast.31), channel_id=1, source_target_pairs={{0,56},{8,0},{16,8},{24,16},{32,24},{40,32},{48,40},{56,48},{1,57}... | collective-permute-start | bytes 442376 | tf_op jit(solution)/shard_map/ppermute | solution.py:132
  25.1 2.8 %collective-permute-done.2.refs_3_ = bf16[128,576]{1,0:T(8,128)(2,1)S(1)} collective-permute-done((bf16[128,576]{1,0:T(8,128)(2,1)S(1)}, bf16[128,576]{1,0:T(8,128)(2,1)S(1)}, u32[]{:S(2)}, u32[]{:S(2)}) %collective-permute-start.2) | collective-permute-done | bytes 147488 | tf_op jit(solution)/shard_map/ppermute | solution.py:132
  27.9 3.7 %collective-permute-start.6 = (bf16[128,576]{1,0:T(8,128)(2,1)S(1)}, bf16[128,576]{1,0:T(8,128)(2,1)S(1)}, u32[]{:S(2)}, u32[]{:S(2)}) collective-permute-start(bf16[128,576]{1,0:T(8,128)(2,1)S(1)} %collective-permute-done.2.refs_3_), channel_id=1, source_target_pairs={{0,56},{8,0},{16,8},{24,16},{32,24},{40,32},{48,40},{56,48},{1,57}... | collective-permute-start | bytes 442376 | tf_op jit(solution)/shard_map/ppermute | solution.py:132
  31.6 3.5 %collective-permute-done.6.refs_0_ = bf16[128,576]{1,0:T(8,128)(2,1)S(1)} collective-permute-done((bf16[128,576]{1,0:T(8,128)(2,1)S(1)}, bf16[128,576]{1,0:T(8,128)(2,1)S(1)}, u32[]{:S(2)}, u32[]{:S(2)}) %collective-permute-start.6) | collective-permute-done | bytes 147488 | tf_op jit(solution)/shard_map/ppermute | solution.py:132
  35.1 3.7 %collective-permute-start.7 = (bf16[128,576]{1,0:T(8,128)(2,1)S(1)}, bf16[128,576]{1,0:T(8,128)(2,1)S(1)}, u32[]{:S(2)}, u32[]{:S(2)}) collective-permute-start(bf16[128,576]{1,0:T(8,128)(2,1)S(1)} %collective-permute-done.6.refs_0_), channel_id=1, source_target_pairs={{0,56},{8,0},{16,8},{24,16},{32,24},{40,32},{48,40},{56,48},{1,57}... | collective-permute-start | bytes 442376 | tf_op jit(solution)/shard_map/ppermute | solution.py:132
  38.8 0.3 collective-permute-done.8.refs_3_
  39.4 3.1 %shard_map.97 = (bf16[4,4,16,1664]{3,2,1,0:T(8,128)(2,1)S(1)}, bf16[4,4,16,1664]{3,2,1,0:T(8,128)(2,1)S(1)}) custom-call(s32[4]{0:T(128)S(1)} %pad_add_fusion.place_ref, bf16[128,576]{1,0:T(8,128)(2,1)S(1)} %collective-permute-done.1.refs_0_, bf16[128,576]{1,0:T(8,128)(2,1)S(1)} %collective-permute-done.refs_1_, bf16[128,576]{1,0:T(8,128)(2,1)S(1)} %bitcast.32, ...), custom_call_target="tpu_custom_call" | custom-call | flops 981467136 | bytes 4161536 | tf_op jit(solution)/shard_map/pallas_call | solution.py:47
  42.7 2.9 %collective-permute-done.9.refs_2_ = bf16[128,576]{1,0:T(8,128)(2,1)S(1)} collective-permute-done((bf16[128,576]{1,0:T(8,128)(2,1)S(1)}, bf16[128,576]{1,0:T(8,128)(2,1)S(1)}, u32[]{:S(2)}, u32[]{:S(2)}) %collective-permute-start.9) | collective-permute-done | bytes 147488 | tf_op jit(solution)/shard_map/ppermute | solution.py:132
  45.6 3.0 %shard_map.98 = (bf16[4,4,16,1664]{3,2,1,0:T(8,128)(2,1)S(1)}, bf16[4,4,16,1664]{3,2,1,0:T(8,128)(2,1)S(1)}) custom-call(s32[4]{0:T(128)S(1)} %pad_add_fusion.place_ref, bf16[128,576]{1,0:T(8,128)(2,1)S(1)} %collective-permute-done.6.refs_0_, bf16[128,576]{1,0:T(8,128)(2,1)S(1)} %collective-permute-done.7.refs_1_, ...), custom_call_target="tpu_custom_call" | custom-call | flops 981467136 | bytes 4161536 | tf_op jit(solution)/shard_map/pallas_call | solution.py:47
  48.8 2.4 %collective-permute-done.11.refs_3_ = bf16[4,4,16,1664]{3,2,1,0:T(8,128)(2,1)S(1)} collective-permute-done((bf16[4,4,16,1664]{3,2,1,0:T(8,128)(2,1)S(1)}, bf16[4,4,16,1664]{3,2,1,0:T(8,128)(2,1)S(1)}, u32[]{:S(2)}, u32[]{:S(2)}) %collective-permute-start.11) | collective-permute-done | bytes 852000 | tf_op jit(solution)/shard_map/ppermute | solution.py:339
  51.1 2.2 %shard_map.99 = bf16[16,32,1664]{2,1,0:T(8,128)(2,1)} custom-call(s32[4]{0:T(128)S(1)} %pad_add_fusion.place_ref, bf16[4,4,16,1664]{3,2,1,0:T(8,128)(2,1)S(1)} %get-tuple-element.40.refs_0_, bf16[4,4,16,1664]{3,2,1,0:T(8,128)(2,1)S(1)} %get-tuple-element.41.refs_1_, bf16[4,4,16,1664]{3,2,1,0:T(8,128)(2,1)S(1)} %collective-permute-done.10.refs_2_, ...), custom_call_target="tpu_custom_call" | custom-call | bytes 5111808 | tf_op jit(solution)/shard_map/pallas_call | solution.py:47
  53.3 7.4 %all-to-all-start.1 = ((bf16[16,32,1664]{2,1,0:T(8,128)(2,1)}), bf16[16,32,1664]{2,1,0:T(8,128)(2,1)S(1)}, u32[]{:S(2)}, u32[]{:S(2)}) async-start(bf16[16,32,1664]{2,1,0:T(8,128)(2,1)} %shard_map.99), calls=%async_computation.1 | async-start | bytes 3407872 | tf_op jit(solution)/shard_map/all_to_all | solution.py:341
  60.7 1.5 copy-done.1
  62.1 1.2 shard_map.101
  63.4 0.8 copy-done.2
  64.3 20.9 %all-to-all-done.1.terms_ref = bf16[16,32,1664]{2,1,0:T(8,128)(2,1)S(1)} async-done(((bf16[16,32,1664]{2,1,0:T(8,128)(2,1)}), bf16[16,32,1664]{2,1,0:T(8,128)(2,1)S(1)}, u32[]{:S(2)}, u32[]{:S(2)}) %all-to-all-start.1) | async-done | bytes 1703968 | tf_op jit(solution)/shard_map/all_to_all | solution.py:341
  85.3 0.8 shard_map.100
  86.1 0.7 reshape.97
  86.7 6.4 %all-to-all-start.2 = ((bf16[8,4,1664]{2,1,0:T(4,128)(2,1)}), bf16[8,4,1664]{2,1,0:T(4,128)(2,1)S(1)}, u32[]{:S(2)}, u32[]{:S(2)}) async-start(bf16[8,4,1664]{2,1,0:T(4,128)(2,1)} %reshape.97), calls=%async_computation.2 | async-start | bytes 212992 | tf_op jit(solution)/shard_map/all_to_all | solution.py:345
  93.3 3.5 %collective-permute-start.13 = (bf16[384,576]{1,0:T(8,128)(2,1)S(1)}, bf16[384,576]{1,0:T(8,128)(2,1)S(1)}, u32[]{:S(2)}, u32[]{:S(2)}) collective-permute-start(bf16[384,576]{1,0:T(8,128)(2,1)S(1)} %get-tuple-element.51), channel_id=1, source_target_pairs={{0,128},{64,192},{128,0},{192,64},{1,129},{65,193},{129,1},{193,65... | collective-permute-start | bytes 1327112 | tf_op jit(solution)/shard_map/ppermute | solution.py:132
  96.8 5.2 %all-to-all-done.2 = bf16[8,4,1664]{2,1,0:T(4,128)(2,1)S(1)} async-done(((bf16[8,4,1664]{2,1,0:T(4,128)(2,1)}), bf16[8,4,1664]{2,1,0:T(4,128)(2,1)S(1)}, u32[]{:S(2)}, u32[]{:S(2)}) %all-to-all-start.2) | async-done | bytes 106528 | tf_op jit(solution)/shard_map/all_to_all | solution.py:345
  102.5 2.6 %fusion.26 = (f32[2,96]{1,0:T(2,128)S(1)}, f32[2,96,2048]{2,1,0:T(8,128)S(1)}) fusion(bf16[2,96,256]{2,1,0:T(8,128)(2,1)S(1)} %bitcast.34, bf16[2,2048,512]{2,1,0:T(8,128)(2,1)} %param.14, pred[2,2048]{1,0:T(4,128)(4,1)S(1)} %iota_compare_fusion), kind=kOutput, calls=%fused_computation.34 | convolution fusion | flops 202506048 | bytes 3773184 | tf_op jit(solution)/shard_map/srd,smd->srm/dot_general | solution.py:25
  105.5 0.4 fusion.4
  105.9 0.5 fusion.12
  106.7 11.1 %all_to_all.30 = bf16[8,4,1536]{2,1,0:T(4,128)(2,1)S(1)} all-to-all(bf16[8,4,1536]{2,1,0:T(4,128)(2,1)S(1)} %copy.38), channel_id=1, replica_groups=mesh['y'=4,'z'=8,'x'=4,'core'=2] {'z'}, dimensions={0} | all-to-all | bytes 196608 | tf_op jit(solution)/shard_map/all_to_all | solution.py:356
  118.1 25.3 %all_to_all.31.rows_ref = bf16[16,32,1536]{2,1,0:T(8,128)(2,1)S(1)} all-to-all(bf16[16,32,1536]{2,1,0:T(8,128)(2,1)S(1)} %broadcast_in_dim.60), channel_id=1, replica_groups=mesh['y'=4,'z'=8,'x'=4,'core'=2] {'x','y'}, dimensions={0} | all-to-all | bytes 3145728 | tf_op jit(solution)/shard_map/all_to_all | solution.py:360
  143.4 2.2 %shard_map.102.own_ref = f32[512,576]{1,0:T(8,128)S(1)} custom-call(s32[4]{0:T(128)S(1)} %pad_add_fusion.place_ref, bf16[16,32,1536]{2,1,0:T(8,128)(2,1)S(1)} %all_to_all.31.rows_ref, bf16[384,576]{1,0:T(8,128)(2,1)S(1)} %get-tuple-element.54.refs_0_, bf16[384,576]{1,0:T(8,128)(2,1)S(1)} %collective-permute-done.12.refs_1_, ...), custom_call_target="tpu_custom_call" | custom-call | flops 905969664 | bytes 4521984 | tf_op jit(solution)/shard_map/pallas_call | solution.py:47
  145.6 1.2 collective-permute-done.15.rows_ref
  146.8 2.2 %shard_map.103.other_ref = f32[512,576]{1,0:T(8,128)S(1)} custom-call(s32[4]{0:T(128)S(1)} %pad_add_fusion.place_ref, bf16[16,32,1536]{2,1,0:T(8,128)(2,1)S(1)} %collective-permute-done.15.rows_ref, bf16[384,576]{1,0:T(8,128)(2,1)S(1)} %get-tuple-element.54.refs_0_, bf16[384,576]{1,0:T(8,128)(2,1)S(1)} %collective-permute-done.12.refs_1_, ...), custom_call_target="tpu_custom_call" | custom-call | flops 905969664 | bytes 4521984 | tf_op jit(solution)/shard_map/pallas_call | solution.py:47
  149.1 1.4 shard_map.104
  150.5 1.5 collective-permute-start.16
  151.9 1.8 collective-permute-start.20
  153.8 4.2 %collective-permute-done.16 = bf16[128,576]{1,0:T(8,128)(2,1)S(1)} collective-permute-done((bf16[128,576]{1,0:T(8,128)(2,1)S(1)}, bf16[128,576]{1,0:T(8,128)(2,1)S(1)}, u32[]{:S(2)}, u32[]{:S(2)}) %collective-permute-start.16) | collective-permute-done | bytes 147488 | tf_op jit(solution)/shard_map/ppermute | solution.py:132
  158.4 3.1 %collective-permute-start.21 = (bf16[128,576]{1,0:T(8,128)(2,1)S(1)}, bf16[128,576]{1,0:T(8,128)(2,1)S(1)}, u32[]{:S(2)}, u32[]{:S(2)}) collective-permute-start(bf16[128,576]{1,0:T(8,128)(2,1)S(1)} %add_convert_fusion.2), channel_id=1, source_target_pairs={{0,56},{8,0},{16,8},{24,16},{32,24},{40,32},{48,40},{56,48},{1,57}... | collective-permute-start | bytes 442376 | tf_op jit(solution)/shard_map/ppermute | solution.py:132
  161.5 3.3 %collective-permute-done.17 = bf16[128,576]{1,0:T(8,128)(2,1)S(1)} collective-permute-done((bf16[128,576]{1,0:T(8,128)(2,1)S(1)}, bf16[128,576]{1,0:T(8,128)(2,1)S(1)}, u32[]{:S(2)}, u32[]{:S(2)}) %collective-permute-start.17) | collective-permute-done | bytes 147488 | tf_op jit(solution)/shard_map/ppermute | solution.py:132
  164.9 3.3 %collective-permute-start.22 = (bf16[128,576]{1,0:T(8,128)(2,1)S(1)}, bf16[128,576]{1,0:T(8,128)(2,1)S(1)}, u32[]{:S(2)}, u32[]{:S(2)}) collective-permute-start(bf16[128,576]{1,0:T(8,128)(2,1)S(1)} %add_convert_fusion.1), channel_id=1, source_target_pairs={{0,56},{8,0},{16,8},{24,16},{32,24},{40,32},{48,40},{56,48},{1,57}... | collective-permute-start | bytes 442376 | tf_op jit(solution)/shard_map/ppermute | solution.py:132
  168.2 3.2 %collective-permute-done.18 = bf16[128,576]{1,0:T(8,128)(2,1)S(1)} collective-permute-done((bf16[128,576]{1,0:T(8,128)(2,1)S(1)}, bf16[128,576]{1,0:T(8,128)(2,1)S(1)}, u32[]{:S(2)}, u32[]{:S(2)}) %collective-permute-start.18) | collective-permute-done | bytes 147488 | tf_op jit(solution)/shard_map/ppermute | solution.py:132
  171.6 6.5 %collective-permute-done.19 = bf16[128,576]{1,0:T(8,128)(2,1)S(1)} collective-permute-done((bf16[128,576]{1,0:T(8,128)(2,1)S(1)}, bf16[128,576]{1,0:T(8,128)(2,1)S(1)}, u32[]{:S(2)}, u32[]{:S(2)}) %collective-permute-start.19) | collective-permute-done | bytes 147488 | tf_op jit(solution)/shard_map/ppermute | solution.py:132
  178.1 8.7 %all_to_all.32.blocks_ref = bf16[4,32,576]{2,1,0:T(8,128)(2,1)S(1)} all-to-all(bf16[4,32,576]{2,1,0:T(8,128)(2,1)S(1)} %bitcast.33), channel_id=1, replica_groups=mesh['y'=4,'z'=8,'x'=4,'core'=2] {'y'}, dimensions={0} | all-to-all | bytes 294912 | tf_op jit(solution)/shard_map/all_to_all | solution.py:366
  186.8 1.3 shard_map.105
  (66 shorter events, 3.2 us)
Async XLA Ops:
  0.6 15.4 %copy-start = (bf16[2304,384]{1,0:T(8,128)(2,1)S(1)}, bf16[2304,384]{1,0:T(8,128)(2,1)}, u32[]{:S(2)}) copy-start(bf16[2304,384]{1,0:T(8,128)(2,1)} %query_ref) | copy-start | bytes 5308420
  3.3 10.2 %all-to-all-start = ((bf16[4,32,576]{2,1,0:T(8,128)(2,1)}), bf16[4,32,576]{2,1,0:T(8,128)(2,1)S(1)}, u32[]{:S(2)}, u32[]{:S(2)}) async-start(bf16[4,32,576]{2,1,0:T(8,128)(2,1)} %shard_map.95), calls=%async_computation | async-start | bytes 327680 | tf_op jit(solution)/shard_map/all_to_all | solution.py:327
  13.5 11.6 %collective-permute-start = (bf16[128,576]{1,0:T(8,128)(2,1)S(1)}, bf16[128,576]{1,0:T(8,128)(2,1)S(1)}, u32[]{:S(2)}, u32[]{:S(2)}) collective-permute-start(bf16[128,576]{1,0:T(8,128)(2,1)S(1)} %bitcast.30), channel_id=1, source_target_pairs={{0,8},{8,16},{16,24},{24,32},{32,40},{40,48},{48,56},{56,0},{1,9},... | collective-permute-start | bytes 442376 | tf_op jit(solution)/shard_map/ppermute | solution.py:132
  16.9 22.1 %collective-permute-start.3 = (bf16[608,384]{1,0:T(8,128)(2,1)S(1)}, bf16[608,384]{1,0:T(8,128)(2,1)S(1)}, u32[]{:S(2)}, u32[]{:S(2)}) collective-permute-start(bf16[608,384]{1,0:T(8,128)(2,1)S(1)} %get-tuple-element.37), channel_id=1, source_target_pairs={{0,64},{64,128},{128,192},{192,0},{1,65},{65,129},{129,193},{193,1... | collective-permute-start | bytes 1400840 | tf_op jit(solution)/shard_map/ppermute | solution.py:132
  17.1 21.9 %collective-permute-start.4 = (bf16[608,384]{1,0:T(8,128)(2,1)S(1)}, bf16[608,384]{1,0:T(8,128)(2,1)S(1)}, u32[]{:S(2)}, u32[]{:S(2)}) collective-permute-start(bf16[608,384]{1,0:T(8,128)(2,1)S(1)} %get-tuple-element.38), channel_id=1, source_target_pairs={{0,128},{64,192},{128,0},{192,64},{1,129},{65,193},{129,1},{193,65... | collective-permute-start | bytes 1400840 | tf_op jit(solution)/shard_map/ppermute | solution.py:132
  20.6 18.8 %collective-permute-start.5 = (bf16[608,384]{1,0:T(8,128)(2,1)S(1)}, bf16[608,384]{1,0:T(8,128)(2,1)S(1)}, u32[]{:S(2)}, u32[]{:S(2)}) collective-permute-start(bf16[608,384]{1,0:T(8,128)(2,1)S(1)} %get-tuple-element.39), channel_id=1, source_target_pairs={{0,192},{64,0},{128,64},{192,128},{1,193},{65,1},{129,65},{193,129... | collective-permute-start | bytes 1400840 | tf_op jit(solution)/shard_map/ppermute | solution.py:132
  21.1 6.8 %collective-permute-start.2 = (bf16[128,576]{1,0:T(8,128)(2,1)S(1)}, bf16[128,576]{1,0:T(8,128)(2,1)S(1)}, u32[]{:S(2)}, u32[]{:S(2)}) collective-permute-start(bf16[128,576]{1,0:T(8,128)(2,1)S(1)} %bitcast.31), channel_id=1, source_target_pairs={{0,56},{8,0},{16,8},{24,16},{32,24},{40,32},{48,40},{56,48},{1,57}... | collective-permute-start | bytes 442376 | tf_op jit(solution)/shard_map/ppermute | solution.py:132
  25.1 6.5 %collective-permute-start.1 = (bf16[128,576]{1,0:T(8,128)(2,1)S(1)}, bf16[128,576]{1,0:T(8,128)(2,1)S(1)}, u32[]{:S(2)}, u32[]{:S(2)}) collective-permute-start(bf16[128,576]{1,0:T(8,128)(2,1)S(1)} %collective-permute-done.refs_1_), channel_id=1, source_target_pairs={{0,8},{8,16},{16,24},{24,32},{32,40},{40,48},{48,56},{56,0},{1,9},... | collective-permute-start | bytes 442376 | tf_op jit(solution)/shard_map/ppermute | solution.py:132
  27.9 7.2 %collective-permute-start.6 = (bf16[128,576]{1,0:T(8,128)(2,1)S(1)}, bf16[128,576]{1,0:T(8,128)(2,1)S(1)}, u32[]{:S(2)}, u32[]{:S(2)}) collective-permute-start(bf16[128,576]{1,0:T(8,128)(2,1)S(1)} %collective-permute-done.2.refs_3_), channel_id=1, source_target_pairs={{0,56},{8,0},{16,8},{24,16},{32,24},{40,32},{48,40},{56,48},{1,57}... | collective-permute-start | bytes 442376 | tf_op jit(solution)/shard_map/ppermute | solution.py:132
  31.6 7.5 %collective-permute-start.8 = (bf16[128,576]{1,0:T(8,128)(2,1)S(1)}, bf16[128,576]{1,0:T(8,128)(2,1)S(1)}, u32[]{:S(2)}, u32[]{:S(2)}) collective-permute-start(bf16[128,576]{1,0:T(8,128)(2,1)S(1)} %collective-permute-done.1.refs_0_), channel_id=1, source_target_pairs={{0,8},{8,16},{16,24},{24,32},{32,40},{40,48},{48,56},{56,0},{1,9},... | collective-permute-start | bytes 442376 | tf_op jit(solution)/shard_map/ppermute | solution.py:132
  35.1 7.6 %collective-permute-start.7 = (bf16[128,576]{1,0:T(8,128)(2,1)S(1)}, bf16[128,576]{1,0:T(8,128)(2,1)S(1)}, u32[]{:S(2)}, u32[]{:S(2)}) collective-permute-start(bf16[128,576]{1,0:T(8,128)(2,1)S(1)} %collective-permute-done.6.refs_0_), channel_id=1, source_target_pairs={{0,56},{8,0},{16,8},{24,16},{32,24},{40,32},{48,40},{56,48},{1,57}... | collective-permute-start | bytes 442376 | tf_op jit(solution)/shard_map/ppermute | solution.py:132
  39.1 6.5 %collective-permute-start.9 = (bf16[128,576]{1,0:T(8,128)(2,1)S(1)}, bf16[128,576]{1,0:T(8,128)(2,1)S(1)}, u32[]{:S(2)}, u32[]{:S(2)}) collective-permute-start(bf16[128,576]{1,0:T(8,128)(2,1)S(1)} %collective-permute-done.8.refs_3_), channel_id=1, source_target_pairs={{0,8},{8,16},{16,24},{24,32},{32,40},{40,48},{48,56},{56,0},{1,9},... | collective-permute-start | bytes 442376 | tf_op jit(solution)/shard_map/ppermute | solution.py:132
  42.4 6.3 %collective-permute-start.10 = (bf16[4,4,16,1664]{3,2,1,0:T(8,128)(2,1)S(1)}, bf16[4,4,16,1664]{3,2,1,0:T(8,128)(2,1)S(1)}, u32[]{:S(2)}, u32[]{:S(2)}) collective-permute-start(bf16[4,4,16,1664]{3,2,1,0:T(8,128)(2,1)S(1)} %get-tuple-element.42), channel_id=1, source_target_pairs={{0,1},{1,0},{2,3},{3,2},{4,5},{5,4},{6,7},{7,6},{8,9},{9,8},{10,11... | collective-permute-start | bytes 2555912 | tf_op jit(solution)/shard_map/ppermute | solution.py:339
  48.6 2.5 %collective-permute-start.11 = (bf16[4,4,16,1664]{3,2,1,0:T(8,128)(2,1)S(1)}, bf16[4,4,16,1664]{3,2,1,0:T(8,128)(2,1)S(1)}, u32[]{:S(2)}, u32[]{:S(2)}) collective-permute-start(bf16[4,4,16,1664]{3,2,1,0:T(8,128)(2,1)S(1)} %get-tuple-element.43), channel_id=1, source_target_pairs={{0,1},{1,0},{2,3},{3,2},{4,5},{5,4},{6,7},{7,6},{8,9},{9,8},{10,11... | collective-permute-start | bytes 2555912 | tf_op jit(solution)/shard_map/ppermute | solution.py:339
  53.3 32.0 %all-to-all-start.1 = ((bf16[16,32,1664]{2,1,0:T(8,128)(2,1)}), bf16[16,32,1664]{2,1,0:T(8,128)(2,1)S(1)}, u32[]{:S(2)}, u32[]{:S(2)}) async-start(bf16[16,32,1664]{2,1,0:T(8,128)(2,1)} %shard_map.99), calls=%async_computation.1 | async-start | bytes 3407872 | tf_op jit(solution)/shard_map/all_to_all | solution.py:341
  60.7 1.5 copy-start.1
  62.1 2.1 %copy-start.3 = (s32[2]{0:T(128)S(1)}, s32[2]{0:T(128)}, u32[]{:S(2)}) copy-start(s32[2]{0:T(128)} %param.15) | copy-start | bytes 28
  63.4 0.8 copy-start.2
  86.7 15.3 %all-to-all-start.2 = ((bf16[8,4,1664]{2,1,0:T(4,128)(2,1)}), bf16[8,4,1664]{2,1,0:T(4,128)(2,1)S(1)}, u32[]{:S(2)}, u32[]{:S(2)}) async-start(bf16[8,4,1664]{2,1,0:T(4,128)(2,1)} %reshape.97), calls=%async_computation.2 | async-start | bytes 212992 | tf_op jit(solution)/shard_map/all_to_all | solution.py:345
  93.2 24.7 %collective-permute-start.12 = (bf16[384,576]{1,0:T(8,128)(2,1)}, bf16[384,576]{1,0:T(8,128)(2,1)S(1)}, u32[]{:S(2)}, u32[]{:S(2)}) collective-permute-start(bf16[384,576]{1,0:T(8,128)(2,1)} %copy-done.2), channel_id=1, source_target_pairs={{0,64},{64,128},{128,192},{192,0},{1,65},{65,129},{129,193},{193,1... | collective-permute-start | bytes 1327112 | tf_op jit(solution)/shard_map/ppermute | solution.py:132
  93.3 24.6 %collective-permute-start.13 = (bf16[384,576]{1,0:T(8,128)(2,1)S(1)}, bf16[384,576]{1,0:T(8,128)(2,1)S(1)}, u32[]{:S(2)}, u32[]{:S(2)}) collective-permute-start(bf16[384,576]{1,0:T(8,128)(2,1)S(1)} %get-tuple-element.51), channel_id=1, source_target_pairs={{0,128},{64,192},{128,0},{192,64},{1,129},{65,193},{129,1},{193,65... | collective-permute-start | bytes 1327112 | tf_op jit(solution)/shard_map/ppermute | solution.py:132
  96.8 21.1 %collective-permute-start.14 = (bf16[384,576]{1,0:T(8,128)(2,1)S(1)}, bf16[384,576]{1,0:T(8,128)(2,1)S(1)}, u32[]{:S(2)}, u32[]{:S(2)}) collective-permute-start(bf16[384,576]{1,0:T(8,128)(2,1)S(1)} %get-tuple-element.52), channel_id=1, source_target_pairs={{0,192},{64,0},{128,64},{192,128},{1,193},{65,1},{129,65},{193,129... | collective-permute-start | bytes 1327112 | tf_op jit(solution)/shard_map/ppermute | solution.py:132
  102.4 3.5 %copy-start.4 = (bf16[2,2048,512]{2,1,0:T(8,128)(2,1)S(1)}, bf16[2,2048,512]{2,1,0:T(8,128)(2,1)}, u32[]{:S(2)}) copy-start(bf16[2,2048,512]{2,1,0:T(8,128)(2,1)} %param.14) | copy-start | bytes 12582916
  143.4 3.4 %collective-permute-start.15 = (bf16[16,32,1536]{2,1,0:T(8,128)(2,1)S(1)}, bf16[16,32,1536]{2,1,0:T(8,128)(2,1)S(1)}, u32[]{:S(2)}, u32[]{:S(2)}) collective-permute-start(bf16[16,32,1536]{2,1,0:T(8,128)(2,1)S(1)} %all_to_all.31.rows_ref), channel_id=1, source_target_pairs={{0,1},{1,0},{2,3},{3,2},{4,5},{5,4},{6,7},{7,6},{8,9},{9,8},{10,11... | collective-permute-start | bytes 4718600 | tf_op jit(solution)/shard_map/ppermute | solution.py:361
  150.5 7.5 %collective-permute-start.16 = (bf16[128,576]{1,0:T(8,128)(2,1)S(1)}, bf16[128,576]{1,0:T(8,128)(2,1)S(1)}, u32[]{:S(2)}, u32[]{:S(2)}) collective-permute-start(bf16[128,576]{1,0:T(8,128)(2,1)S(1)} %get-tuple-element.62), channel_id=1, source_target_pairs={{0,8},{8,16},{16,24},{24,32},{32,40},{40,48},{48,56},{56,0},{1,9},... | collective-permute-start | bytes 442376 | tf_op jit(solution)/shard_map/ppermute | solution.py:132
  151.9 6.4 %collective-permute-start.20 = (bf16[128,576]{1,0:T(8,128)(2,1)S(1)}, bf16[128,576]{1,0:T(8,128)(2,1)S(1)}, u32[]{:S(2)}, u32[]{:S(2)}) collective-permute-start(bf16[128,576]{1,0:T(8,128)(2,1)S(1)} %get-tuple-element.65), channel_id=1, source_target_pairs={{0,56},{8,0},{16,8},{24,16},{32,24},{40,32},{48,40},{56,48},{1,57}... | collective-permute-start | bytes 442376 | tf_op jit(solution)/shard_map/ppermute | solution.py:132
  158.1 6.7 %collective-permute-start.17 = (bf16[128,576]{1,0:T(8,128)(2,1)S(1)}, bf16[128,576]{1,0:T(8,128)(2,1)S(1)}, u32[]{:S(2)}, u32[]{:S(2)}) collective-permute-start(bf16[128,576]{1,0:T(8,128)(2,1)S(1)} %add_convert_fusion.5), channel_id=1, source_target_pairs={{0,8},{8,16},{16,24},{24,32},{32,40},{40,48},{48,56},{56,0},{1,9},... | collective-permute-start | bytes 442376 | tf_op jit(solution)/shard_map/ppermute | solution.py:132
  158.4 6.5 %collective-permute-start.21 = (bf16[128,576]{1,0:T(8,128)(2,1)S(1)}, bf16[128,576]{1,0:T(8,128)(2,1)S(1)}, u32[]{:S(2)}, u32[]{:S(2)}) collective-permute-start(bf16[128,576]{1,0:T(8,128)(2,1)S(1)} %add_convert_fusion.2), channel_id=1, source_target_pairs={{0,56},{8,0},{16,8},{24,16},{32,24},{40,32},{48,40},{56,48},{1,57}... | collective-permute-start | bytes 442376 | tf_op jit(solution)/shard_map/ppermute | solution.py:132
  164.8 6.6 %collective-permute-start.18 = (bf16[128,576]{1,0:T(8,128)(2,1)S(1)}, bf16[128,576]{1,0:T(8,128)(2,1)S(1)}, u32[]{:S(2)}, u32[]{:S(2)}) collective-permute-start(bf16[128,576]{1,0:T(8,128)(2,1)S(1)} %add_convert_fusion.4), channel_id=1, source_target_pairs={{0,8},{8,16},{16,24},{24,32},{32,40},{40,48},{48,56},{56,0},{1,9},... | collective-permute-start | bytes 442376 | tf_op jit(solution)/shard_map/ppermute | solution.py:132
  164.9 6.6 %collective-permute-start.22 = (bf16[128,576]{1,0:T(8,128)(2,1)S(1)}, bf16[128,576]{1,0:T(8,128)(2,1)S(1)}, u32[]{:S(2)}, u32[]{:S(2)}) collective-permute-start(bf16[128,576]{1,0:T(8,128)(2,1)S(1)} %add_convert_fusion.1), channel_id=1, source_target_pairs={{0,56},{8,0},{16,8},{24,16},{32,24},{40,32},{48,40},{56,48},{1,57}... | collective-permute-start | bytes 442376 | tf_op jit(solution)/shard_map/ppermute | solution.py:132
  171.5 6.6 %collective-permute-start.19 = (bf16[128,576]{1,0:T(8,128)(2,1)S(1)}, bf16[128,576]{1,0:T(8,128)(2,1)S(1)}, u32[]{:S(2)}, u32[]{:S(2)}) collective-permute-start(bf16[128,576]{1,0:T(8,128)(2,1)S(1)} %add_convert_fusion.3), channel_id=1, source_target_pairs={{0,8},{8,16},{16,24},{24,32},{32,40},{40,48},{48,56},{56,0},{1,9},... | collective-permute-start | bytes 442376 | tf_op jit(solution)/shard_map/ppermute | solution.py:132

commit v6 on v5

--- a/solution.py
+++ b/solution.py
@@ -324,8 +324,8 @@
 
     start = ((places[3] * nc + places[1]) * width).astype(jnp.int32).reshape(1)
     mine = normalize(start, (step_one, step_two), gain, nx, nc, ny, width)
+    w_query, mine = lax.optimization_barrier((w_query, mine))
     column = lax.all_to_all(mine, "y", split_axis=0, concat_axis=0, tiled=True)
-    w_query, column = lax.optimization_barrier((w_query, column))
     quarters = input_quarters(place, w_query, w_keyval, ny)
     weights = [quarters[0]] + [shift(quarters[k], "y", k) for k in range(1, ny)]
     pieces = ring_pieces(column.reshape(ny * narrow * per, depth), "z")

time: 189 us -> 189 us (level)
  no operation moved by 1% of the time
where the time goes in v6:
time: 189 us; the launch traced here: 188 us
  waiting for transfers between devices  61.3 us (32%)
  starting transfers between devices  50.3 us (27%)
  blocking collectives  45.2 us (24%)
  Pallas kernels  20.9 us (11%)
  local copies, waits for them, and re-layouts  5.07 us (3%)
  matrix products  3.48 us (2%)
    ppermute x20, starting transfers between devices, shift(): lax.ppermute(value, axis, [(i, (i + by) % count) for i in range(count)])  30.6 us
    ppermute x20, waiting for transfers between devices, shift(): lax.ppermute(value, axis, [(i, (i + by) % count) for i in range(count)])  27 us
    all_to_all x1, blocking collectives, shards(): lax.all_to_all(copies, ('x', 'y'), split_axis=0, concat_axis=0, tiled=True)  25.3 us
    all_to_all x1, waiting for transfers between devices, shards(): lax.all_to_all(pair, ('x', 'y'), split_axis=0, concat_axis=0, tiled=True)  20.9 us
    pallas_call x11, Pallas kernels, call(): pl.pallas_call(kernel, in_specs=[SMEM] + [VMEM] * (len(inputs) - 1), out_...  20.9 us
    all_to_all x1, blocking collectives, shards(): lax.all_to_all(leaving, 'z', split_axis=0, concat_axis=0, tiled=True)  11.1 us
    all_to_all x1, blocking collectives, shards(): out = lax.all_to_all(out, 'y', split_axis=0, concat_axis=0, tiled=True)  8.71 us
    all_to_all x1, starting transfers between devices, shards(): lax.all_to_all(pair, ('x', 'y'), split_axis=0, concat_axis=0, tiled=True)  7.37 us
  transfers between devices with their start and end apart: 26, of which 14 were waited for; matrix products, arithmetic and copies ran while one was open for 3% of the time, Pallas kernels for 6%

profile of v6, /device:TPU:8, one launch (start us, length us, event | category | flops | bytes accessed | tf_op | source)
XLA Modules:
  0.0 188.1 jit_solution(5754468961589917751)
XLA Ops:
  0.6 2.6 %shard_map.95 = bf16[4,32,576]{2,1,0:T(8,128)(2,1)} custom-call(s32[1]{0:T(128)} %bitcast.4.start_ref, bf16[16,18432]{1,0:T(8,128)(2,1)} %one_ref.1, bf16[16,18432]{1,0:T(8,128)(2,1)} %two_ref.1, f32[1,18432]{1,0:T(1,128)} %bitcast.41), custom_call_target="tpu_custom_call" | custom-call | bytes 1400832 | tf_op jit(solution)/shard_map/pallas_call | solution.py:47
  3.3 5.5 %all-to-all-start = ((bf16[4,32,576]{2,1,0:T(8,128)(2,1)}), bf16[4,32,576]{2,1,0:T(8,128)(2,1)S(1)}, u32[]{:S(2)}, u32[]{:S(2)}) async-start(bf16[4,32,576]{2,1,0:T(8,128)(2,1)} %shard_map.95), calls=%async_computation | async-start | bytes 327680 | tf_op jit(solution)/shard_map/all_to_all | solution.py:328
  8.8 4.7 %all-to-all-done = bf16[4,32,576]{2,1,0:T(8,128)(2,1)S(1)} async-done(((bf16[4,32,576]{2,1,0:T(8,128)(2,1)}), bf16[4,32,576]{2,1,0:T(8,128)(2,1)S(1)}, u32[]{:S(2)}, u32[]{:S(2)}) %all-to-all-start) | async-done | bytes 147488 | tf_op jit(solution)/shard_map/all_to_all | solution.py:328
  13.5 1.3 collective-permute-start
  14.9 1.2 copy.30.keyval_ref
  16.1 0.9 shard_map.96
  17.1 3.4 %collective-permute-start.4 = (bf16[608,384]{1,0:T(8,128)(2,1)S(1)}, bf16[608,384]{1,0:T(8,128)(2,1)S(1)}, u32[]{:S(2)}, u32[]{:S(2)}) collective-permute-start(bf16[608,384]{1,0:T(8,128)(2,1)S(1)} %get-tuple-element.38), channel_id=1, source_target_pairs={{0,128},{64,192},{128,0},{192,64},{1,129},{65,193},{129,1},{193,65... | collective-permute-start | bytes 1400840 | tf_op jit(solution)/shard_map/ppermute | solution.py:132
  20.6 0.6 collective-permute-start.5
  21.1 3.9 %collective-permute-start.2 = (bf16[128,576]{1,0:T(8,128)(2,1)S(1)}, bf16[128,576]{1,0:T(8,128)(2,1)S(1)}, u32[]{:S(2)}, u32[]{:S(2)}) collective-permute-start(bf16[128,576]{1,0:T(8,128)(2,1)S(1)} %bitcast.31), channel_id=1, source_target_pairs={{0,56},{8,0},{16,8},{24,16},{32,24},{40,32},{48,40},{56,48},{1,57}... | collective-permute-start | bytes 442376 | tf_op jit(solution)/shard_map/ppermute | solution.py:132
  25.1 2.8 %collective-permute-done.2.refs_3_ = bf16[128,576]{1,0:T(8,128)(2,1)S(1)} collective-permute-done((bf16[128,576]{1,0:T(8,128)(2,1)S(1)}, bf16[128,576]{1,0:T(8,128)(2,1)S(1)}, u32[]{:S(2)}, u32[]{:S(2)}) %collective-permute-start.2) | collective-permute-done | bytes 147488 | tf_op jit(solution)/shard_map/ppermute | solution.py:132
  27.9 3.7 %collective-permute-start.6 = (bf16[128,576]{1,0:T(8,128)(2,1)S(1)}, bf16[128,576]{1,0:T(8,128)(2,1)S(1)}, u32[]{:S(2)}, u32[]{:S(2)}) collective-permute-start(bf16[128,576]{1,0:T(8,128)(2,1)S(1)} %collective-permute-done.2.refs_3_), channel_id=1, source_target_pairs={{0,56},{8,0},{16,8},{24,16},{32,24},{40,32},{48,40},{56,48},{1,57}... | collective-permute-start | bytes 442376 | tf_op jit(solution)/shard_map/ppermute | solution.py:132
  31.6 3.5 %collective-permute-done.6.refs_0_ = bf16[128,576]{1,0:T(8,128)(2,1)S(1)} collective-permute-done((bf16[128,576]{1,0:T(8,128)(2,1)S(1)}, bf16[128,576]{1,0:T(8,128)(2,1)S(1)}, u32[]{:S(2)}, u32[]{:S(2)}) %collective-permute-start.6) | collective-permute-done | bytes 147488 | tf_op jit(solution)/shard_map/ppermute | solution.py:132
  35.1 3.7 %collective-permute-start.7 = (bf16[128,576]{1,0:T(8,128)(2,1)S(1)}, bf16[128,576]{1,0:T(8,128)(2,1)S(1)}, u32[]{:S(2)}, u32[]{:S(2)}) collective-permute-start(bf16[128,576]{1,0:T(8,128)(2,1)S(1)} %collective-permute-done.6.refs_0_), channel_id=1, source_target_pairs={{0,56},{8,0},{16,8},{24,16},{32,24},{40,32},{48,40},{56,48},{1,57}... | collective-permute-start | bytes 442376 | tf_op jit(solution)/shard_map/ppermute | solution.py:132
  38.8 0.3 collective-permute-done.8.refs_3_
  39.4 3.1 %shard_map.97 = (bf16[4,4,16,1664]{3,2,1,0:T(8,128)(2,1)S(1)}, bf16[4,4,16,1664]{3,2,1,0:T(8,128)(2,1)S(1)}) custom-call(s32[4]{0:T(128)S(1)} %pad_add_fusion.place_ref, bf16[128,576]{1,0:T(8,128)(2,1)S(1)} %collective-permute-done.1.refs_0_, bf16[128,576]{1,0:T(8,128)(2,1)S(1)} %collective-permute-done.refs_1_, bf16[128,576]{1,0:T(8,128)(2,1)S(1)} %bitcast.32, ...), custom_call_target="tpu_custom_call" | custom-call | flops 981467136 | bytes 4161536 | tf_op jit(solution)/shard_map/pallas_call | solution.py:47
  42.7 2.9 %collective-permute-done.9.refs_2_ = bf16[128,576]{1,0:T(8,128)(2,1)S(1)} collective-permute-done((bf16[128,576]{1,0:T(8,128)(2,1)S(1)}, bf16[128,576]{1,0:T(8,128)(2,1)S(1)}, u32[]{:S(2)}, u32[]{:S(2)}) %collective-permute-start.9) | collective-permute-done | bytes 147488 | tf_op jit(solution)/shard_map/ppermute | solution.py:132
  45.6 3.0 %shard_map.98 = (bf16[4,4,16,1664]{3,2,1,0:T(8,128)(2,1)S(1)}, bf16[4,4,16,1664]{3,2,1,0:T(8,128)(2,1)S(1)}) custom-call(s32[4]{0:T(128)S(1)} %pad_add_fusion.place_ref, bf16[128,576]{1,0:T(8,128)(2,1)S(1)} %collective-permute-done.6.refs_0_, bf16[128,576]{1,0:T(8,128)(2,1)S(1)} %collective-permute-done.7.refs_1_, ...), custom_call_target="tpu_custom_call" | custom-call | flops 981467136 | bytes 4161536 | tf_op jit(solution)/shard_map/pallas_call | solution.py:47
  48.8 2.4 %collective-permute-done.11.refs_3_ = bf16[4,4,16,1664]{3,2,1,0:T(8,128)(2,1)S(1)} collective-permute-done((bf16[4,4,16,1664]{3,2,1,0:T(8,128)(2,1)S(1)}, bf16[4,4,16,1664]{3,2,1,0:T(8,128)(2,1)S(1)}, u32[]{:S(2)}, u32[]{:S(2)}) %collective-permute-start.11) | collective-permute-done | bytes 852000 | tf_op jit(solution)/shard_map/ppermute | solution.py:339
  51.1 2.2 %shard_map.99 = bf16[16,32,1664]{2,1,0:T(8,128)(2,1)} custom-call(s32[4]{0:T(128)S(1)} %pad_add_fusion.place_ref, bf16[4,4,16,1664]{3,2,1,0:T(8,128)(2,1)S(1)} %get-tuple-element.40.refs_0_, bf16[4,4,16,1664]{3,2,1,0:T(8,128)(2,1)S(1)} %get-tuple-element.41.refs_1_, bf16[4,4,16,1664]{3,2,1,0:T(8,128)(2,1)S(1)} %collective-permute-done.10.refs_2_, ...), custom_call_target="tpu_custom_call" | custom-call | bytes 5111808 | tf_op jit(solution)/shard_map/pallas_call | solution.py:47
  53.3 7.4 %all-to-all-start.1 = ((bf16[16,32,1664]{2,1,0:T(8,128)(2,1)}), bf16[16,32,1664]{2,1,0:T(8,128)(2,1)S(1)}, u32[]{:S(2)}, u32[]{:S(2)}) async-start(bf16[16,32,1664]{2,1,0:T(8,128)(2,1)} %shard_map.99), calls=%async_computation.1 | async-start | bytes 3407872 | tf_op jit(solution)/shard_map/all_to_all | solution.py:341
  60.7 1.5 copy-done.1
  62.1 1.2 shard_map.101
  63.4 0.8 copy-done.2
  64.3 20.9 %all-to-all-done.1.terms_ref = bf16[16,32,1664]{2,1,0:T(8,128)(2,1)S(1)} async-done(((bf16[16,32,1664]{2,1,0:T(8,128)(2,1)}), bf16[16,32,1664]{2,1,0:T(8,128)(2,1)S(1)}, u32[]{:S(2)}, u32[]{:S(2)}) %all-to-all-start.1) | async-done | bytes 1703968 | tf_op jit(solution)/shard_map/all_to_all | solution.py:341
  85.3 0.8 shard_map.100
  86.1 0.7 reshape.97
  86.7 6.4 %all-to-all-start.2 = ((bf16[8,4,1664]{2,1,0:T(4,128)(2,1)}), bf16[8,4,1664]{2,1,0:T(4,128)(2,1)S(1)}, u32[]{:S(2)}, u32[]{:S(2)}) async-start(bf16[8,4,1664]{2,1,0:T(4,128)(2,1)} %reshape.97), calls=%async_computation.2 | async-start | bytes 212992 | tf_op jit(solution)/shard_map/all_to_all | solution.py:345
  93.3 3.5 %collective-permute-start.13 = (bf16[384,576]{1,0:T(8,128)(2,1)S(1)}, bf16[384,576]{1,0:T(8,128)(2,1)S(1)}, u32[]{:S(2)}, u32[]{:S(2)}) collective-permute-start(bf16[384,576]{1,0:T(8,128)(2,1)S(1)} %get-tuple-element.51), channel_id=1, source_target_pairs={{0,128},{64,192},{128,0},{192,64},{1,129},{65,193},{129,1},{193,65... | collective-permute-start | bytes 1327112 | tf_op jit(solution)/shard_map/ppermute | solution.py:132
  96.8 5.2 %all-to-all-done.2 = bf16[8,4,1664]{2,1,0:T(4,128)(2,1)S(1)} async-done(((bf16[8,4,1664]{2,1,0:T(4,128)(2,1)}), bf16[8,4,1664]{2,1,0:T(4,128)(2,1)S(1)}, u32[]{:S(2)}, u32[]{:S(2)}) %all-to-all-start.2) | async-done | bytes 106528 | tf_op jit(solution)/shard_map/all_to_all | solution.py:345
  102.5 2.6 %fusion.26 = (f32[2,96]{1,0:T(2,128)S(1)}, f32[2,96,2048]{2,1,0:T(8,128)S(1)}) fusion(bf16[2,96,256]{2,1,0:T(8,128)(2,1)S(1)} %bitcast.34, bf16[2,2048,512]{2,1,0:T(8,128)(2,1)} %param.14, pred[2,2048]{1,0:T(4,128)(4,1)S(1)} %iota_compare_fusion), kind=kOutput, calls=%fused_computation.34 | convolution fusion | flops 202506048 | bytes 3773184 | tf_op jit(solution)/shard_map/srd,smd->srm/dot_general | solution.py:25
  105.5 0.4 fusion.4
  105.9 0.5 fusion.12
  106.7 11.1 %all_to_all.30 = bf16[8,4,1536]{2,1,0:T(4,128)(2,1)S(1)} all-to-all(bf16[8,4,1536]{2,1,0:T(4,128)(2,1)S(1)} %copy.38), channel_id=1, replica_groups=mesh['y'=4,'z'=8,'x'=4,'core'=2] {'z'}, dimensions={0} | all-to-all | bytes 196608 | tf_op jit(solution)/shard_map/all_to_all | solution.py:356
  118.1 25.3 %all_to_all.31.rows_ref = bf16[16,32,1536]{2,1,0:T(8,128)(2,1)S(1)} all-to-all(bf16[16,32,1536]{2,1,0:T(8,128)(2,1)S(1)} %broadcast_in_dim.60), channel_id=1, replica_groups=mesh['y'=4,'z'=8,'x'=4,'core'=2] {'x','y'}, dimensions={0} | all-to-all | bytes 3145728 | tf_op jit(solution)/shard_map/all_to_all | solution.py:360
  143.4 2.2 %shard_map.102.own_ref = f32[512,576]{1,0:T(8,128)S(1)} custom-call(s32[4]{0:T(128)S(1)} %pad_add_fusion.place_ref, bf16[16,32,1536]{2,1,0:T(8,128)(2,1)S(1)} %all_to_all.31.rows_ref, bf16[384,576]{1,0:T(8,128)(2,1)S(1)} %get-tuple-element.54.refs_0_, bf16[384,576]{1,0:T(8,128)(2,1)S(1)} %collective-permute-done.12.refs_1_, ...), custom_call_target="tpu_custom_call" | custom-call | flops 905969664 | bytes 4521984 | tf_op jit(solution)/shard_map/pallas_call | solution.py:47
  145.6 1.2 collective-permute-done.15.rows_ref
  146.8 2.2 %shard_map.103.other_ref = f32[512,576]{1,0:T(8,128)S(1)} custom-call(s32[4]{0:T(128)S(1)} %pad_add_fusion.place_ref, bf16[16,32,1536]{2,1,0:T(8,128)(2,1)S(1)} %collective-permute-done.15.rows_ref, bf16[384,576]{1,0:T(8,128)(2,1)S(1)} %get-tuple-element.54.refs_0_, bf16[384,576]{1,0:T(8,128)(2,1)S(1)} %collective-permute-done.12.refs_1_, ...), custom_call_target="tpu_custom_call" | custom-call | flops 905969664 | bytes 4521984 | tf_op jit(solution)/shard_map/pallas_call | solution.py:47
  149.1 1.4 shard_map.104
  150.5 1.5 collective-permute-start.16
  151.9 1.8 collective-permute-start.20
  153.8 4.2 %collective-permute-done.16 = bf16[128,576]{1,0:T(8,128)(2,1)S(1)} collective-permute-done((bf16[128,576]{1,0:T(8,128)(2,1)S(1)}, bf16[128,576]{1,0:T(8,128)(2,1)S(1)}, u32[]{:S(2)}, u32[]{:S(2)}) %collective-permute-start.16) | collective-permute-done | bytes 147488 | tf_op jit(solution)/shard_map/ppermute | solution.py:132
  158.4 3.1 %collective-permute-start.21 = (bf16[128,576]{1,0:T(8,128)(2,1)S(1)}, bf16[128,576]{1,0:T(8,128)(2,1)S(1)}, u32[]{:S(2)}, u32[]{:S(2)}) collective-permute-start(bf16[128,576]{1,0:T(8,128)(2,1)S(1)} %add_convert_fusion.2), channel_id=1, source_target_pairs={{0,56},{8,0},{16,8},{24,16},{32,24},{40,32},{48,40},{56,48},{1,57}... | collective-permute-start | bytes 442376 | tf_op jit(solution)/shard_map/ppermute | solution.py:132
  161.5 3.3 %collective-permute-done.17 = bf16[128,576]{1,0:T(8,128)(2,1)S(1)} collective-permute-done((bf16[128,576]{1,0:T(8,128)(2,1)S(1)}, bf16[128,576]{1,0:T(8,128)(2,1)S(1)}, u32[]{:S(2)}, u32[]{:S(2)}) %collective-permute-start.17) | collective-permute-done | bytes 147488 | tf_op jit(solution)/shard_map/ppermute | solution.py:132
  164.9 3.3 %collective-permute-start.22 = (bf16[128,576]{1,0:T(8,128)(2,1)S(1)}, bf16[128,576]{1,0:T(8,128)(2,1)S(1)}, u32[]{:S(2)}, u32[]{:S(2)}) collective-permute-start(bf16[128,576]{1,0:T(8,128)(2,1)S(1)} %add_convert_fusion.1), channel_id=1, source_target_pairs={{0,56},{8,0},{16,8},{24,16},{32,24},{40,32},{48,40},{56,48},{1,57}... | collective-permute-start | bytes 442376 | tf_op jit(solution)/shard_map/ppermute | solution.py:132
  168.2 3.2 %collective-permute-done.18 = bf16[128,576]{1,0:T(8,128)(2,1)S(1)} collective-permute-done((bf16[128,576]{1,0:T(8,128)(2,1)S(1)}, bf16[128,576]{1,0:T(8,128)(2,1)S(1)}, u32[]{:S(2)}, u32[]{:S(2)}) %collective-permute-start.18) | collective-permute-done | bytes 147488 | tf_op jit(solution)/shard_map/ppermute | solution.py:132
  171.6 6.5 %collective-permute-done.19 = bf16[128,576]{1,0:T(8,128)(2,1)S(1)} collective-permute-done((bf16[128,576]{1,0:T(8,128)(2,1)S(1)}, bf16[128,576]{1,0:T(8,128)(2,1)S(1)}, u32[]{:S(2)}, u32[]{:S(2)}) %collective-permute-start.19) | collective-permute-done | bytes 147488 | tf_op jit(solution)/shard_map/ppermute | solution.py:132
  178.1 8.7 %all_to_all.32.blocks_ref = bf16[4,32,576]{2,1,0:T(8,128)(2,1)S(1)} all-to-all(bf16[4,32,576]{2,1,0:T(8,128)(2,1)S(1)} %bitcast.33), channel_id=1, replica_groups=mesh['y'=4,'z'=8,'x'=4,'core'=2] {'y'}, dimensions={0} | all-to-all | bytes 294912 | tf_op jit(solution)/shard_map/all_to_all | solution.py:366
  186.8 1.3 shard_map.105
  (66 shorter events, 3.2 us)
Async XLA Ops:
  0.6 15.4 %copy-start = (bf16[2304,384]{1,0:T(8,128)(2,1)S(1)}, bf16[2304,384]{1,0:T(8,128)(2,1)}, u32[]{:S(2)}) copy-start(bf16[2304,384]{1,0:T(8,128)(2,1)} %query_ref) | copy-start | bytes 5308420
  3.3 10.2 %all-to-all-start = ((bf16[4,32,576]{2,1,0:T(8,128)(2,1)}), bf16[4,32,576]{2,1,0:T(8,128)(2,1)S(1)}, u32[]{:S(2)}, u32[]{:S(2)}) async-start(bf16[4,32,576]{2,1,0:T(8,128)(2,1)} %shard_map.95), calls=%async_computation | async-start | bytes 327680 | tf_op jit(solution)/shard_map/all_to_all | solution.py:328
  13.5 11.6 %collective-permute-start = (bf16[128,576]{1,0:T(8,128)(2,1)S(1)}, bf16[128,576]{1,0:T(8,128)(2,1)S(1)}, u32[]{:S(2)}, u32[]{:S(2)}) collective-permute-start(bf16[128,576]{1,0:T(8,128)(2,1)S(1)} %bitcast.30), channel_id=1, source_target_pairs={{0,8},{8,16},{16,24},{24,32},{32,40},{40,48},{48,56},{56,0},{1,9},... | collective-permute-start | bytes 442376 | tf_op jit(solution)/shard_map/ppermute | solution.py:132
  16.9 22.1 %collective-permute-start.3 = (bf16[608,384]{1,0:T(8,128)(2,1)S(1)}, bf16[608,384]{1,0:T(8,128)(2,1)S(1)}, u32[]{:S(2)}, u32[]{:S(2)}) collective-permute-start(bf16[608,384]{1,0:T(8,128)(2,1)S(1)} %get-tuple-element.37), channel_id=1, source_target_pairs={{0,64},{64,128},{128,192},{192,0},{1,65},{65,129},{129,193},{193,1... | collective-permute-start | bytes 1400840 | tf_op jit(solution)/shard_map/ppermute | solution.py:132
  17.1 21.9 %collective-permute-start.4 = (bf16[608,384]{1,0:T(8,128)(2,1)S(1)}, bf16[608,384]{1,0:T(8,128)(2,1)S(1)}, u32[]{:S(2)}, u32[]{:S(2)}) collective-permute-start(bf16[608,384]{1,0:T(8,128)(2,1)S(1)} %get-tuple-element.38), channel_id=1, source_target_pairs={{0,128},{64,192},{128,0},{192,64},{1,129},{65,193},{129,1},{193,65... | collective-permute-start | bytes 1400840 | tf_op jit(solution)/shard_map/ppermute | solution.py:132
  20.6 18.8 %collective-permute-start.5 = (bf16[608,384]{1,0:T(8,128)(2,1)S(1)}, bf16[608,384]{1,0:T(8,128)(2,1)S(1)}, u32[]{:S(2)}, u32[]{:S(2)}) collective-permute-start(bf16[608,384]{1,0:T(8,128)(2,1)S(1)} %get-tuple-element.39), channel_id=1, source_target_pairs={{0,192},{64,0},{128,64},{192,128},{1,193},{65,1},{129,65},{193,129... | collective-permute-start | bytes 1400840 | tf_op jit(solution)/shard_map/ppermute | solution.py:132
  21.1 6.8 %collective-permute-start.2 = (bf16[128,576]{1,0:T(8,128)(2,1)S(1)}, bf16[128,576]{1,0:T(8,128)(2,1)S(1)}, u32[]{:S(2)}, u32[]{:S(2)}) collective-permute-start(bf16[128,576]{1,0:T(8,128)(2,1)S(1)} %bitcast.31), channel_id=1, source_target_pairs={{0,56},{8,0},{16,8},{24,16},{32,24},{40,32},{48,40},{56,48},{1,57}... | collective-permute-start | bytes 442376 | tf_op jit(solution)/shard_map/ppermute | solution.py:132
  25.1 6.5 %collective-permute-start.1 = (bf16[128,576]{1,0:T(8,128)(2,1)S(1)}, bf16[128,576]{1,0:T(8,128)(2,1)S(1)}, u32[]{:S(2)}, u32[]{:S(2)}) collective-permute-start(bf16[128,576]{1,0:T(8,128)(2,1)S(1)} %collective-permute-done.refs_1_), channel_id=1, source_target_pairs={{0,8},{8,16},{16,24},{24,32},{32,40},{40,48},{48,56},{56,0},{1,9},... | collective-permute-start | bytes 442376 | tf_op jit(solution)/shard_map/ppermute | solution.py:132
  27.9 7.2 %collective-permute-start.6 = (bf16[128,576]{1,0:T(8,128)(2,1)S(1)}, bf16[128,576]{1,0:T(8,128)(2,1)S(1)}, u32[]{:S(2)}, u32[]{:S(2)}) collective-permute-start(bf16[128,576]{1,0:T(8,128)(2,1)S(1)} %collective-permute-done.2.refs_3_), channel_id=1, source_target_pairs={{0,56},{8,0},{16,8},{24,16},{32,24},{40,32},{48,40},{56,48},{1,57}... | collective-permute-start | bytes 442376 | tf_op jit(solution)/shard_map/ppermute | solution.py:132
  31.6 7.5 %collective-permute-start.8 = (bf16[128,576]{1,0:T(8,128)(2,1)S(1)}, bf16[128,576]{1,0:T(8,128)(2,1)S(1)}, u32[]{:S(2)}, u32[]{:S(2)}) collective-permute-start(bf16[128,576]{1,0:T(8,128)(2,1)S(1)} %collective-permute-done.1.refs_0_), channel_id=1, source_target_pairs={{0,8},{8,16},{16,24},{24,32},{32,40},{40,48},{48,56},{56,0},{1,9},... | collective-permute-start | bytes 442376 | tf_op jit(solution)/shard_map/ppermute | solution.py:132
  35.1 7.6 %collective-permute-start.7 = (bf16[128,576]{1,0:T(8,128)(2,1)S(1)}, bf16[128,576]{1,0:T(8,128)(2,1)S(1)}, u32[]{:S(2)}, u32[]{:S(2)}) collective-permute-start(bf16[128,576]{1,0:T(8,128)(2,1)S(1)} %collective-permute-done.6.refs_0_), channel_id=1, source_target_pairs={{0,56},{8,0},{16,8},{24,16},{32,24},{40,32},{48,40},{56,48},{1,57}... | collective-permute-start | bytes 442376 | tf_op jit(solution)/shard_map/ppermute | solution.py:132
  39.1 6.5 %collective-permute-start.9 = (bf16[128,576]{1,0:T(8,128)(2,1)S(1)}, bf16[128,576]{1,0:T(8,128)(2,1)S(1)}, u32[]{:S(2)}, u32[]{:S(2)}) collective-permute-start(bf16[128,576]{1,0:T(8,128)(2,1)S(1)} %collective-permute-done.8.refs_3_), channel_id=1, source_target_pairs={{0,8},{8,16},{16,24},{24,32},{32,40},{40,48},{48,56},{56,0},{1,9},... | collective-permute-start | bytes 442376 | tf_op jit(solution)/shard_map/ppermute | solution.py:132
  42.4 6.3 %collective-permute-start.10 = (bf16[4,4,16,1664]{3,2,1,0:T(8,128)(2,1)S(1)}, bf16[4,4,16,1664]{3,2,1,0:T(8,128)(2,1)S(1)}, u32[]{:S(2)}, u32[]{:S(2)}) collective-permute-start(bf16[4,4,16,1664]{3,2,1,0:T(8,128)(2,1)S(1)} %get-tuple-element.42), channel_id=1, source_target_pairs={{0,1},{1,0},{2,3},{3,2},{4,5},{5,4},{6,7},{7,6},{8,9},{9,8},{10,11... | collective-permute-start | bytes 2555912 | tf_op jit(solution)/shard_map/ppermute | solution.py:339
  48.6 2.5 %collective-permute-start.11 = (bf16[4,4,16,1664]{3,2,1,0:T(8,128)(2,1)S(1)}, bf16[4,4,16,1664]{3,2,1,0:T(8,128)(2,1)S(1)}, u32[]{:S(2)}, u32[]{:S(2)}) collective-permute-start(bf16[4,4,16,1664]{3,2,1,0:T(8,128)(2,1)S(1)} %get-tuple-element.43), channel_id=1, source_target_pairs={{0,1},{1,0},{2,3},{3,2},{4,5},{5,4},{6,7},{7,6},{8,9},{9,8},{10,11... | collective-permute-start | bytes 2555912 | tf_op jit(solution)/shard_map/ppermute | solution.py:339
  53.3 32.0 %all-to-all-start.1 = ((bf16[16,32,1664]{2,1,0:T(8,128)(2,1)}), bf16[16,32,1664]{2,1,0:T(8,128)(2,1)S(1)}, u32[]{:S(2)}, u32[]{:S(2)}) async-start(bf16[16,32,1664]{2,1,0:T(8,128)(2,1)} %shard_map.99), calls=%async_computation.1 | async-start | bytes 3407872 | tf_op jit(solution)/shard_map/all_to_all | solution.py:341
  60.7 1.5 copy-start.1
  62.1 2.1 %copy-start.3 = (s32[2]{0:T(128)S(1)}, s32[2]{0:T(128)}, u32[]{:S(2)}) copy-start(s32[2]{0:T(128)} %param.15) | copy-start | bytes 28
  63.4 0.8 copy-start.2
  86.7 15.3 %all-to-all-start.2 = ((bf16[8,4,1664]{2,1,0:T(4,128)(2,1)}), bf16[8,4,1664]{2,1,0:T(4,128)(2,1)S(1)}, u32[]{:S(2)}, u32[]{:S(2)}) async-start(bf16[8,4,1664]{2,1,0:T(4,128)(2,1)} %reshape.97), calls=%async_computation.2 | async-start | bytes 212992 | tf_op jit(solution)/shard_map/all_to_all | solution.py:345
  93.2 24.7 %collective-permute-start.12 = (bf16[384,576]{1,0:T(8,128)(2,1)}, bf16[384,576]{1,0:T(8,128)(2,1)S(1)}, u32[]{:S(2)}, u32[]{:S(2)}) collective-permute-start(bf16[384,576]{1,0:T(8,128)(2,1)} %copy-done.2), channel_id=1, source_target_pairs={{0,64},{64,128},{128,192},{192,0},{1,65},{65,129},{129,193},{193,1... | collective-permute-start | bytes 1327112 | tf_op jit(solution)/shard_map/ppermute | solution.py:132
  93.3 24.6 %collective-permute-start.13 = (bf16[384,576]{1,0:T(8,128)(2,1)S(1)}, bf16[384,576]{1,0:T(8,128)(2,1)S(1)}, u32[]{:S(2)}, u32[]{:S(2)}) collective-permute-start(bf16[384,576]{1,0:T(8,128)(2,1)S(1)} %get-tuple-element.51), channel_id=1, source_target_pairs={{0,128},{64,192},{128,0},{192,64},{1,129},{65,193},{129,1},{193,65... | collective-permute-start | bytes 1327112 | tf_op jit(solution)/shard_map/ppermute | solution.py:132
  96.8 21.1 %collective-permute-start.14 = (bf16[384,576]{1,0:T(8,128)(2,1)S(1)}, bf16[384,576]{1,0:T(8,128)(2,1)S(1)}, u32[]{:S(2)}, u32[]{:S(2)}) collective-permute-start(bf16[384,576]{1,0:T(8,128)(2,1)S(1)} %get-tuple-element.52), channel_id=1, source_target_pairs={{0,192},{64,0},{128,64},{192,128},{1,193},{65,1},{129,65},{193,129... | collective-permute-start | bytes 1327112 | tf_op jit(solution)/shard_map/ppermute | solution.py:132
  102.4 3.5 %copy-start.4 = (bf16[2,2048,512]{2,1,0:T(8,128)(2,1)S(1)}, bf16[2,2048,512]{2,1,0:T(8,128)(2,1)}, u32[]{:S(2)}) copy-start(bf16[2,2048,512]{2,1,0:T(8,128)(2,1)} %param.14) | copy-start | bytes 12582916
  143.4 3.4 %collective-permute-start.15 = (bf16[16,32,1536]{2,1,0:T(8,128)(2,1)S(1)}, bf16[16,32,1536]{2,1,0:T(8,128)(2,1)S(1)}, u32[]{:S(2)}, u32[]{:S(2)}) collective-permute-start(bf16[16,32,1536]{2,1,0:T(8,128)(2,1)S(1)} %all_to_all.31.rows_ref), channel_id=1, source_target_pairs={{0,1},{1,0},{2,3},{3,2},{4,5},{5,4},{6,7},{7,6},{8,9},{9,8},{10,11... | collective-permute-start | bytes 4718600 | tf_op jit(solution)/shard_map/ppermute | solution.py:361
  150.5 7.5 %collective-permute-start.16 = (bf16[128,576]{1,0:T(8,128)(2,1)S(1)}, bf16[128,576]{1,0:T(8,128)(2,1)S(1)}, u32[]{:S(2)}, u32[]{:S(2)}) collective-permute-start(bf16[128,576]{1,0:T(8,128)(2,1)S(1)} %get-tuple-element.62), channel_id=1, source_target_pairs={{0,8},{8,16},{16,24},{24,32},{32,40},{40,48},{48,56},{56,0},{1,9},... | collective-permute-start | bytes 442376 | tf_op jit(solution)/shard_map/ppermute | solution.py:132
  151.9 6.4 %collective-permute-start.20 = (bf16[128,576]{1,0:T(8,128)(2,1)S(1)}, bf16[128,576]{1,0:T(8,128)(2,1)S(1)}, u32[]{:S(2)}, u32[]{:S(2)}) collective-permute-start(bf16[128,576]{1,0:T(8,128)(2,1)S(1)} %get-tuple-element.65), channel_id=1, source_target_pairs={{0,56},{8,0},{16,8},{24,16},{32,24},{40,32},{48,40},{56,48},{1,57}... | collective-permute-start | bytes 442376 | tf_op jit(solution)/shard_map/ppermute | solution.py:132
  158.1 6.7 %collective-permute-start.17 = (bf16[128,576]{1,0:T(8,128)(2,1)S(1)}, bf16[128,576]{1,0:T(8,128)(2,1)S(1)}, u32[]{:S(2)}, u32[]{:S(2)}) collective-permute-start(bf16[128,576]{1,0:T(8,128)(2,1)S(1)} %add_convert_fusion.5), channel_id=1, source_target_pairs={{0,8},{8,16},{16,24},{24,32},{32,40},{40,48},{48,56},{56,0},{1,9},... | collective-permute-start | bytes 442376 | tf_op jit(solution)/shard_map/ppermute | solution.py:132
  158.4 6.5 %collective-permute-start.21 = (bf16[128,576]{1,0:T(8,128)(2,1)S(1)}, bf16[128,576]{1,0:T(8,128)(2,1)S(1)}, u32[]{:S(2)}, u32[]{:S(2)}) collective-permute-start(bf16[128,576]{1,0:T(8,128)(2,1)S(1)} %add_convert_fusion.2), channel_id=1, source_target_pairs={{0,56},{8,0},{16,8},{24,16},{32,24},{40,32},{48,40},{56,48},{1,57}... | collective-permute-start | bytes 442376 | tf_op jit(solution)/shard_map/ppermute | solution.py:132
  164.8 6.6 %collective-permute-start.18 = (bf16[128,576]{1,0:T(8,128)(2,1)S(1)}, bf16[128,576]{1,0:T(8,128)(2,1)S(1)}, u32[]{:S(2)}, u32[]{:S(2)}) collective-permute-start(bf16[128,576]{1,0:T(8,128)(2,1)S(1)} %add_convert_fusion.4), channel_id=1, source_target_pairs={{0,8},{8,16},{16,24},{24,32},{32,40},{40,48},{48,56},{56,0},{1,9},... | collective-permute-start | bytes 442376 | tf_op jit(solution)/shard_map/ppermute | solution.py:132
  164.9 6.6 %collective-permute-start.22 = (bf16[128,576]{1,0:T(8,128)(2,1)S(1)}, bf16[128,576]{1,0:T(8,128)(2,1)S(1)}, u32[]{:S(2)}, u32[]{:S(2)}) collective-permute-start(bf16[128,576]{1,0:T(8,128)(2,1)S(1)} %add_convert_fusion.1), channel_id=1, source_target_pairs={{0,56},{8,0},{16,8},{24,16},{32,24},{40,32},{48,40},{56,48},{1,57}... | collective-permute-start | bytes 442376 | tf_op jit(solution)/shard_map/ppermute | solution.py:132
  171.5 6.6 %collective-permute-start.19 = (bf16[128,576]{1,0:T(8,128)(2,1)S(1)}, bf16[128,576]{1,0:T(8,128)(2,1)S(1)}, u32[]{:S(2)}, u32[]{:S(2)}) collective-permute-start(bf16[128,576]{1,0:T(8,128)(2,1)S(1)} %add_convert_fusion.3), channel_id=1, source_target_pairs={{0,8},{8,16},{16,24},{24,32},{32,40},{40,48},{48,56},{56,0},{1,9},... | collective-permute-start | bytes 442376 | tf_op jit(solution)/shard_map/ppermute | solution.py:132
